TPU v7x, 32 devices: a whole 2x2x4 slice. The times are simulated.
32 devices in a mesh: ctx: 8 (over z, x), tp: 4 (over y, core).
Axes of the slice: x: 2, y: 2, z: 4, core: 2. Of those that a mesh axis runs over, the one named last changes fastest.
Arguments:
- tokens: bfloat16 [2, 4096, 2048], P(None, 'ctx', 'tp'), may hold values from -6 to 6
- lengths: int32 [2], replicated, may hold values from 256 to 4096, as said below
- teacher: bfloat16 [2, 4096, 2048], P(None, 'ctx', 'tp'), may hold values from -6 to 6
- out_grad: bfloat16 [2, 4096, 2048], P(None, 'ctx', 'tp'), may hold values from -6 to 6
- w_query: bfloat16 [2048, 2048], P(None, 'tp'), may hold values from -0.125 to 0.125
- b_query: bfloat16 [2048], P('tp'), may hold values from -3 to 3
- w_keyval: bfloat16 [2048, 256], replicated, may hold values from -0.125 to 0.125
- b_value: bfloat16 [128], replicated, may hold values from -0.29882812 to 0.29882812
- w_output: bfloat16 [2048, 2048], P('tp'), may hold values from -1 to 1
- b_output: bfloat16 [2048], P('tp'), may hold values from -0.29882812 to 0.29882812
- w_expand: bfloat16 [2048, 8192], P(None, 'tp'), may hold values from -0.125 to 0.125
- b_expand: bfloat16 [8192], P('tp'), may hold values from -0.29882812 to 0.29882812
- w_shrink: bfloat16 [8192, 2048], P('tp'), may hold values from -0.0625 to 0.0625
- b_shrink: bfloat16 [2048], P('tp'), may hold values from -0.29882812 to 0.29882812
- gain_first: bfloat16 [2048], P('tp'), may hold values from 0.099609375 to 1.8984375
- bias_first: bfloat16 [2048], P('tp'), may hold values from -0.1796875 to 0.1796875
- gain_second: bfloat16 [2048], P('tp'), may hold values from 0.099609375 to 1.8984375
- bias_second: bfloat16 [2048], P('tp'), may hold values from -0.1796875 to 0.1796875
Outputs:
- output: bfloat16 [2, 4096, 2048], P(None, 'ctx', 'tp')
- tokens_grad: float32 [2, 4096, 2048], P(None, 'ctx', 'tp')
- loss: float32 [], replicated
- grad_w_query: float32 [2048, 2048], P(None, 'tp')
- grad_b_query: float32 [2048], P('tp')
- grad_w_keyval: float32 [2048, 256], replicated
- grad_b_value: float32 [128], replicated
- grad_w_output: float32 [2048, 2048], P('tp')
- grad_b_output: float32 [2048], P('tp')
- grad_w_expand: float32 [2048, 8192], P(None, 'tp')
- grad_b_expand: float32 [8192], P('tp')
- grad_w_shrink: float32 [8192, 2048], P('tp')
- grad_b_shrink: float32 [2048], P('tp')
- grad_gain_first: float32 [2048], P('tp')
- grad_bias_first: float32 [2048], P('tp')
- grad_gain_second: float32 [2048], P('tp')
- grad_bias_second: float32 [2048], P('tp')
Inputs may be any that keep to these rules, and one draw needn't show every extreme that they name: `lengths`: each sequence's valid tokens form a prefix; in every draw one sequence, drawn from the seed, is valid in full.
All inputs are finite; a program needn't handle non-finite values.
Results may differ from a plain program's by a relative error of at most 0.015.
Values may be sent and summed in bfloat16 or wider, within the bound.
No kernel may reach another device: no remote copies, remote signals or barrier semaphores. Data moves between devices by JAX's collectives and lax.ppermute only.
A program may use at most 256 MiB of HBM per device.

v0:
```python
import math

import jax
import jax.numpy as jnp
from jax import lax
from jax.sharding import PartitionSpec as P

BLOCK = 256


EPS = 1e-05
NEG = -1e30


def gelu_tanh(values):
    return jax.nn.gelu(values, approximate=True)


def pair_sums(first_part, second_part):
    return lax.psum((jnp.sum(first_part, axis=-1), jnp.sum(second_part, axis=-1)), "tp")


def layer_norm(values, gain, shift, width):
    total, square = pair_sums(values, values * values)
    mean = total / width
    var = square / width - mean * mean
    factor = lax.rsqrt(var + EPS)
    normed = (values - mean[:, None]) * factor[:, None]
    return (normed, factor, normed * gain.astype(jnp.float32) + shift.astype(jnp.float32))


def layer_norm_back(grad, normed, factor, gain, width):
    scaled = grad * gain.astype(jnp.float32)
    total, cross = pair_sums(scaled, scaled * normed)
    back = factor[:, None] * (scaled - total[:, None] / width - normed * (cross[:, None] / width))
    return (back, jnp.sum(grad * normed, axis=0), jnp.sum(grad, axis=0))


def full_rows(values):
    return lax.all_gather(values, "tp", axis=1, tiled=True)


def shard_sums(partial_value):
    return lax.psum_scatter(
        partial_value.astype(jnp.bfloat16), "tp", scatter_dimension=1, tiled=True
    ).astype(jnp.float32)


def contract_rows(left, right):
    return lax.dot_general(
        left, right, (((0,), (0,)), ((), ())), preferred_element_type=jnp.float32
    )


def contract_cols(left, right):
    return lax.dot_general(
        left, right, (((1,), (1,)), ((), ())), preferred_element_type=jnp.float32
    )


def allowed_mask(query_pos, key_start, key_rows, lengths):
    key_pos = key_start + jnp.arange(key_rows, dtype=jnp.int32)
    causal = (key_pos // BLOCK)[None, :] <= (query_pos // BLOCK)[:, None]
    inside = key_pos[None, :] < lengths[:, None]
    return causal[None, :, None, :] & inside[:, None, None, :]


def column_sum(values):
    return jnp.sum(values.astype(jnp.float32), axis=0)


def shards(
    tokens,
    lengths,
    teacher,
    out_grad,
    w_query,
    b_query,
    w_keyval,
    b_value,
    w_output,
    b_output,
    w_expand,
    b_expand,
    w_shrink,
    b_shrink,
    gain_first,
    bias_first,
    gain_second,
    bias_second,
):
    seqs, tok_rows, part_width = tokens.shape
    rows = seqs * tok_rows
    width = w_query.shape[0]
    head = w_keyval.shape[1] // 2
    local_heads = w_query.shape[1] // head
    factor_qk = head ** (-0.5)
    full_len = tok_rows * lax.axis_size("ctx")
    key_rows = math.gcd(full_len, 512)
    key_steps = full_len // key_rows
    position = lax.axis_index("ctx")
    query_pos = position * tok_rows + jnp.arange(tok_rows, dtype=jnp.int32)
    steps_index = jnp.arange(key_steps, dtype=jnp.int32)

    def run_keys(step, carry):
        return lax.scan(step, carry, steps_index)[0]

    inputs = tokens.astype(jnp.float32).reshape(rows, part_width)
    normed_one, factor_one, first_f = layer_norm(inputs, gain_first, bias_first, width)
    first = full_rows(first_f.astype(jnp.bfloat16))
    queries = (
        jnp.dot(first, w_query, preferred_element_type=jnp.float32) + b_query.astype(jnp.float32)
    ).astype(jnp.bfloat16)
    kv_bias = jnp.concatenate([jnp.zeros((head,), jnp.float32), b_value.astype(jnp.float32)])
    keyval = (jnp.dot(first, w_keyval, preferred_element_type=jnp.float32) + kv_bias).astype(
        jnp.bfloat16
    )
    keyval = keyval.reshape(seqs, tok_rows, 2 * head)
    every_kv = lax.all_gather(keyval, "ctx", axis=1, tiled=True)
    query_four = queries.reshape(seqs, tok_rows, local_heads, head)

    def block_scores(source, start):
        piece = lax.dynamic_slice_in_dim(source, start, key_rows, 1)
        raw = (
            jnp.einsum(
                "sqhd,skd->sqhk", query_four, piece[..., :head], preferred_element_type=jnp.float32
            )
            * factor_qk
        )
        return (piece, raw, allowed_mask(query_pos, start, key_rows, lengths))

    def top_step(carry, index):
        top, total = carry
        piece, raw, allowed = block_scores(every_kv, index * key_rows)
        masked = jnp.where(allowed, raw, NEG)
        new_top = jnp.maximum(top, jnp.max(masked, axis=-1))
        fresh = jnp.where(allowed, jnp.exp(masked - new_top[..., None]), 0.0)
        total = total * jnp.exp(top - new_top) + jnp.sum(fresh, axis=-1)
        return ((new_top, total), None)

    start_top = jnp.full((seqs, tok_rows, local_heads), NEG, jnp.float32)
    top, total = run_keys(top_step, (start_top, jnp.zeros_like(start_top)))
    log_total = top + jnp.log(total)

    def mix_step(accum, index):
        piece, raw, allowed = block_scores(every_kv, index * key_rows)
        weights = jnp.exp(jnp.where(allowed, raw - log_total[..., None], NEG)).astype(jnp.bfloat16)
        return (
            accum
            + jnp.einsum(
                "sqhk,skd->sqhd", weights, piece[..., head:], preferred_element_type=jnp.float32
            ),
            None,
        )

    mixed = run_keys(mix_step, jnp.zeros((seqs, tok_rows, local_heads, head), jnp.float32))
    attended = mixed.reshape(rows, local_heads * head).astype(jnp.bfloat16)
    middle = (
        inputs
        + shard_sums(jnp.dot(attended, w_output, preferred_element_type=jnp.float32))
        + b_output.astype(jnp.float32)
    )
    normed_two, factor_two, second_f = layer_norm(middle, gain_second, bias_second, width)
    second = full_rows(second_f.astype(jnp.bfloat16))
    hidden = jnp.dot(second, w_expand, preferred_element_type=jnp.float32) + b_expand.astype(
        jnp.float32
    )
    activated_f, gelu_back = jax.vjp(gelu_tanh, hidden)
    activated = activated_f.astype(jnp.bfloat16)
    final = (
        middle
        + shard_sums(jnp.dot(activated, w_shrink, preferred_element_type=jnp.float32))
        + b_shrink.astype(jnp.float32)
    )
    output = final.astype(jnp.bfloat16).reshape(seqs, tok_rows, part_width)
    valid = (query_pos[None, :] < lengths[:, None]).astype(jnp.float32).reshape(rows, 1)
    target = teacher.astype(jnp.float32).reshape(rows, part_width)
    weight_out = out_grad.astype(jnp.float32).reshape(rows, part_width)
    diff = final - target
    objective = jnp.sum(valid * (weight_out * final + 0.5 * diff * diff))
    d_final = valid * (weight_out + diff)
    g_shrink = d_final.astype(jnp.bfloat16)
    grad_b_shrink = column_sum(g_shrink)
    g_shrink_full = full_rows(g_shrink)
    grad_w_shrink = contract_rows(activated, g_shrink_full)
    d_hidden = gelu_back(contract_cols(g_shrink_full, w_shrink))[0].astype(jnp.bfloat16)
    grad_b_expand = column_sum(d_hidden)
    grad_w_expand = contract_rows(second, d_hidden)
    d_second = shard_sums(contract_cols(d_hidden, w_expand))
    d_mid_norm, grad_gain_second, grad_bias_second = layer_norm_back(
        d_second, normed_two, factor_two, gain_second, width
    )
    d_middle = d_final + d_mid_norm
    g_output = d_middle.astype(jnp.bfloat16)
    grad_b_output = column_sum(g_output)
    g_output_full = full_rows(g_output)
    grad_w_output = contract_rows(attended, g_output_full)
    d_attended = (
        contract_cols(g_output_full, w_output)
        .astype(jnp.bfloat16)
        .reshape(seqs, tok_rows, local_heads, head)
    )
    delta = jnp.sum(d_attended.astype(jnp.float32) * mixed, axis=-1)
    back_kv = lax.all_gather(keyval, "ctx", axis=1, tiled=True)

    def back_step(carry, index):
        d_query, d_keyval = carry
        start = index * key_rows
        piece, raw, allowed = block_scores(back_kv, start)
        probs = jnp.exp(jnp.where(allowed, raw - log_total[..., None], NEG))
        d_probs = jnp.einsum(
            "sqhd,skd->sqhk", d_attended, piece[..., head:], preferred_element_type=jnp.float32
        )
        d_scores = (probs * (d_probs - delta[..., None])).astype(jnp.bfloat16)
        d_query = d_query + jnp.einsum(
            "sqhk,skd->sqhd", d_scores, piece[..., :head], preferred_element_type=jnp.float32
        )
        d_keys = (
            jnp.einsum("sqhk,sqhd->skd", d_scores, query_four, preferred_element_type=jnp.float32)
            * factor_qk
        )
        d_values = jnp.einsum(
            "sqhk,sqhd->skd",
            probs.astype(jnp.bfloat16),
            d_attended,
            preferred_element_type=jnp.float32,
        )
        d_keyval = lax.dynamic_update_slice_in_dim(
            d_keyval, jnp.concatenate([d_keys, d_values], axis=-1), start, 1
        )
        return ((d_query, d_keyval), None)

    start_back = (
        jnp.zeros((seqs, tok_rows, local_heads, head), jnp.float32),
        jnp.zeros((seqs, full_len, 2 * head), jnp.float32),
    )
    d_query, d_keyval = run_keys(back_step, start_back)
    own_kv = lax.psum_scatter(d_keyval.astype(jnp.bfloat16), "ctx", scatter_dimension=1, tiled=True)
    d_kv = lax.psum(own_kv, "tp").reshape(rows, 2 * head)
    grad_b_value = column_sum(d_kv[:, head:])
    grad_w_keyval = contract_rows(first, d_kv)
    d_queries = (d_query * factor_qk).reshape(rows, local_heads * head).astype(jnp.bfloat16)
    grad_b_query = column_sum(d_queries)
    grad_w_query = contract_rows(first, d_queries)
    kv_cols = lax.dynamic_slice_in_dim(w_keyval, lax.axis_index("tp") * part_width, part_width, 0)
    d_first = shard_sums(contract_cols(d_queries, w_query)) + contract_cols(d_kv, kv_cols)
    d_in_norm, grad_gain_first, grad_bias_first = layer_norm_back(
        d_first, normed_one, factor_one, gain_first, width
    )
    tokens_grad = (d_middle + d_in_norm).reshape(seqs, tok_rows, part_width)
    (
        grad_w_query,
        grad_b_query,
        grad_w_keyval,
        grad_b_value,
        grad_w_output,
        grad_b_output,
        grad_w_expand,
        grad_b_expand,
        grad_w_shrink,
        grad_b_shrink,
        grad_gain_first,
        grad_bias_first,
        grad_gain_second,
        grad_bias_second,
    ) = (
        lax.psum(grad_w_query.astype(jnp.bfloat16), "ctx").astype(jnp.float32),
        lax.psum(grad_b_query.astype(jnp.bfloat16), "ctx").astype(jnp.float32),
        lax.psum(grad_w_keyval.astype(jnp.bfloat16), "ctx").astype(jnp.float32),
        lax.psum(grad_b_value.astype(jnp.bfloat16), "ctx").astype(jnp.float32),
        lax.psum(grad_w_output.astype(jnp.bfloat16), "ctx").astype(jnp.float32),
        lax.psum(grad_b_output.astype(jnp.bfloat16), "ctx").astype(jnp.float32),
        lax.psum(grad_w_expand.astype(jnp.bfloat16), "ctx").astype(jnp.float32),
        lax.psum(grad_b_expand.astype(jnp.bfloat16), "ctx").astype(jnp.float32),
        lax.psum(grad_w_shrink.astype(jnp.bfloat16), "ctx").astype(jnp.float32),
        lax.psum(grad_b_shrink.astype(jnp.bfloat16), "ctx").astype(jnp.float32),
        lax.psum(grad_gain_first.astype(jnp.bfloat16), "ctx").astype(jnp.float32),
        lax.psum(grad_bias_first.astype(jnp.bfloat16), "ctx").astype(jnp.float32),
        lax.psum(grad_gain_second.astype(jnp.bfloat16), "ctx").astype(jnp.float32),
        lax.psum(grad_bias_second.astype(jnp.bfloat16), "ctx").astype(jnp.float32),
    )
    grand_total = lax.psum(objective, ("ctx", "tp"))
    loss = grand_total / (jnp.sum(lengths).astype(jnp.float32) * width)
    return (
        output,
        tokens_grad,
        loss,
        grad_w_query,
        grad_b_query,
        grad_w_keyval,
        grad_b_value,
        grad_w_output,
        grad_b_output,
        grad_w_expand,
        grad_b_expand,
        grad_w_shrink,
        grad_b_shrink,
        grad_gain_first,
        grad_bias_first,
        grad_gain_second,
        grad_bias_second,
    )


def solution(mesh):
    placed = (
        P(None, "ctx", "tp"),
        P(),
        P(None, "ctx", "tp"),
        P(None, "ctx", "tp"),
        P(None, "tp"),
        P("tp"),
        P(),
        P(),
        P("tp", None),
        P("tp"),
        P(None, "tp"),
        P("tp"),
        P("tp", None),
        P("tp"),
        P("tp"),
        P("tp"),
        P("tp"),
        P("tp"),
    )
    return jax.shard_map(
        shards,
        mesh=mesh,
        in_specs=placed,
        out_specs=(
            P(None, "ctx", "tp"),
            P(None, "ctx", "tp"),
            P(),
            P(None, "tp"),
            P("tp"),
            P(),
            P(),
            P("tp", None),
            P("tp"),
            P(None, "tp"),
            P("tp"),
            P("tp", None),
            P("tp"),
            P("tp"),
            P("tp"),
            P("tp"),
            P("tp"),
        ),
        check_vma=False,
    )
```

profile of v0, /device:TPU:0, one launch (start us, length us, event | category | flops | bytes accessed | tf_op | source)
XLA Modules:
  0.0 1649.1 jit_solution(4123834332571096811)
XLA Ops:
  10.5 8.5 all-reduce.4
  22.4 34.9 %all-gather.6.cloned.1.call-done = bf16[1024,2048]{1,0:T(8,128)(2,1)} async-done(((bf16[1024,512]{1,0:T(8,128)(2,1)}), bf16[1024,2048]{1,0:T(8,128)(2,1)}) %all-gather.6.cloned.1.call-update) | async-done | bytes 4194320 | tf_op jit(solution)/shard_map/all_gather | solution.py:40
  57.2 4.2 fusion.107
  61.8 5.2 add_convert_fusion.1
  69.6 65.4 %all-gather.8.cloned.1.call-done = bf16[2,4096,256]{2,1,0:T(8,128)(2,1)} async-done(((bf16[2,512,256]{2,1,0:T(8,128)(2,1)}), bf16[2,4096,256]{2,1,0:T(8,128)(2,1)}) %all-gather.8.cloned.1.call-update) | async-done | bytes 4194320 | tf_op jit(solution)/shard_map/all_gather | solution.py:119
  135.0 53.4 %while.52 = (s32[]{:T(128)}, f32[2,512,4]{1,2,0:T(4,128)S(1)}, f32[2,512,4]{1,2,0:T(4,128)S(1)}, s32[8]{0:T(128)S(1)}, s32[2]{0:T(128)S(1)}, /*index=5*/bf16[2,4...) while((s32[]{:T(128)}, f32[2,512,4]{1,2,0:T(4,128)S(1)}, ...), condition=%wide.region_7.8_spmd.clone.clone.clone, body=%wide.region_4.7_spmd.clone.clone.clone.sunk | while | flops 554473472 | bytes 20417756 | solution.py:106
  188.5 63.0 %while.53 = (s32[]{:T(128)}, f32[2,512,4,128]{3,1,2,0:T(8,128)}, s32[8]{0:T(128)S(1)}, s32[2]{0:T(128)S(1)}, bf16[2,4096,256]{2,1,0:T(8,128)(2,1)}, /*index=5*/b...) while((s32[]{:T(128)}, f32[2,512,4,128]{3,1,2,0:T(8,128)}, ...), condition=%wide.region_9.10_spmd.clone.clone.clone, body=%wide.region_8.9_spmd.clone.clone.clone.sunk | while | flops 1083983872 | bytes 7378156 | solution.py:106
  190.3 5.7 select_add_fusion.4
  197.9 6.0 select_add_fusion.4
  205.8 6.0 select_add_fusion.4
  213.7 6.0 select_add_fusion.4
  221.6 6.0 select_add_fusion.4
  229.6 6.0 select_add_fusion.4
  237.5 6.0 select_add_fusion.4
  245.4 6.0 select_add_fusion.4
  255.0 4.4 convolution_convert_fusion.5
  260.0 42.3 %reduce-scatter.6.cloned.1.call-done = bf16[1024,512]{1,0:T(8,128)(2,1)} async-done(((bf16[1024,2048]{1,0:T(8,128)(2,1)}), bf16[1024,512]{1,0:T(8,128)(2,1)}) %reduce-scatter.6.cloned.1.call-update) | async-done | bytes 1048592 | tf_op jit(solution)/shard_map/reduce_scatter | solution.py:44
  304.1 5.9 all-reduce.3
  313.3 35.3 %all-gather.10.cloned.1.call-done = bf16[1024,2048]{1,0:T(8,128)(2,1)} async-done(((bf16[1024,512]{1,0:T(8,128)(2,1)}), bf16[1024,2048]{1,0:T(8,128)(2,1)}) %all-gather.10.cloned.1.call-update) | async-done | bytes 4194320 | tf_op jit(solution)/shard_map/all_gather | solution.py:40
  348.6 12.5 fusion.129
  364.4 14.4 convolution_convert_fusion.4
  379.6 43.9 %reduce-scatter.8.cloned.1.call-done = bf16[1024,512]{1,0:T(8,128)(2,1)} async-done(((bf16[1024,2048]{1,0:T(8,128)(2,1)}), bf16[1024,512]{1,0:T(8,128)(2,1)}) %reduce-scatter.8.cloned.1.call-update) | async-done | bytes 1048592 | tf_op jit(solution)/shard_map/reduce_scatter | solution.py:44
  423.5 4.6 fusion.122
  428.4 34.4 %all-gather.12.cloned.1.call-done = bf16[1024,2048]{1,0:T(8,128)(2,1)} async-done(((bf16[1024,512]{1,0:T(8,128)(2,1)}), bf16[1024,2048]{1,0:T(8,128)(2,1)}) %all-gather.12.cloned.1.call-update) | async-done | bytes 4194320 | tf_op jit(solution)/shard_map/all_gather | solution.py:40
  462.8 19.2 %fusion.124 = (bf16[2048]{0:T(1024)(128)(2,1)}, bf16[1024,2048]{1,0:T(8,128)(2,1)S(1)}) fusion(f32[1024,2048]{1,0:T(8,128)} %copy-done.34, f32[2048]{0:T(1024)S(1)} %convert_element_type.231, bf16[1024,2048]{1,0:T(8,128)(2,1)} %all-gather.12.cloned.1.call-done, bf16[2048,2048]{1,0:T(8,128)(2,1)} %param.36), kind=kOutput, calls=%fused_computation.213 | convolution fusion | flops 8636069888 | bytes 25178112 | tf_op jit(solution)/shard_map/dot_general | solution.py:56
  484.0 12.8 convolution_convert_fusion.3
  496.9 44.6 %reduce-scatter.10.cloned.1.call-done = bf16[1024,512]{1,0:T(8,128)(2,1)} async-done(((bf16[1024,2048]{1,0:T(8,128)(2,1)}), bf16[1024,512]{1,0:T(8,128)(2,1)}) %reduce-scatter.10.cloned.1.call-update) | async-done | bytes 1048592 | tf_op jit(solution)/shard_map/reduce_scatter | solution.py:44
  541.5 5.5 fusion.88
  547.0 5.8 all-reduce.2
  552.8 5.5 fusion.126
  560.0 34.1 %all-gather.14.cloned.1.call-done = bf16[1024,2048]{1,0:T(8,128)(2,1)} async-done(((bf16[1024,512]{1,0:T(8,128)(2,1)}), bf16[1024,2048]{1,0:T(8,128)(2,1)}) %all-gather.14.cloned.1.call-update) | async-done | bytes 4194320 | tf_op jit(solution)/shard_map/all_gather | solution.py:40
  594.1 5.5 convolution_convert_fusion.9
  609.2 162.2 %while.54 = (s32[]{:T(128)}, f32[2,512,4,128]{3,1,2,0:T(8,128)S(1)}, bf16[2,4096,256]{2,1,0:T(8,128)(2,1)}, s32[8]{0:T(128)S(1)}, s32[2]{0:T(128)S(1)}, /*index=...) while((s32[]{:T(128)}, ...), condition=%wide.region_23.24_spmd.clone.clone.clone, body=%wide.region_22.23_spmd.clone.clone.clone.sunk | while | flops 2708490240 | bytes 56954164 | solution.py:106
  616.2 3.8 fusion.195
  636.4 3.8 fusion.195
  641.7 3.5 select_add_fusion.5
  656.6 3.8 fusion.195
  661.9 3.5 select_add_fusion.5
  676.9 3.8 fusion.195
  682.2 3.5 select_add_fusion.5
  697.1 3.8 fusion.195
  702.4 3.5 select_add_fusion.5
  717.3 3.8 fusion.195
  722.6 3.5 select_add_fusion.5
  737.5 3.8 fusion.195
  742.8 3.5 select_add_fusion.5
  757.7 3.8 fusion.195
  763.0 3.5 select_add_fusion.5
  772.5 87.1 %reduce-scatter.14.cloned.1.call-done = bf16[2,512,256]{2,1,0:T(8,128)(2,1)} async-done(((bf16[2,4096,256]{2,1,0:T(8,128)(2,1)}), bf16[2,512,256]{2,1,0:T(8,128)(2,1)}) %reduce-scatter.14.cloned.1.call-update) | async-done | bytes 524304 | tf_op jit(solution)/shard_map/reduce_scatter | solution.py:238
  859.6 6.0 convolution_convert_fusion.2
  865.7 14.4 convolution_convert_fusion.1
  880.2 18.9 %convolution_convert_fusion = bf16[2048,2048]{1,0:T(8,128)(2,1)} fusion(bf16[1024,2048]{1,0:T(8,128)(2,1)S(1)} %copy-done.30, f32[1024,2048]{1,0:T(8,128)} %copy-done.34, f32[2048]{0:T(1024)S(1)} %convert_element_type.231), kind=kOutput, calls=%fused_computation.128 | convolution fusion | flops 8615100416 | bytes 20979712 | tf_op jit(solution)/shard_map/dot_general | solution.py:50
  899.1 3.8 convolution_convert_fusion.6
  902.8 3.8 convolution_convert_fusion.7
  906.6 5.0 convolution_convert_fusion.8
  913.0 40.8 %psum.177 = f32[]{:T(128)} all-reduce(f32[]{:T(128)} %get-tuple-element.817), channel_id=1, replica_groups=mesh['ctx'=8,'tp'=4] {'ctx','tp'}, use_global_device_ids=true, to_apply=%region_32.33 | all-reduce | flops 1 | bytes 8 | tf_op jit(solution)/shard_map/psum | solution.py:282
  954.7 4.0 fusion.105
  958.7 38.5 %all-reduce.5 = (bf16[512]{0:T(512)(128)(2,1)S(1)}, bf16[128]{0:T(256)(128)(2,1)S(1)}, bf16[512]{0:T(512)(128)(2,1)S(1)}, bf16[2048]{0:T(1024)(128)(2,1)S(1)}, b...) all-reduce(bf16[512]{0:T(512)(128)(2,1)S(1)} %bitcast.280, ...), channel_id=1, replica_groups=mesh['ctx'=8,'tp'=4] {'ctx'}, use_global_device_ids=true, to_apply=%region_36.37 | all-reduce | flops 5760 | bytes 23040 | tf_op jit(solution)/shard_map/psum | solution.py:268
  1002.4 6.1 all-reduce.1
  1008.5 4.1 fusion.104
  1012.6 596.4 %all-reduce.12.cloned.1.call-done = (bf16[2048,512]{1,0:T(8,128)(2,1)}, bf16[2048,256]{1,0:T(8,128)(2,1)}, bf16[512,2048]{1,0:T(8,128)(2,1)}, bf16[2048,2048]{1,0:T(8,128)(2,1)}, bf16[2048,2048]{1,0:T(8,128)(2,1)}) async-done(((bf16[2048,512]{1,0:T(8,128)(2,1)}, bf16[2048,256]{1,0:T(8,128)(2,1)}, bf16[512,2048]{1,0:T(8,128)(2,1)}, bf16[2048,2048]{1,0:T(8,128)(2,1)}, bf16[2048,2048]{1,0:T(8,128)(2,1)}), ...) | async-done | bytes 22020112 | tf_op jit(solution)/shard_map/psum | solution.py:267
  1609.0 4.3 convert_element_type.253
  1617.3 11.7 convert_element_type.262
  1629.0 11.8 convert_element_type.265
  (448 shorter events, 205.0 us)
Async XLA Ops:
  7.2 247.8 %copy-start = (bf16[512,2048]{1,0:T(8,128)(2,1)S(1)}, bf16[512,2048]{1,0:T(8,128)(2,1)}, u32[]{:S(2)}) copy-start(bf16[512,2048]{1,0:T(8,128)(2,1)} %param.32) | copy-start | bytes 6291460
  7.2 15.1 copy-start.33
  7.2 50.0 %copy-start.32 = (bf16[2048,256]{1,0:T(8,128)(2,1)S(1)}, bf16[2048,256]{1,0:T(8,128)(2,1)}, u32[]{:S(2)}) copy-start(bf16[2048,256]{1,0:T(8,128)(2,1)} %param.30) | copy-start | bytes 3145732
  7.2 50.0 %all-gather.6.cloned.1.call-start = ((), (), s32[]{:S(2)}) async-start(), calls=%async_computation.5 | async-start | bytes 5242880 | tf_op jit(solution)/shard_map/all_gather | solution.py:40
  8.1 53.4 %copy-start.16 = (f32[512]{0:T(512)}, f32[512]{0:T(512)S(1)}, u32[]{:S(2)}) copy-start(f32[512]{0:T(512)S(1)} %convert_element_type.217) | copy-start | bytes 6148
  19.0 0.6 copy-start.12
  19.0 0.6 copy-start.14
  22.3 112.7 %all-gather.8.cloned.1.call-start = ((), (), s32[]{:S(2)}) async-start(), calls=%async_computation.6 | async-start | bytes 4718592 | tf_op jit(solution)/shard_map/all_gather | solution.py:119
  22.4 39.4 %copy-start.24 = (bf16[512]{0:T(512)(128)(2,1)S(1)}, bf16[512]{0:T(512)(128)(2,1)}, u32[]{:S(2)}) copy-start(bf16[512]{0:T(512)(128)(2,1)} %param.29) | copy-start | bytes 3076
  61.5 240.8 %reduce-scatter.6.cloned.1.call-start = ((), (), s32[]{:S(2)}) async-start(), calls=%async_computation.7 | async-start | bytes 5242880 | tf_op jit(solution)/shard_map/reduce_scatter | solution.py:44
  67.0 68.0 %copy-start.10 = (s32[2]{0:T(128)S(1)}, s32[2]{0:T(128)}, u32[]{:S(2)}) copy-start(s32[2]{0:T(128)} %param.25) | copy-start | bytes 28
  254.0 1.0 copy-start.7
  259.3 0.7 copy-start.25
  259.3 0.7 copy-start.26
  259.3 0.7 copy-start.27
  259.3 43.0 %copy-start.3 = (bf16[2,512,512]{2,1,0:T(8,128)(2,1)S(1)}, bf16[2,512,512]{2,1,0:T(8,128)(2,1)}, u32[]{:S(2)}) copy-start(bf16[2,512,512]{2,1,0:T(8,128)(2,1)} %param.24) | copy-start | bytes 3145732
  259.4 53.9 %copy-start.20 = (bf16[2048]{0:T(1024)(128)(2,1)S(1)}, bf16[2048]{0:T(1024)(128)(2,1)}, u32[]{:S(2)}) copy-start(bf16[2048]{0:T(1024)(128)(2,1)} %param.35) | copy-start | bytes 12292
  259.4 89.2 %all-gather.10.cloned.1.call-start = ((), (), s32[]{:S(2)}) async-start(), calls=%async_computation.8 | async-start | bytes 5242880 | tf_op jit(solution)/shard_map/all_gather | solution.py:40
  312.8 110.7 %reduce-scatter.8.cloned.1.call-start = ((), (), s32[]{:S(2)}) async-start(), calls=%async_computation.9 | async-start | bytes 5242880 | tf_op jit(solution)/shard_map/reduce_scatter | solution.py:44
  361.0 3.4 copy-start.34
  378.8 0.7 copy-start.28
  378.8 84.0 %all-gather.12.cloned.1.call-start = ((), (), s32[]{:S(2)}) async-start(), calls=%async_computation.10 | async-start | bytes 5242880 | tf_op jit(solution)/shard_map/all_gather | solution.py:40
  428.2 113.4 %reduce-scatter.10.cloned.1.call-start = ((), (), s32[]{:S(2)}) async-start(), calls=%async_computation.11 | async-start | bytes 5242880 | tf_op jit(solution)/shard_map/reduce_scatter | solution.py:44
  482.0 2.0 copy-start.35
  496.8 97.3 %all-gather.14.cloned.1.call-start = ((), (), s32[]{:S(2)}) async-start(), calls=%async_computation.12 | async-start | bytes 5242880 | tf_op jit(solution)/shard_map/all_gather | solution.py:40
  558.4 301.2 %reduce-scatter.14.cloned.1.call-start = ((), (), s32[]{:S(2)}) async-start(), calls=%async_computation.14 | async-start | bytes 4718592 | tf_op jit(solution)/shard_map/reduce_scatter | solution.py:238
  601.8 7.3 copy-start.2
  611.5 2.3 copy-start.9
  631.7 2.3 copy-start.9
  651.9 2.3 copy-start.9
  672.2 2.3 copy-start.9
  692.4 2.3 copy-start.9
  712.6 2.3 copy-start.9
  732.8 2.3 copy-start.9
  753.0 2.3 copy-start.9
  771.3 135.3 %all-reduce.10.cloned.1.call-start = ((), (), s32[]{:S(2)}) async-start(), calls=%async_computation.15 | async-start | bytes 1048576 | tf_op jit(solution)/shard_map/psum | solution.py:239
  859.6 95.0 %reduce-scatter.12.cloned.1.call-start = ((), (), s32[]{:S(2)}) async-start(), calls=%async_computation.13 | async-start | bytes 5242880 | tf_op jit(solution)/shard_map/reduce_scatter | solution.py:44
  865.7 743.3 %all-reduce.12.cloned.1.call-start = ((), (), s32[]{:S(2)}) async-start(), calls=%async_computation.16 | async-start | bytes 44040192 | tf_op jit(solution)/shard_map/psum | solution.py:267
  865.7 14.4 copy-start.30
  880.1 18.9 %copy-start.8 = (bf16[2,512,4,128]{3,2,1,0:T(4,128)(2,1)S(1)}, bf16[2,512,4,128]{3,2,1,0:T(4,128)(2,1)}, u32[]{:S(2)}) copy-start(bf16[2,512,4,128]{3,2,1,0:T(4,128)(2,1)} %copy-done.7) | copy-start | bytes 3145732
  880.2 18.9 %copy-start.31 = (bf16[1024,2048]{1,0:T(8,128)(2,1)S(1)}, bf16[1024,2048]{1,0:T(8,128)(2,1)}, u32[]{:S(2)}) copy-start(bf16[1024,2048]{1,0:T(8,128)(2,1)} %all-gather.14.cloned.1.call-done) | copy-start | bytes 12582916
  899.0 3.8 copy-start.29
  911.6 42.8 %copy-start.11 = (bf16[1024,256]{1,0:T(8,128)(2,1)S(1)}, bf16[1024,256]{1,0:T(8,128)(2,1)}, u32[]{:S(2)}) copy-start(bf16[1024,256]{1,0:T(8,128)(2,1)} %all-reduce.10.cloned.1.call-done) | copy-start | bytes 1572868
  911.6 43.0 %copy-start.4 = (bf16[2,512,512]{2,1,0:T(8,128)(2,1)S(1)}, bf16[2,512,512]{2,1,0:T(8,128)(2,1)}, u32[]{:S(2)}) copy-start(bf16[2,512,512]{2,1,0:T(8,128)(2,1)} %param.24) | copy-start | bytes 3145732
  911.6 43.0 %copy-start.13 = (f32[1024]{0:T(1024)S(1)}, f32[1024]{0:T(1024)}, u32[]{:S(2)}) copy-start(f32[1024]{0:T(1024)} %copy-done.12) | copy-start | bytes 12292
  911.6 43.0 %copy-start.15 = (f32[1024]{0:T(1024)S(1)}, f32[1024]{0:T(1024)}, u32[]{:S(2)}) copy-start(f32[1024]{0:T(1024)} %copy-done.14) | copy-start | bytes 12292
  911.6 43.0 %copy-start.17 = (f32[512]{0:T(512)S(1)}, f32[512]{0:T(512)}, u32[]{:S(2)}) copy-start(f32[512]{0:T(512)} %copy-done.16) | copy-start | bytes 6148
  911.7 47.0 %copy-start.18 = (bf16[512]{0:T(512)(128)(2,1)S(1)}, bf16[512]{0:T(512)(128)(2,1)}, u32[]{:S(2)}) copy-start(bf16[512]{0:T(512)(128)(2,1)} %get-tuple-element.904) | copy-start | bytes 3076
  911.7 47.0 %copy-start.19 = (bf16[512]{0:T(512)(128)(2,1)S(1)}, bf16[512]{0:T(512)(128)(2,1)}, u32[]{:S(2)}) copy-start(bf16[512]{0:T(512)(128)(2,1)} %get-tuple-element.918) | copy-start | bytes 3076
  911.7 47.0 %copy-start.21 = (bf16[2048]{0:T(1024)(128)(2,1)S(1)}, bf16[2048]{0:T(1024)(128)(2,1)}, u32[]{:S(2)}) copy-start(bf16[2048]{0:T(1024)(128)(2,1)} %get-tuple-element.902) | copy-start | bytes 12292
  911.7 47.0 %copy-start.22 = (bf16[512]{0:T(512)(128)(2,1)S(1)}, bf16[512]{0:T(512)(128)(2,1)}, u32[]{:S(2)}) copy-start(bf16[512]{0:T(512)(128)(2,1)} %get-tuple-element.900) | copy-start | bytes 3076
  911.7 47.0 %copy-start.23 = (bf16[512]{0:T(512)(128)(2,1)S(1)}, bf16[512]{0:T(512)(128)(2,1)}, u32[]{:S(2)}) copy-start(bf16[512]{0:T(512)(128)(2,1)} %get-tuple-element.812) | copy-start | bytes 3076
  1609.0 4.4 copy-start.6
  1609.0 5.8 copy-start.5
  1629.0 11.8 copy-start.1
Sparse Core Ops, SparseCore 0:
  22.4 34.7 all-gather.5
  61.6 73.3 all-gather.7
  259.5 42.7 reduce-scatter.5
  312.9 35.5 all-gather.9
  379.0 44.5 reduce-scatter.7
  428.3 34.4 all-gather.11
  497.0 44.5 reduce-scatter.9
  558.5 35.6 all-gather.13
  771.5 88.0 reduce-scatter.13
  861.8 32.9 all-reduce.9
  897.9 45.2 reduce-scatter.11
  950.1 658.8 all-reduce.11
where the time goes:
time: 1650 us
  waiting for transfers between devices  1020 us (62%)
  matrix products  310 us (19%)
  other arithmetic  112 us (7%)
  blocking collectives  106 us (6%)
  local copies, waits for them, and re-layouts  66.5 us (4%)
  loops' own time  17.8 us (1%)
  between operations  17.5 us (1%)
    psum x1, waiting for transfers between devices, shards(): lax.psum(grad_w_query.astype(jnp.bfloat16), 'ctx').astype(jnp.float32)  596 us
    all_gather x4, waiting for transfers between devices, full_rows(): return lax.all_gather(values, 'tp', axis=1, tiled=True)  139 us
    reduce_scatter x4, waiting for transfers between devices, shard_sums(): lax.psum_scatter(partial_value.astype(jnp.bfloat16), 'tp', scatter_dimens...  131 us
    reduce_scatter x1, waiting for transfers between devices, shards(): lax.psum_scatter(d_keyval.astype(jnp.bfloat16), 'ctx', scatter_dimension=...  87.1 us
    all_gather x1, waiting for transfers between devices, shards(): every_kv = lax.all_gather(keyval, 'ctx', axis=1, tiled=True)  65.4 us
    dot_general x8, matrix products, mix_step(): jnp.einsum('sqhk,skd->sqhd', weights, piece[..., head:], preferred_elemen...  48 us
    dot_general x5, matrix products, contract_cols(): lax.dot_general(left, right, (((1,), (1,)), ((), ())), preferred_element_...  47.5 us
    dot_general x5, matrix products, contract_rows(): lax.dot_general(left, right, (((0,), (0,)), ((), ())), preferred_element_...  45.9 us
  transfers between devices with their start and end apart: 12, of which 10 were waited for; matrix products, arithmetic and copies ran while one was open for 5% of the time, Pallas kernels for 0%

commit v1 on v0

v1 whole, which is shorter than its diff:
```python
import functools
import math

import jax
import jax.numpy as jnp
from jax import lax
from jax.experimental import pallas as pl
from jax.experimental.pallas import tpu as pltpu
from jax.sharding import PartitionSpec as P

BLOCK = 256
EPS = 1e-05
NEG = -1e30
LOG2E = math.log2(math.e)
CORES = 2
MIB = 2**20
F32 = jnp.float32
BF16 = jnp.bfloat16


def dot_nn(left, right):
    return lax.dot_general(left, right, (((1,), (0,)), ((), ())), preferred_element_type=F32)


def dot_nt(left, right):
    return lax.dot_general(left, right, (((1,), (1,)), ((), ())), preferred_element_type=F32)


def dot_tn(left, right):
    return lax.dot_general(left, right, (((0,), (0,)), ((), ())), preferred_element_type=F32)


def attend_kernel(heads, head, rows, per, info, q_ref, kv_ref, mix_ref, att_ref, lse_ref, acc, top):
    block = pl.program_id(0)
    length, position = info[0], info[1]
    scale = head**-0.5 * LOG2E
    keys = jnp.minimum((position * pl.num_programs(0) + block + 1) * BLOCK, length)
    chunk = per * rows
    acc[...] = jnp.zeros_like(acc)
    top[...] = jnp.full_like(top, NEG)

    def step(index, masked):
        start = index * chunk
        spots = [pl.multiple_of(info[2 + index * per + i] * rows, rows) for i in range(per)]
        k = jnp.concatenate([kv_ref[pl.ds(spot, rows), :head] for spot in spots], axis=0)
        v = jnp.concatenate([kv_ref[pl.ds(spot, rows), head:] for spot in spots], axis=0)
        wide = jnp.concatenate([v, jnp.ones_like(v)], axis=1)
        for h in range(heads):
            s = dot_nt(q_ref[:, h * head : (h + 1) * head], k) * scale
            if masked:
                col = start + lax.broadcasted_iota(jnp.int32, s.shape, 1)
                s = jnp.where(col < keys, s, NEG)
            old = top[h]
            new = jnp.maximum(old, jnp.max(s, axis=1, keepdims=True))
            p = jnp.exp2(s - new[:, :1])
            top[h] = new
            acc[h] = acc[h] * jnp.exp2(old - new)[:, :1] + dot_nn(p.astype(BF16), wide)

    def body(index, carry):
        step(index, False)
        return carry

    whole = keys // chunk
    lax.fori_loop(0, whole, body, 0)

    @pl.when(keys % chunk != 0)
    def _():
        step(whole, True)

    for h in range(heads):
        cols = slice(h * head, (h + 1) * head)
        total = acc[h][:, head:]
        mixed = acc[h][:, :head] / total
        mix_ref[:, cols] = mixed
        att_ref[:, cols] = mixed.astype(BF16)
        lse_ref[:, cols] = top[h] + jnp.log2(total)


def attend(q, kv, info, head):
    rows, width = q.shape
    full = kv.shape[0]
    heads = width // head
    per = math.gcd(full // rows, max(1, 1024 // rows))
    block = pl.BlockSpec((BLOCK, width), lambda i, info: (i, 0))
    pairs = rows * heads * full
    return pl.pallas_call(
        functools.partial(attend_kernel, heads, head, rows, per),
        grid_spec=pltpu.PrefetchScalarGridSpec(
            num_scalar_prefetch=1,
            grid=(rows // BLOCK,),
            in_specs=[block, pl.BlockSpec((full, 2 * head), lambda i, info: (0, 0))],
            out_specs=[block, block, block],
            scratch_shapes=[
                pltpu.VMEM((heads, BLOCK, 2 * head), F32),
                pltpu.VMEM((heads, BLOCK, head), F32),
            ],
        ),
        out_shape=[
            jax.ShapeDtypeStruct((rows, width), F32),
            jax.ShapeDtypeStruct((rows, width), BF16),
            jax.ShapeDtypeStruct((rows, width), F32),
        ],
        compiler_params=pltpu.CompilerParams(vmem_limit_bytes=40 * MIB),
        cost_estimate=pl.CostEstimate(
            flops=8 * pairs * head, bytes_accessed=4 * MIB, transcendentals=pairs
        ),
    )(info, q, kv)


def attend_back_kernel(
    heads, head, rows, per, info, q_ref, do_ref, mix_ref, lse_ref, kv_ref, dq_ref, dkv_ref, dkv, dq, dlt
):
    block = pl.program_id(0)
    length, position = info[0], info[1]
    blocks = pl.num_programs(0)
    factor = head**-0.5
    scale = factor * LOG2E
    chunk = per * rows
    first = (position * blocks + block) * BLOCK
    keys = jnp.where(first < length, jnp.minimum(first + BLOCK, length), 0)

    @pl.when(block == 0)
    def _():
        dkv[...] = jnp.zeros_like(dkv)

    dq[...] = jnp.zeros_like(dq)
    for h in range(heads):
        cols = slice(h * head, (h + 1) * head)
        delta = jnp.sum(do_ref[:, cols].astype(F32) * mix_ref[:, cols], axis=1, keepdims=True)
        dlt[h] = jnp.broadcast_to(delta, (BLOCK, head))

    def step(index, masked):
        start = index * chunk
        spots = [pl.multiple_of(info[2 + index * per + i] * rows, rows) for i in range(per)]
        k = jnp.concatenate([kv_ref[pl.ds(spot, rows), :head] for spot in spots], axis=0)
        v = jnp.concatenate([kv_ref[pl.ds(spot, rows), head:] for spot in spots], axis=0)
        dk_sum = dv_sum = None
        for h in range(heads):
            cols = slice(h * head, (h + 1) * head)
            q, do = q_ref[:, cols], do_ref[:, cols]
            p = jnp.exp2(dot_nt(q, k) * scale - lse_ref[:, h * head : h * head + 1])
            if masked:
                col = start + lax.broadcasted_iota(jnp.int32, p.shape, 1)
                p = jnp.where(col < keys, p, 0.0)
            ds = (p * (dot_nt(do, v) - dlt[h][:, :1])).astype(BF16)
            dq[h] += dot_nn(ds, k)
            dk, dv = dot_tn(ds, q), dot_tn(p.astype(BF16), do)
            dk_sum, dv_sum = (dk, dv) if h == 0 else (dk_sum + dk, dv_sum + dv)
        for i, spot in enumerate(spots):
            part = slice(i * rows, (i + 1) * rows)
            dkv[pl.ds(spot, rows), :head] += dk_sum[part]
            dkv[pl.ds(spot, rows), head:] += dv_sum[part]

    def body(index, carry):
        step(index, False)
        return carry

    whole = keys // chunk
    lax.fori_loop(0, whole, body, 0)

    @pl.when(keys % chunk != 0)
    def _():
        step(whole, True)

    for h in range(heads):
        dq_ref[:, h * head : (h + 1) * head] = (dq[h] * factor).astype(BF16)

    @pl.when(block == blocks - 1)
    def _():
        dkv_ref[:, :head] = (dkv[:, :head] * factor).astype(BF16)
        dkv_ref[:, head:] = dkv[:, head:].astype(BF16)


def attend_back(q, do, mixed, lse, kv, info, head):
    rows, width = q.shape
    full = kv.shape[0]
    heads = width // head
    per = math.gcd(full // rows, max(1, 1024 // rows))
    block = pl.BlockSpec((BLOCK, width), lambda i, info: (i, 0))
    whole = pl.BlockSpec((full, 2 * head), lambda i, info: (0, 0))
    pairs = rows * heads * full
    return pl.pallas_call(
        functools.partial(attend_back_kernel, heads, head, rows, per),
        grid_spec=pltpu.PrefetchScalarGridSpec(
            num_scalar_prefetch=1,
            grid=(rows // BLOCK,),
            in_specs=[block, block, block, block, whole],
            out_specs=[block, whole],
            scratch_shapes=[
                pltpu.VMEM((full, 2 * head), F32),
                pltpu.VMEM((heads, BLOCK, head), F32),
                pltpu.VMEM((heads, BLOCK, head), F32),
            ],
        ),
        out_shape=[
            jax.ShapeDtypeStruct((rows, width), BF16),
            jax.ShapeDtypeStruct((full, 2 * head), BF16),
        ],
        compiler_params=pltpu.CompilerParams(vmem_limit_bytes=56 * MIB),
        cost_estimate=pl.CostEstimate(
            flops=12 * pairs * head, bytes_accessed=8 * MIB, transcendentals=pairs
        ),
    )(info, q, do, mixed, lse, kv)


def grad_kernel(count, *refs):
    total = dot_tn(refs[0][...], refs[count][...])
    for i in range(1, count):
        total += dot_tn(refs[i][...], refs[count + i][...])
    refs[-1][...] = total.astype(BF16)


def weight_grad(lefts, rights):
    rows, m = lefts[0].shape
    n = rights[0].shape[1]
    bm = min(m, 256)
    count = len(lefts)
    return pl.pallas_call(
        functools.partial(grad_kernel, count),
        grid=(m // bm,),
        in_specs=[pl.BlockSpec((rows, bm), lambda i: (0, i))] * count
        + [pl.BlockSpec((rows, n), lambda i: (0, 0))] * count,
        out_specs=pl.BlockSpec((bm, n), lambda i: (i, 0)),
        out_shape=jax.ShapeDtypeStruct((m, n), BF16),
        compiler_params=pltpu.CompilerParams(vmem_limit_bytes=40 * MIB),
        cost_estimate=pl.CostEstimate(
            flops=2 * count * rows * m * n,
            bytes_accessed=2 * (count * rows * (m + n) + m * n),
            transcendentals=0,
        ),
    )(*lefts, *rights)


def place_kernel(index, block_ref, out_ref):
    out_ref[...] = block_ref[...].astype(F32)


def place_first(block, index, shape):
    rows, cols = block.shape
    steps = max(1, rows // 128)
    return pl.pallas_call(
        place_kernel,
        grid_spec=pltpu.PrefetchScalarGridSpec(
            num_scalar_prefetch=1,
            grid=(steps,),
            in_specs=[pl.BlockSpec((rows // steps, cols), lambda i, index: (i, 0))],
            out_specs=pl.BlockSpec((rows // steps, cols), lambda i, index: (index[0] * steps + i, 0)),
        ),
        out_shape=jax.ShapeDtypeStruct(shape, F32),
        compiler_params=pltpu.CompilerParams(vmem_limit_bytes=60 * MIB),
        cost_estimate=pl.CostEstimate(
            flops=0, bytes_accessed=6 * rows * cols, transcendentals=0
        ),
    )(index.astype(jnp.int32).reshape(1), block)


def place_of(axis):
    return lax.axis_index(axis).astype(jnp.uint32)


def tp_place():
    t = place_of("tp")
    return lax.div(t, jnp.uint32(CORES)), lax.rem(t, jnp.uint32(CORES))


def shifted(place, shift, size):
    return lax.rem(place + jnp.uint32(shift + 2 * size), jnp.uint32(size))


def rows_at(source, index, count):
    return lax.dynamic_slice_in_dim(source, index * jnp.uint32(count), count, 0)


def cols_at(source, index, count):
    return lax.dynamic_slice_in_dim(source, index * jnp.uint32(count), count, 1)


def put_rows(target, block, index):
    zero = jnp.uint32(0)
    return lax.dynamic_update_slice(target, block, (index * jnp.uint32(block.shape[0]), zero))


def tp_pairs(size, shift, flip):
    rows = size // CORES
    return [
        (y * CORES + c, (y + shift) % rows * CORES + (c ^ flip))
        for y in range(rows)
        for c in range(CORES)
    ]


def after(value, *before):
    return lax.optimization_barrier((value, before))[0]


def tp_near(values):
    size = lax.axis_size("tp")
    return [values] + [
        lax.ppermute(values, "tp", tp_pairs(size, k, 0)) for k in range(1, size // CORES)
    ]


def tp_cross(near):
    return [(v, lax.ppermute(v, "tp", tp_pairs(lax.axis_size("tp"), 0, 1))) for v in near]


def tp_ordered(blocks):
    rows = len(blocks)
    y, c = tp_place()
    out = []
    for want in range(rows):
        for core in range(CORES):
            picks = [jnp.where(c == core, own, other) for own, other in blocks]
            chosen = picks[0]
            for k in range(1, rows):
                chosen = jnp.where(y == (want + k) % rows, picks[k], chosen)
            out.append(chosen)
    return out


def tp_join(near):
    return jnp.concatenate(tp_ordered(tp_cross(near)), axis=1)


class TpSum:
    def __init__(self, partial_sum):
        self.size = lax.axis_size("tp")
        self.rows = self.size // CORES
        self.width = partial_sum.shape[1] // self.size
        self.y, c = tp_place()

        def side(core):
            blocks = [
                cols_at(partial_sum, jnp.uint32(i * CORES) + core, self.width)
                for i in range(self.rows)
            ]
            return jnp.concatenate(blocks, axis=1)

        self.kept = side(c)
        self.arrived = lax.ppermute(side(jnp.uint32(1) - c), "tp", tp_pairs(self.size, 0, 1))

    def across(self, clock):
        def add(kept, arrived):
            return (kept.astype(F32) + arrived.astype(F32)).astype(BF16)

        self.pair = clock(add, self.kept, self.arrived)
        self.moved = [
            lax.ppermute(
                cols_at(self.pair, shifted(self.y, k, self.rows), self.width),
                "tp",
                tp_pairs(self.size, k, 0),
            )
            for k in range(1, self.rows)
        ]

    def total(self, pair, moved):
        total = cols_at(pair, self.y, self.width).astype(F32)
        for part in moved:
            total = total + part.astype(F32)
        return total


def tp_sum(values):
    size = lax.axis_size("tp")
    pair = values + lax.ppermute(values, "tp", tp_pairs(size, 0, 1))
    total = pair
    for k in range(1, size // CORES):
        total = total + lax.ppermute(pair, "tp", tp_pairs(size, k, 0))
    return total


def ring_order(size):
    across = 2 ** (int(math.log2(size)) // 2)
    down = size // across
    order = [a * across for a in range(down)]
    for i, a in enumerate(reversed(range(down))):
        turn = range(1, across) if i % 2 == 0 else reversed(range(1, across))
        order += [a * across + b for b in turn]
    return order


def ring_table():
    order = ring_order(lax.axis_size("ctx"))
    places = [order.index(i) for i in range(len(order))]
    table = jnp.array(places, jnp.uint32)
    own = lax.dynamic_index_in_dim(table, place_of("ctx"), keepdims=False)
    return order, table, own


def ring_shift(order, shift):
    size = len(order)
    return [(order[i], order[(i + shift) % size]) for i in range(size)]


class Clock:
    def __init__(self):
        self.last = []

    def __call__(self, work, *inputs):
        inputs, _ = lax.optimization_barrier((inputs, self.last))
        out = work(*inputs)
        self.last = jax.tree.leaves(out)
        return out


class Ring:
    def __init__(self, clock, grad, way):
        self.clock, self.grad, self.way = clock, grad, way
        self.order, _, self.place = ring_table()
        self.size = len(self.order)
        self.rows = grad.shape[0] // self.size
        self.step = 0
        self.out = None
        self.send(rows_at(grad, self.place, self.rows))

    def send(self, block):
        self.arrived = lax.ppermute(block, "ctx", ring_shift(self.order, self.way))

    def done(self):
        return self.step == 2 * (self.size - 1)

    def turn(self):
        if self.done():
            return
        self.step += 1
        n = self.size
        index = shifted(self.place, -self.way * self.step % n, n)

        def add(arrived):
            own = rows_at(self.grad, index, self.rows)
            return (arrived.astype(F32) + own.astype(F32)).astype(BF16)

        held = self.clock(add if self.step <= n - 1 else lambda arrived: arrived, self.arrived)
        if not self.done():
            self.send(held)
        if self.step == n - 1:
            self.out = self.clock(lambda block: place_first(block, index, self.grad.shape), held)
        elif self.step >= n:
            self.out = self.clock(
                lambda out, block: put_rows(out, block.astype(F32), index), self.out, held
            )


def grid_of(size):
    across = 2 ** (int(math.log2(size)) // 2)
    return size // across, across


class Grid:
    def __init__(self):
        self.down, self.across = grid_of(lax.axis_size("ctx"))
        me = place_of("ctx")
        self.a, self.b = lax.div(me, jnp.uint32(self.across)), lax.rem(me, jnp.uint32(self.across))

    def send_row(self, values, k):
        n = self.across
        pairs = [(a * n + b, a * n + (b + k) % n) for a in range(self.down) for b in range(n)]
        return lax.ppermute(values, "ctx", pairs)

    def send_column(self, values, k):
        n, m = self.across, self.down
        pairs = [(a * n + b, (a + k) % m * n + b) for a in range(m) for b in range(n)]
        return lax.ppermute(values, "ctx", pairs)


def added(parts):
    total = parts[0].astype(F32)
    for part in parts[1:]:
        total = total + part.astype(F32)
    return total.astype(BF16)


class GridGather(Grid):
    def __init__(self, values):
        super().__init__()
        self.flight = [values] + [self.send_row(values, j) for j in range(1, self.across)]

    def second(self, clock):
        row = clock(lambda *parts: jnp.concatenate(parts, axis=0), *self.flight)
        self.flight = [row] + [self.send_column(row, k) for k in range(1, self.down)]

    def joined(self, clock):
        return clock(lambda *parts: jnp.concatenate(parts, axis=0), *self.flight)


def grid_slots():
    grid = Grid()
    down, across = grid.down, grid.across
    every_a = jnp.array([i // across for i in range(down * across)], jnp.uint32)
    every_b = jnp.array([i % across for i in range(down * across)], jnp.uint32)
    k = lax.rem(grid.a + jnp.uint32(down) - every_a, jnp.full_like(every_a, down))
    j = lax.rem(grid.b + jnp.uint32(across) - every_b, jnp.full_like(every_b, across))
    return (k * jnp.uint32(across) + j).astype(jnp.int32)


class GridScatter(Grid):
    def __init__(self, clock, values):
        super().__init__()
        parts = values.reshape((self.down, self.across) + values.shape[1:])
        kept = clock(lambda v: [v[:, j] for j in range(self.across)], parts)
        self.flight = [kept[0]] + [self.send_row(kept[j], -j) for j in range(1, self.across)]

    def second(self, clock):
        held = clock(lambda *parts: added(parts), *self.flight)
        self.flight = [held[0]] + [self.send_column(held[k], -k) for k in range(1, self.down)]

    def result(self, clock):
        return clock(lambda *parts: added(parts), *self.flight)


class GridSum(Grid):
    def __init__(self, grad):
        super().__init__()
        self.half, self.block = grad.shape[0] // self.across, grad.shape[0] // lax.axis_size("ctx")
        self.shape = grad.shape
        self.flight = [rows_at(grad, self.b, self.half)] + [
            self.send_row(rows_at(grad, shifted(self.b, k, self.across), self.half), k)
            for k in range(1, self.across)
        ]

    def second(self, clock):
        held = clock(lambda *parts: added(parts), *self.flight)
        self.flight = [rows_at(held, self.a, self.block)] + [
            self.send_column(rows_at(held, shifted(self.a, k, self.down), self.block), k)
            for k in range(1, self.down)
        ]

    def third(self, clock):
        held = clock(lambda *parts: added(parts), *self.flight)
        self.flight = [held] + [self.send_column(held, k) for k in range(1, self.down)]

    def fourth(self, clock):
        def joined(*blocks):
            half = jnp.zeros((self.half, self.shape[1]), BF16)
            for k, block in enumerate(blocks):
                half = put_rows(half, block, shifted(self.a, -k, self.down))
            return half

        half = clock(joined, *self.flight)
        self.flight = [half] + [self.send_row(half, k) for k in range(1, self.across)]

    def result(self, clock, dtype=F32):
        def joined(*blocks):
            if self.across == 2:
                first, last = self.b == 0, self.b == 1
                sides = [jnp.where(first, *blocks), jnp.where(last, *blocks)]
                return jnp.concatenate(sides, axis=0).astype(dtype)
            out = jnp.zeros(self.shape, dtype)
            for k, block in enumerate(blocks):
                out = put_rows(out, block.astype(dtype), shifted(self.b, -k, self.across))
            return out

        return clock(joined, *self.flight)


class GridSmallSum(Grid):
    def __init__(self, values):
        super().__init__()
        self.flight = [values] + [self.send_row(values, k) for k in range(1, self.across)]

    def in_order(self, place, size, parts):
        rows = jnp.zeros((size,) + parts[0].shape, F32)
        for k, part in enumerate(parts):
            rows = put_rows(rows, part[None], shifted(place, -k, size))
        return jnp.sum(rows, axis=0)

    def second(self, clock):
        held = clock(lambda *parts: self.in_order(self.b, self.across, parts), *self.flight)
        self.flight = [held] + [self.send_column(held, k) for k in range(1, self.down)]

    def result(self, clock):
        return clock(lambda *parts: self.in_order(self.a, self.down, parts), *self.flight)


def row_stats(values):
    mean = jnp.mean(values, axis=-1, keepdims=True)
    centered = values - mean
    var = jnp.mean(centered * centered, axis=-1, keepdims=True)
    return mean, lax.rsqrt(var + EPS)


def gelu_and_slope(values):
    inner = math.sqrt(2.0 / math.pi)
    square = values * values
    tanh = jnp.tanh(inner * values * (1.0 + 0.044715 * square))
    slope = 0.5 * (1.0 + tanh) + 0.5 * values * (1.0 - tanh * tanh) * inner * (
        1.0 + 3.0 * 0.044715 * square
    )
    return 0.5 * values * (1.0 + tanh), slope


def column_sum(values):
    return jnp.sum(values.astype(F32), axis=0)


def shards(
    tokens,
    lengths,
    teacher,
    out_grad,
    w_query,
    b_query,
    w_keyval,
    b_value,
    w_output,
    b_output,
    w_expand,
    b_expand,
    w_shrink,
    b_shrink,
    gain_first,
    bias_first,
    gain_second,
    bias_second,
):
    seqs, rows, part = tokens.shape
    width = w_query.shape[0]
    head = w_keyval.shape[1] // 2
    every = range(seqs)
    position = lax.axis_index("ctx")
    tp_index = place_of("tp")
    y, core = tp_place()
    core_swap = tp_pairs(lax.axis_size("tp"), 0, 1)
    query_pos = position * rows + jnp.arange(rows, dtype=jnp.int32)
    slots = grid_slots()
    info = [
        jnp.concatenate([jnp.stack([lengths[s], position]).astype(jnp.int32), slots]) for s in every
    ]

    def own_cols(values):
        return cols_at(values, tp_index, part)

    def norm_one(values):
        mean, factor = row_stats(values)
        normed = ((values - mean) * factor * full_gain_first + full_bias_first).astype(BF16)
        return (mean, factor), normed

    def my_half(normed):
        return (dot_nn(normed, my_w_kv) + my_kv_bias).astype(BF16)

    def to_queries(normed):
        return (dot_nn(normed, w_query) + b_query.astype(F32)).astype(BF16)

    def both_halves(mine, other):
        sides = [jnp.where(core == 0, mine, other), jnp.where(core == 0, other, mine)]
        return jnp.concatenate(sides, axis=1)

    def norm_two(s, *blocks):
        heads_all = jnp.concatenate(tp_ordered(pairs_of(blocks)), axis=1)
        mid = inputs[s] + dot_nn(heads_all, w_output_all) + full_b_output
        mean, factor = row_stats(mid)
        normed = ((mid - mean) * factor * full_gain_second + full_bias_second).astype(BF16)
        return mid, (mean, factor), normed

    def expand(normed):
        act, slp = gelu_and_slope(dot_nn(normed, w_expand) + b_expand.astype(F32))
        return act.astype(BF16), slp.astype(BF16)

    def pairs_of(flat):
        return [(flat[i], flat[i + 1]) for i in range(0, len(flat), 2)]

    def crossed(near):
        return [block for pair in tp_cross(near) for block in pair]

    def joined(*blocks):
        return jnp.concatenate(tp_ordered(pairs_of(blocks)), axis=1)

    def finish(s, total, pair, moved):
        final = own_cols(middle[s]) + total(pair, moved) + b_shrink.astype(F32)
        valid = (query_pos < lengths[s]).astype(F32)[:, None]
        weight_out = out_grad[s].astype(F32)
        diff = final - teacher[s].astype(F32)
        value = jnp.sum(valid * (weight_out * final + 0.5 * diff * diff))
        grad = valid * (weight_out + diff)
        return final.astype(BF16), value, grad, grad.astype(BF16)

    def hidden_grad(s, grad):
        return (dot_nt(grad, w_shrink) * slope[s].astype(F32)).astype(BF16)

    kv_bias = jnp.concatenate([jnp.zeros((head,), F32), b_value.astype(F32)])
    my_w_kv = cols_at(w_keyval, core, head)
    my_kv_bias = rows_at(kv_bias, core, head)
    clock = Clock()
    source = clock(lambda t: t, tokens[0])
    near0 = tp_near(source)
    w_output_all = lax.all_gather(w_output, "tp", axis=0, tiled=True)
    vectors = (gain_first, bias_first, gain_second, bias_second, b_output)
    vectors = clock(lambda *v: jnp.stack(v), *vectors)
    vectors = tp_join(tp_near(vectors)).astype(F32)
    full_gain_first, full_bias_first, full_gain_second, full_bias_second, full_b_output = vectors
    own_gain_first, own_gain_second = gain_first.astype(F32), gain_second.astype(F32)
    near1 = tp_near(after(tokens[1], near0))

    def enter(*blocks):
        values = joined(*blocks).astype(F32)
        stats, normed = norm_one(values)
        return values, stats, normed, my_half(normed)

    x0, stats0, first0, mine0 = clock(enter, *crossed(near0))
    kv0 = GridGather(mine0)
    q0 = clock(to_queries, first0)
    cross1 = crossed(after(near1, q0))
    kv0.second(clock)
    x1, stats1, first1, mine1 = clock(enter, *cross1)
    kv1 = GridGather(mine1)
    q1 = clock(to_queries, first1)
    kv1.second(clock)
    inputs, stats_one, first, queries = [x0, x1], [stats0, stats1], [first0, first1], [q0, q1]

    mine = kv0.joined(clock)
    every_kv = [clock(both_halves, mine, lax.ppermute(mine, "tp", core_swap))]
    outs = [clock(lambda q, kv: attend(q, kv, info[0], head), q0, every_kv[0])]
    near0 = tp_near(outs[0][1])
    mine = kv1.joined(clock)
    every_kv.append(clock(both_halves, mine, lax.ppermute(mine, "tp", core_swap)))
    outs.append(clock(lambda q, kv: attend(q, kv, info[1], head), q1, every_kv[1]))
    mixed, attended, lse = zip(*outs)
    near1 = tp_near(attended[1])

    mid0, stats0, sec0 = clock(functools.partial(norm_two, 0), *crossed(after(near0, attended[1])))
    act0, slope0 = clock(expand, sec0)
    part0 = clock(lambda act: dot_nn(act, w_shrink).astype(BF16), act0)
    sum0 = TpSum(part0)
    mid1, stats1, sec1 = clock(functools.partial(norm_two, 1), *crossed(after(near1, sec0)))
    sum0.across(clock)
    act1, slope1 = clock(expand, sec1)
    middle, stats_two, second = [mid0, mid1], [stats0, stats1], [sec0, sec1]
    activated, slope = [act0, act1], [slope0, slope1]
    out0, value0, d_final0, g0 = clock(
        lambda *v: finish(0, sum0.total, *v), sum0.pair, sum0.moved
    )
    near_g0 = tp_near(g0)
    part1 = clock(lambda act: dot_nn(act, w_shrink).astype(BF16), act1)
    sum1 = TpSum(part1)
    sum1.across(clock)
    g0_all = clock(joined, *crossed(after(near_g0, part1)))
    d_hidden0 = clock(lambda g: hidden_grad(0, g), g0_all)
    out1, value1, d_final1, g1 = clock(
        lambda *v: finish(1, sum1.total, *v), sum1.pair, sum1.moved
    )
    near_g1 = tp_near(g1)

    def second_partial(hidden):
        return dot_nt(hidden, w_expand).astype(BF16)

    def d_second(back):
        own = clock(back.total, back.pair, back.moved)
        return own, tp_near(own.astype(BF16))

    def norm_two_back(s, *blocks):
        mean, factor = stats_two[s]
        d_all = joined(*blocks).astype(F32)
        scaled = d_all * full_gain_second
        normed = (middle[s] - mean) * factor
        total = jnp.mean(scaled, axis=-1, keepdims=True)
        cross = jnp.mean(scaled * normed, axis=-1, keepdims=True)
        grad = g_shrink_all[s].astype(F32) + factor * (scaled - total - normed * cross)
        grad = grad.astype(BF16)
        return total, cross, grad, dot_nt(grad, w_output).astype(BF16)

    def norm_two_own(s, d_own, total, cross):
        mean, factor = stats_two[s]
        normed = (own_cols(middle[s]) - mean) * factor
        d_mid = d_final[s] + factor * (d_own * own_gain_second - total - normed * cross)
        sums = (jnp.sum(d_own * normed, axis=0), jnp.sum(d_own, axis=0), column_sum(d_mid.astype(BF16)))
        return d_mid, sums

    def attention_back(s, d_attended):
        return attend_back(queries[s], d_attended, mixed[s], lse[s], every_kv[s], info[s], head)

    def swap_halves(d_keyval):
        sent, kept = cols_at(d_keyval, jnp.uint32(1) - core, head), cols_at(d_keyval, core, head)
        return kept, lax.ppermute(sent, "tp", core_swap)

    def add_halves(kept, moved):
        pair = (kept.astype(F32) + moved.astype(F32)).astype(BF16)
        return pair.reshape(-1, yrows, rows // yrows, head)

    partial0 = clock(second_partial, d_hidden0)
    back0 = TpSum(partial0)
    back0.across(clock)
    g1_all = clock(joined, *crossed(after(near_g1, partial0)))
    output = jnp.stack([out0, out1])
    objective = value0 + value1
    d_final, g_shrink, g_shrink_all = [d_final0, d_final1], [g0, g1], [g0_all, g1_all]
    yrows = lax.axis_size("tp") // CORES

    ring_a = Ring(clock, clock(weight_grad, activated, g_shrink_all), 1)
    d_own0, near0 = d_second(back0)
    d_hidden1 = clock(lambda g: hidden_grad(1, g), g1_all)
    d_hidden = [d_hidden0, d_hidden1]
    ring_b = Ring(clock, clock(weight_grad, second, d_hidden), -1)
    ring_a.turn()
    cross0 = crossed(after(near0, ring_b.grad))
    partial1 = clock(second_partial, d_hidden1)
    back1 = TpSum(partial1)
    total0, cross_sum0, g_output0, d_att0 = clock(functools.partial(norm_two_back, 0), *cross0)
    back1.across(clock)
    ring_b.turn()
    ring_a.turn()
    d_query0, d_keyval0 = clock(functools.partial(attention_back, 0), d_att0)
    halves0 = swap_halves(d_keyval0)
    d_own1, near1 = d_second(back1)
    d_mid0, sums0 = clock(functools.partial(norm_two_own, 0), d_own0, total0, cross_sum0)
    ring_b.turn()
    ring_a.turn()
    pair0 = clock(add_halves, *halves0)
    total1, cross_sum1, g_output1, d_att1 = clock(
        functools.partial(norm_two_back, 1), *crossed(after(near1, pair0))
    )
    grad_output = GridSum(clock(weight_grad, attended, (g_output0, g_output1)))
    ring_b.turn()
    ring_a.turn()
    d_query1, d_keyval1 = clock(functools.partial(attention_back, 1), d_att1)
    halves1 = swap_halves(d_keyval1)
    d_mid1, sums1 = clock(functools.partial(norm_two_own, 1), d_own1, total1, cross_sum1)
    d_middle, d_queries = [d_mid0, d_mid1], [d_query0, d_query1]
    ring_b.turn()
    ring_a.turn()
    grad_output.second(clock)
    grad_query = GridSum(clock(weight_grad, first, d_queries))
    pair1 = clock(add_halves, *halves1)
    pair = clock(lambda *v: jnp.concatenate(v, axis=2), pair0, pair1)

    def split(index):
        return lax.dynamic_index_in_dim(pair, index, 1, keepdims=False)

    kept = split(y)
    moved = [
        lax.ppermute(split(shifted(y, k, yrows)), "tp", tp_pairs(lax.axis_size("tp"), k, 0))
        for k in range(1, yrows)
    ]
    ring_b.turn()
    ring_a.turn()
    partials = [
        clock(lambda d: dot_nt(d, w_query).astype(BF16), d_query) for d_query in d_queries
    ]
    sums = [TpSum(p) for p in partials]
    kv_scatter = GridScatter(clock, clock(lambda *parts: added(parts), kept, *moved))
    grad_output.third(clock)
    ring_b.turn()
    ring_a.turn()
    for part_sum in sums:
        part_sum.across(clock)
    kv_scatter.second(clock)
    grad_query.second(clock)
    ring_b.turn()
    ring_a.turn()
    mine = kv_scatter.result(clock).reshape(seqs, -1, head)
    near = tp_near(mine)
    grad_output.fourth(clock)
    ring_b.turn()
    ring_a.turn()
    grad_query.third(clock)

    def join_kv(*blocks):
        blocks = tp_ordered(pairs_of(blocks))
        halves = [jnp.concatenate(blocks[c::CORES], axis=1) for c in range(CORES)]
        return jnp.concatenate(halves, axis=2)

    d_kv_all = clock(join_kv, *crossed(near))
    d_kv = [d_kv_all[s] for s in every]
    grad_kv = GridSum(clock(weight_grad, [own_cols(f) for f in first], d_kv))
    kv_rows = rows_at(w_keyval, tp_index, part)

    def norm_one_back(s, total, pair, moved):
        mean, factor = stats_one[s]
        d_first = total(pair, moved) + dot_nt(d_kv[s], kv_rows)
        normed = (tokens[s].astype(F32) - mean) * factor
        scaled = d_first * own_gain_first
        return d_first, jnp.stack([jnp.sum(scaled, axis=-1), jnp.sum(scaled * normed, axis=-1)])

    d_firsts, row_sums = zip(
        *[
            clock(functools.partial(norm_one_back, s, sums[s].total), sums[s].pair, sums[s].moved)
            for s in every
        ]
    )
    row_sums = tp_sum(jnp.concatenate(row_sums, axis=0))
    ring_b.turn()
    ring_a.turn()
    grad_w_output = grad_output.result(clock)
    grad_kv.second(clock)
    grad_query.fourth(clock)

    def norm_one_end(s, d_first, row_sums):
        mean, factor = stats_one[s]
        total, cross = row_sums[2 * s][:, None] / width, row_sums[2 * s + 1][:, None] / width
        normed = (tokens[s].astype(F32) - mean) * factor
        grad = d_middle[s] + factor * (d_first * own_gain_first - total - normed * cross)
        return grad, (jnp.sum(d_first * normed, axis=0), jnp.sum(d_first, axis=0))

    tokens_grad, sums_first = zip(
        *[clock(functools.partial(norm_one_end, s), d_firsts[s], row_sums) for s in every]
    )
    shares = tp_ordered(tp_cross(tp_near(jnp.broadcast_to(objective, (8, 128)))))
    ring_b.turn()
    ring_a.turn()
    grad_kv.third(clock)
    objective = sum(part_sum[0, 0] for part_sum in shares)
    small = [
        sum(column_sum(d) for d in d_queries),
        sum(column_sum(d[:, head:]) for d in d_kv),
        sums0[2] + sums1[2],
        sum(column_sum(d) for d in d_hidden),
        sum(column_sum(g) for g in g_shrink),
        sums_first[0][0] + sums_first[1][0],
        sums_first[0][1] + sums_first[1][1],
        sums0[0] + sums1[0],
        sums0[1] + sums1[1],
        jnp.broadcast_to(objective, (128,)),
    ]
    small_sum = GridSmallSum(clock(lambda v: jnp.concatenate(v), small))
    grad_w_query = grad_query.result(clock)
    ring_b.turn()
    ring_a.turn()
    grad_kv.fourth(clock)
    small_sum.second(clock)
    ring_b.turn()
    ring_a.turn()
    grad_w_keyval = grad_kv.result(clock, BF16)
    grad_w_keyval = lax.all_gather(grad_w_keyval, "tp", axis=0, tiled=True)
    summed = small_sum.result(clock)
    while not (ring_a.done() and ring_b.done()):
        ring_b.turn()
        ring_a.turn()
    grad_w_keyval = clock(lambda g: g.astype(F32), grad_w_keyval)
    grad_w_shrink, grad_w_expand = ring_a.out, ring_b.out

    pieces, start = [], 0
    for vector in small:
        pieces.append(summed[start : start + vector.shape[0]])
        start += vector.shape[0]
    (
        grad_b_query,
        grad_b_value,
        grad_b_output,
        grad_b_expand,
        grad_b_shrink,
        grad_gain_first,
        grad_bias_first,
        grad_gain_second,
        grad_bias_second,
        grand_total,
    ) = pieces
    loss = grand_total[0] / (jnp.sum(lengths).astype(F32) * width)
    return (
        output,
        jnp.stack(tokens_grad),
        loss,
        grad_w_query,
        grad_b_query,
        grad_w_keyval,
        grad_b_value,
        grad_w_output,
        grad_b_output,
        grad_w_expand,
        grad_b_expand,
        grad_w_shrink,
        grad_b_shrink,
        grad_gain_first,
        grad_bias_first,
        grad_gain_second,
        grad_bias_second,
    )


def solution(mesh):
    placed = (
        P(None, "ctx", "tp"),
        P(),
        P(None, "ctx", "tp"),
        P(None, "ctx", "tp"),
        P(None, "tp"),
        P("tp"),
        P(),
        P(),
        P("tp", None),
        P("tp"),
        P(None, "tp"),
        P("tp"),
        P("tp", None),
        P("tp"),
        P("tp"),
        P("tp"),
        P("tp"),
        P("tp"),
    )
    return jax.shard_map(
        shards,
        mesh=mesh,
        in_specs=placed,
        out_specs=(
            P(None, "ctx", "tp"),
            P(None, "ctx", "tp"),
            P(),
            P(None, "tp"),
            P("tp"),
            P(),
            P(),
            P("tp", None),
            P("tp"),
            P(None, "tp"),
            P("tp"),
            P("tp", None),
            P("tp"),
            P("tp"),
            P("tp"),
            P("tp"),
            P("tp"),
        ),
        check_vma=False,
    )
```

time: 1650 us -> 884 us (0.54)
  waiting for transfers between devices: 1020 us -> 322 us
  matrix products: 310 us -> 98.6 us
  starting transfers between devices: 1.26 us -> 179 us
  blocking collectives: 106 us -> 0 us
  Pallas kernels: 0 us -> 71 us
  other arithmetic: 112 us -> 140 us
  local copies, waits for them, and re-layouts: 66.5 us -> 38.9 us
  loops' own time: 17.8 us -> 0 us
    psum x2 -> x0, waiting for transfers between devices: 596 us -> none  [the longest x1 596 us: shards(): lax.psum(grad_w_query.astype(jnp.bfloat16), 'ctx').astype(jnp.float32)]
    ppermute x0 -> x120, waiting for transfers between devices: none -> 322 us  [the longest x28 172 us: send(): self.arrived = lax.ppermute(block, 'ctx', ring_shift(self.order, self.way))]
    reduce_scatter x5 -> x0, waiting for transfers between devices: 218 us -> none  [the longest x4 131 us: shard_sums(): lax.psum_scatter(partial_value.astype(jnp.bfloat16), 'tp', scatter_dimens...]
    dot_general x71 -> x20, matrix products: 310 us -> 98.6 us  [the longest x10 56.7 us: dot_nn(): lax.dot_general(left, right, (((1,), (0,)), ((), ())), preferred_element_...]
    all_gather x5 -> x2, waiting for transfers between devices: 204 us -> 0.01 us  [the longest x1 0.01 us: shards(): w_output_all = lax.all_gather(w_output, 'tp', axis=0, tiled=True)]
    ppermute x0 -> x120, starting transfers between devices: none -> 179 us  [the longest x30 81.6 us: send_column(): return lax.ppermute(values, 'ctx', pairs)]
    psum x6 -> x0, blocking collectives: 106 us -> none  [the longest x1 40.8 us: shards(): grand_total = lax.psum(objective, ('ctx', 'tp'))]
    pallas_call x0 -> x11, Pallas kernels: none -> 71 us  [the longest x5 31.6 us: weight_grad(): pl.pallas_call(functools.partial(grad_kernel, count), grid=(m // bm,), in...]
  transfers between devices with their start and end apart: 12 -> 122, of which waited for: 10 -> 40; matrix products, arithmetic and copies ran while one was open for 5% -> 28% of each run, Pallas kernels for 0% -> 8%
where the time goes in v1:
time: 884 us; the launch traced here: 879 us
  waiting for transfers between devices  322 us (36%)
  starting transfers between devices  179 us (20%)
  other arithmetic  140 us (16%)
  matrix products  98.6 us (11%)
  Pallas kernels  71 us (8%)
  local copies, waits for them, and re-layouts  38.9 us (4%)
  between operations  29.3 us (3%)
    ppermute x28, waiting for transfers between devices, send(): self.arrived = lax.ppermute(block, 'ctx', ring_shift(self.order, self.way))  172 us
    ppermute x30, starting transfers between devices, send_column(): return lax.ppermute(values, 'ctx', pairs)  81.6 us
    dot_general x10, matrix products, dot_nn(): lax.dot_general(left, right, (((1,), (0,)), ((), ())), preferred_element_...  56.7 us
    ppermute x28, starting transfers between devices, send(): self.arrived = lax.ppermute(block, 'ctx', ring_shift(self.order, self.way))  49.2 us
    ppermute x11, waiting for transfers between devices, tp_near(): lax.ppermute(values, 'tp', tp_pairs(size, k, 0))  44.7 us
    ppermute x10, waiting for transfers between devices, send_row(): return lax.ppermute(values, 'ctx', pairs)  42.4 us
    dot_general x10, matrix products, dot_nt(): lax.dot_general(left, right, (((1,), (1,)), ((), ())), preferred_element_...  41.9 us
    ppermute x30, waiting for transfers between devices, send_column(): return lax.ppermute(values, 'ctx', pairs)  36.9 us
  transfers between devices with their start and end apart: 122, of which 40 were waited for; matrix products, arithmetic and copies ran while one was open for 28% of the time, Pallas kernels for 8%

profile of v1, /device:TPU:0, one launch (start us, length us, event | category | flops | bytes accessed | tf_op | source)
XLA Modules:
  0.0 879.0 jit_solution(3152192349922573540)
XLA Ops:
  8.7 3.0 collective-permute-start.1
  15.9 8.0 collective-permute-done.3
  33.2 16.6 %collective-permute-done.10 = bf16[512,512]{1,0:T(8,128)(2,1)S(1)} collective-permute-done((bf16[512,512]{1,0:T(8,128)(2,1)S(1)}, bf16[512,512]{1,0:T(8,128)(2,1)S(1)}, u32[]{:S(2)}, u32[]{:S(2)}) %collective-permute-start.10) | collective-permute-done | bytes 524320 | tf_op jit(solution)/shard_map/ppermute | solution.py:299
  52.2 3.7 collective-permute-done.6
  55.9 4.2 collective-permute-start.9
  69.7 11.9 %collective-permute-done.8 = bf16[1024,128]{1,0:T(8,128)(2,1)S(1)} collective-permute-done((bf16[1024,128]{1,0:T(8,128)(2,1)S(1)}, bf16[1024,128]{1,0:T(8,128)(2,1)S(1)}, u32[]{:S(2)}, u32[]{:S(2)}) %collective-permute-start.8) | collective-permute-done | bytes 262176 | tf_op jit(solution)/shard_map/ppermute | solution.py:463
  86.5 3.0 collective-permute-start.17
  93.6 5.1 shard_map.341
  98.8 14.5 %collective-permute-done.17 = bf16[1024,128]{1,0:T(8,128)(2,1)S(1)} collective-permute-done((bf16[1024,128]{1,0:T(8,128)(2,1)S(1)}, bf16[1024,128]{1,0:T(8,128)(2,1)S(1)}, u32[]{:S(2)}, u32[]{:S(2)}) %collective-permute-start.17) | collective-permute-done | bytes 262176 | tf_op jit(solution)/shard_map/ppermute | solution.py:463
  116.6 5.5 shard_map.342
  124.1 3.9 collective-permute-done.15
  131.7 3.0 broadcast_select_fusion.67
  134.7 9.2 %fusion.61 = (f32[512]{0:T(512)S(1)}, f32[512,2048]{1,0:T(8,128)S(1)}) fusion(f32[2048]{0:T(1024)S(1)} %bitcast.172, bf16[2048,2048]{1,0:T(8,128)(2,1)} %all-gather.3.cloned.1.call-done, bf16[512,512]{1,0:T(8,128)(2,1)} %get-tuple-element.679, bf16[512,512]{1,0:T(8,128)(2,1)} %get-tuple-element.680, bf16[512,512]{1,0:T(8,128)(2,1)} %get-tuple-element.681, ...), kind=kOutput, calls=%fused_computation.440 | convolution fusion | flops 4314889728 | bytes 16787456 | tf_op jit(solution)/shard_map/dot_general | solution.py:22
  145.9 12.9 %add_convert_fusion.4 = (bf16[512,2048]{1,0:T(8,128)(2,1)}, bf16[512,2048]{1,0:T(8,128)(2,1)S(1)}) fusion(f32[2048]{0:T(1024)S(1)} %convert_element_type.666, bf16[512,2048]{1,0:T(8,128)(2,1)S(1)} %add_convert_fusion.5.refs_0_, bf16[2048,2048]{1,0:T(8,128)(2,1)} %param.32), kind=kOutput, calls=%fused_computation.18 | convolution fusion | flops 4315938816 | bytes 14688256 | tf_op jit(solution)/shard_map/dot_general | solution.py:22
  158.9 4.9 convolution_convert_fusion.5
  166.0 8.3 fusion.62
  177.3 11.6 %add_convert_fusion.2 = (bf16[512,2048]{1,0:T(8,128)(2,1)}, bf16[512,2048]{1,0:T(8,128)(2,1)S(1)}) fusion(f32[2048]{0:T(1024)S(1)} %convert_element_type.666, bf16[512,2048]{1,0:T(8,128)(2,1)S(1)} %add_convert_fusion.3.refs_1_, bf16[2048,2048]{1,0:T(8,128)(2,1)} %param.32), kind=kOutput, calls=%fused_computation.12 | convolution fusion | flops 4315938816 | bytes 14688256 | tf_op jit(solution)/shard_map/dot_general | solution.py:22
  193.7 5.0 convolution_convert_fusion.4
  200.3 13.2 %collective-permute-done.29 = bf16[512,512]{1,0:T(8,128)(2,1)S(1)} collective-permute-done((bf16[512,512]{1,0:T(8,128)(2,1)S(1)}, bf16[512,512]{1,0:T(8,128)(2,1)S(1)}, u32[]{:S(2)}, u32[]{:S(2)}) %collective-permute-start.29) | collective-permute-done | bytes 524320 | tf_op jit(solution)/shard_map/ppermute | solution.py:299
  218.9 9.0 %convert_reduce_fusion.1 = (f32[2048]{0:T(1024)S(1)}, bf16[512,2048]{1,0:T(8,128)(2,1)S(1)}) fusion(bf16[512,2048]{1,0:T(8,128)(2,1)S(1)} %copy-done.113, bf16[512,2048]{1,0:T(8,128)(2,1)S(1)} %pad_maximum_fusion.4.refs_2_, bf16[2048,2048]{1,0:T(8,128)(2,1)} %param.34), kind=kOutput, calls=%fused_computation.1 | convolution fusion | flops 4300208128 | bytes 14688256 | tf_op jit(solution)/shard_map/dot_general | solution.py:26
  233.6 8.1 convolution_convert_fusion.3
  265.9 11.8 %shard_map.343 = bf16[2048,2048]{1,0:T(8,128)(2,1)} custom-call(bf16[512,2048]{1,0:T(8,128)(2,1)S(1)} %copy-done.24, bf16[512,2048]{1,0:T(8,128)(2,1)S(1)} %copy-done.26, bf16[512,2048]{1,0:T(8,128)(2,1)S(1)} %copy-done.8, bf16[512,2048]{1,0:T(8,128)(2,1)S(1)} %pad_maximum_fusion.5.refs_3_), custom_call_target="tpu_custom_call" | custom-call | flops 8589934592 | bytes 16777216 | tf_op jit(solution)/shard_map/pallas_call | solution.py:218
  279.4 9.1 %convert_reduce_fusion = (f32[2048]{0:T(1024)S(1)}, bf16[512,2048]{1,0:T(8,128)(2,1)S(1)}) fusion(bf16[512,2048]{1,0:T(8,128)(2,1)} %get-tuple-element.614, bf16[512,2048]{1,0:T(8,128)(2,1)S(1)} %pad_maximum_fusion.5.refs_3_, bf16[2048,2048]{1,0:T(8,128)(2,1)} %param.34), kind=kOutput, calls=%fused_computation | convolution fusion | flops 4300208128 | bytes 14688256 | tf_op jit(solution)/shard_map/dot_general | solution.py:26
  289.4 11.9 %shard_map.344 = bf16[2048,2048]{1,0:T(8,128)(2,1)} custom-call(bf16[512,2048]{1,0:T(8,128)(2,1)S(1)} %copy-done.10, bf16[512,2048]{1,0:T(8,128)(2,1)S(1)} %copy-done.12, bf16[512,2048]{1,0:T(8,128)(2,1)S(1)} %copy-done.28, bf16[512,2048]{1,0:T(8,128)(2,1)S(1)} %get-tuple-element.395.refs_3_), custom_call_target="tpu_custom_call" | custom-call | flops 8589934592 | bytes 16777216 | tf_op jit(solution)/shard_map/pallas_call | solution.py:218
  309.4 8.1 convolution_convert_fusion.2
  326.4 3.4 collective-permute-done.44
  335.1 3.4 collective-permute-start.45
  339.5 11.8 %shard_map.345 = (bf16[512,512]{1,0:T(8,128)(2,1)}, bf16[4096,256]{1,0:T(8,128)(2,1)}) custom-call(s32[10]{0:T(128)} %copy-done.20, bf16[512,512]{1,0:T(8,128)(2,1)} %copy-done.22, bf16[512,512]{1,0:T(8,128)(2,1)} %convolution_convert_fusion.7.do_ref, f32[512,512]{1,0:T(8,128)} %copy-done.31, f32[512,512]{1,0:T(8,128)} %copy-done.32, bf16[4096,256]{1,0:T(8,128)(2,1)} %copy-done.6), custom_call_target="tpu_custom_call" | custom-call | flops 12884901888 | bytes 8388608 | tf_op jit(solution)/shard_map/pallas_call | solution.py:182
  358.4 4.1 collective-permute-done.46
  376.3 8.0 collective-permute-start.47
  394.8 20.3 %collective-permute-done.48 = bf16[256,2048]{1,0:T(8,128)(2,1)S(1)} collective-permute-done((bf16[256,2048]{1,0:T(8,128)(2,1)S(1)}, bf16[256,2048]{1,0:T(8,128)(2,1)S(1)}, u32[]{:S(2)}, u32[]{:S(2)}) %collective-permute-start.48) | collective-permute-done | bytes 1048608 | tf_op jit(solution)/shard_map/ppermute | solution.py:417
  420.3 7.4 collective-permute-start.53
  427.7 12.1 %shard_map.347 = (bf16[512,512]{1,0:T(8,128)(2,1)}, bf16[4096,256]{1,0:T(8,128)(2,1)}) custom-call(s32[10]{0:T(128)} %copy-done.19, bf16[512,512]{1,0:T(8,128)(2,1)} %fusion.17.q_ref, bf16[512,512]{1,0:T(8,128)(2,1)} %convolution_convert_fusion.6.do_ref, f32[512,512]{1,0:T(8,128)} %copy-done.29, f32[512,512]{1,0:T(8,128)} %copy-done.30, ...), custom_call_target="tpu_custom_call" | custom-call | flops 12884901888 | bytes 8388608 | tf_op jit(solution)/shard_map/pallas_call | solution.py:182
  439.8 3.2 fusion.53
  443.4 8.8 %collective-permute-done.54 = bf16[256,2048]{1,0:T(8,128)(2,1)} collective-permute-done((bf16[256,2048]{1,0:T(8,128)(2,1)}, bf16[256,2048]{1,0:T(8,128)(2,1)}, u32[]{:S(2)}, u32[]{:S(2)}) %collective-permute-start.54) | collective-permute-done | bytes 1048608 | tf_op jit(solution)/shard_map/ppermute | solution.py:417
  460.3 4.4 shard_map.348
  465.1 16.3 %collective-permute-start.64 = (bf16[64,2048]{1,0:T(8,128)(2,1)S(1)}, bf16[64,2048]{1,0:T(8,128)(2,1)S(1)}, u32[]{:S(2)}, u32[]{:S(2)}) collective-permute-start(bf16[64,2048]{1,0:T(8,128)(2,1)S(1)} %get-tuple-element.698), channel_id=1, source_target_pairs={{0,24},{4,28},{8,0},{12,4},{16,8},{20,12},{24,16},{28,20},{1,25},{... | collective-permute-start | bytes 786440 | tf_op jit(solution)/shard_map/ppermute | solution.py:463
  491.3 15.9 %collective-permute-done.65 = bf16[8,512,128]{2,1,0:T(8,128)(2,1)S(1)} collective-permute-done((bf16[8,512,128]{2,1,0:T(8,128)(2,1)S(1)}, bf16[8,512,128]{2,1,0:T(8,128)(2,1)S(1)}, u32[]{:S(2)}, u32[]{:S(2)}) %collective-permute-start.65) | collective-permute-done | bytes 1048608 | tf_op jit(solution)/shard_map/ppermute | solution.py:830
  511.3 19.1 %collective-permute-start.85 = (bf16[64,2048]{1,0:T(8,128)(2,1)S(1)}, bf16[64,2048]{1,0:T(8,128)(2,1)}, u32[]{:S(2)}, u32[]{:S(2)}) collective-permute-start(bf16[64,2048]{1,0:T(8,128)(2,1)S(1)} %add_convert_fusion.35), channel_id=1, source_target_pairs={{0,24},{4,28},{8,0},{12,4},{16,8},{20,12},{24,16},{28,20},{1,25},{... | collective-permute-start | bytes 786440 | tf_op jit(solution)/shard_map/ppermute | solution.py:463
  535.3 5.3 collective-permute-done.61
  543.3 11.1 %collective-permute-start.84 = (bf16[64,2048]{1,0:T(8,128)(2,1)S(1)}, bf16[64,2048]{1,0:T(8,128)(2,1)}, u32[]{:S(2)}, u32[]{:S(2)}) collective-permute-start(bf16[64,2048]{1,0:T(8,128)(2,1)S(1)} %add_convert_fusion.35), channel_id=1, source_target_pairs={{0,16},{4,20},{8,24},{12,28},{16,0},{20,4},{24,8},{28,12},{1,17},{... | collective-permute-start | bytes 786440 | tf_op jit(solution)/shard_map/ppermute | solution.py:463
  568.3 6.1 collective-permute-done.67
  582.0 18.0 %collective-permute-done.73 = bf16[256,2048]{1,0:T(8,128)(2,1)S(1)} collective-permute-done((bf16[256,2048]{1,0:T(8,128)(2,1)S(1)}, bf16[256,2048]{1,0:T(8,128)(2,1)S(1)}, u32[]{:S(2)}, u32[]{:S(2)}) %collective-permute-start.73) | collective-permute-done | bytes 1048608 | tf_op jit(solution)/shard_map/ppermute | solution.py:417
  609.1 2.8 convert_dynamic-update-slice_fusion.13
  611.9 3.5 collective-permute-done.70
  624.6 18.2 %collective-permute-done.82 = bf16[256,2048]{1,0:T(8,128)(2,1)S(1)} collective-permute-done((bf16[256,2048]{1,0:T(8,128)(2,1)}, bf16[256,2048]{1,0:T(8,128)(2,1)S(1)}, u32[]{:S(2)}, u32[]{:S(2)}) %collective-permute-start.82) | collective-permute-done | bytes 1048608 | tf_op jit(solution)/shard_map/ppermute | solution.py:417
  645.7 9.9 %collective-permute-done.81 = bf16[256,2048]{1,0:T(8,128)(2,1)S(1)} collective-permute-done((bf16[256,2048]{1,0:T(8,128)(2,1)}, bf16[256,2048]{1,0:T(8,128)(2,1)S(1)}, u32[]{:S(2)}, u32[]{:S(2)}) %collective-permute-start.81) | collective-permute-done | bytes 1048608 | tf_op jit(solution)/shard_map/ppermute | solution.py:417
  659.2 5.2 collective-permute-done.79
  666.9 4.9 collective-permute-start.91
  675.2 3.4 collective-permute-start.94
  685.1 25.2 %collective-permute-done.95 = bf16[256,2048]{1,0:T(8,128)(2,1)S(1)} collective-permute-done((bf16[256,2048]{1,0:T(8,128)(2,1)S(1)}, bf16[256,2048]{1,0:T(8,128)(2,1)S(1)}, u32[]{:S(2)}, u32[]{:S(2)}) %collective-permute-start.95) | collective-permute-done | bytes 1048608 | tf_op jit(solution)/shard_map/ppermute | solution.py:417
  720.9 5.8 collective-permute-start.110
  729.5 13.3 %collective-permute-done.103 = bf16[256,2048]{1,0:T(8,128)(2,1)S(1)} collective-permute-done((bf16[256,2048]{1,0:T(8,128)(2,1)S(1)}, bf16[256,2048]{1,0:T(8,128)(2,1)S(1)}, u32[]{:S(2)}, u32[]{:S(2)}) %collective-permute-start.103) | collective-permute-done | bytes 1048608 | tf_op jit(solution)/shard_map/ppermute | solution.py:417
  754.2 11.6 %collective-permute-done.110 = bf16[1024,512]{1,0:T(8,128)(2,1)S(1)} collective-permute-done((bf16[1024,512]{1,0:T(8,128)(2,1)S(1)}, bf16[1024,512]{1,0:T(8,128)(2,1)S(1)}, u32[]{:S(2)}, u32[]{:S(2)}) %collective-permute-start.110) | collective-permute-done | bytes 1048608 | tf_op jit(solution)/shard_map/ppermute | solution.py:458
  768.6 16.0 %collective-permute-done.109 = bf16[256,2048]{1,0:T(8,128)(2,1)} collective-permute-done((bf16[256,2048]{1,0:T(8,128)(2,1)S(1)}, bf16[256,2048]{1,0:T(8,128)(2,1)}, u32[]{:S(2)}, u32[]{:S(2)}) %collective-permute-start.109) | collective-permute-done | bytes 1048608 | tf_op jit(solution)/shard_map/ppermute | solution.py:417
  787.2 2.8 convert_dynamic-update-slice_fusion.6
  790.0 2.8 convert_dynamic-update-slice_fusion.5
  794.9 19.6 %collective-permute-done.104 = f32[5888]{0:T(1024)S(1)} collective-permute-done((f32[5888]{0:T(1024)S(1)}, f32[5888]{0:T(1024)S(1)}, u32[]{:S(2)}, u32[]{:S(2)}) %collective-permute-start.104) | collective-permute-done | bytes 23584 | tf_op jit(solution)/shard_map/ppermute | solution.py:458
  819.1 2.8 convert_dynamic-update-slice_fusion.4
  823.5 2.8 collective-permute-start.119
  830.7 14.0 %collective-permute-done.117 = bf16[256,2048]{1,0:T(8,128)(2,1)} collective-permute-done((bf16[256,2048]{1,0:T(8,128)(2,1)}, bf16[256,2048]{1,0:T(8,128)(2,1)}, u32[]{:S(2)}, u32[]{:S(2)}) %collective-permute-start.117) | collective-permute-done | bytes 1048608 | tf_op jit(solution)/shard_map/ppermute | solution.py:417
  845.7 2.8 convert_dynamic-update-slice_fusion.2
  848.5 2.8 convert_dynamic-update-slice_fusion.1
  851.3 15.2 %collective-permute-done.118 = bf16[256,2048]{1,0:T(8,128)(2,1)S(1)} collective-permute-done((bf16[256,2048]{1,0:T(8,128)(2,1)}, bf16[256,2048]{1,0:T(8,128)(2,1)S(1)}, u32[]{:S(2)}, u32[]{:S(2)}) %collective-permute-start.118) | collective-permute-done | bytes 1048608 | tf_op jit(solution)/shard_map/ppermute | solution.py:417
  (703 shorter events, 279.9 us)
Async XLA Ops:
  7.2 127.5 %all-gather.3.cloned.1.call-start = ((), (), s32[]{:S(2)}) async-start(), calls=%async_computation | async-start | bytes 10485760 | tf_op jit(solution)/shard_map/all_gather | solution.py:686
  15.8 852.3 %all-gather.5.cloned.1.call-start = ((), (), s32[]{:S(2)}) async-start(), calls=%async_computation.1 | async-start | bytes 1310720 | tf_op jit(solution)/shard_map/all_gather | solution.py:922
  25.0 24.7 %collective-permute-start.10 = (bf16[512,512]{1,0:T(8,128)(2,1)S(1)}, bf16[512,512]{1,0:T(8,128)(2,1)S(1)}, u32[]{:S(2)}, u32[]{:S(2)}) collective-permute-start(bf16[512,512]{1,0:T(8,128)(2,1)S(1)} %get-tuple-element.314), channel_id=1, source_target_pairs={{0,2},{1,3},{2,0},{3,1},{4,6},{5,7},{6,4},{7,5},{8,10},{9,11},{10,... | collective-permute-start | bytes 1572872 | tf_op jit(solution)/shard_map/ppermute | solution.py:299
  60.1 21.5 %collective-permute-start.8 = (bf16[1024,128]{1,0:T(8,128)(2,1)S(1)}, bf16[1024,128]{1,0:T(8,128)(2,1)S(1)}, u32[]{:S(2)}, u32[]{:S(2)}) collective-permute-start(bf16[1024,128]{1,0:T(8,128)(2,1)S(1)} %constant_dynamic-update-slice_fusion), channel_id=1, source_target_pairs={{0,16},{4,20},{8,24},{12,28},{16,0},{20,4},{24,8},{28,12},{1,17},{... | collective-permute-start | bytes 786440 | tf_op jit(solution)/shard_map/ppermute | solution.py:463
  60.1 21.5 %collective-permute-start.7 = (bf16[1024,128]{1,0:T(8,128)(2,1)S(1)}, bf16[1024,128]{1,0:T(8,128)(2,1)S(1)}, u32[]{:S(2)}, u32[]{:S(2)}) collective-permute-start(bf16[1024,128]{1,0:T(8,128)(2,1)S(1)} %constant_dynamic-update-slice_fusion), channel_id=1, source_target_pairs={{0,8},{4,12},{8,16},{12,20},{16,24},{20,28},{24,0},{28,4},{1,9},{5... | collective-permute-start | bytes 786440 | tf_op jit(solution)/shard_map/ppermute | solution.py:463
  86.5 26.8 %collective-permute-start.17 = (bf16[1024,128]{1,0:T(8,128)(2,1)S(1)}, bf16[1024,128]{1,0:T(8,128)(2,1)S(1)}, u32[]{:S(2)}, u32[]{:S(2)}) collective-permute-start(bf16[1024,128]{1,0:T(8,128)(2,1)S(1)} %constant_dynamic-update-slice_fusion.2), channel_id=1, source_target_pairs={{0,16},{4,20},{8,24},{12,28},{16,0},{20,4},{24,8},{28,12},{1,17},{... | collective-permute-start | bytes 786440 | tf_op jit(solution)/shard_map/ppermute | solution.py:463
  89.5 23.8 %collective-permute-start.16 = (bf16[1024,128]{1,0:T(8,128)(2,1)S(1)}, bf16[1024,128]{1,0:T(8,128)(2,1)S(1)}, u32[]{:S(2)}, u32[]{:S(2)}) collective-permute-start(bf16[1024,128]{1,0:T(8,128)(2,1)S(1)} %constant_dynamic-update-slice_fusion.2), channel_id=1, source_target_pairs={{0,8},{4,12},{8,16},{12,20},{16,24},{20,28},{24,0},{28,4},{1,9},{5... | collective-permute-start | bytes 786440 | tf_op jit(solution)/shard_map/ppermute | solution.py:463
  145.3 19.1 %collective-permute-start.24 = (bf16[512,512]{1,0:T(8,128)(2,1)S(1)}, bf16[512,512]{1,0:T(8,128)(2,1)S(1)}, u32[]{:S(2)}, u32[]{:S(2)}) collective-permute-start(bf16[512,512]{1,0:T(8,128)(2,1)S(1)} %get-tuple-element.423.refs_1_), channel_id=1, source_target_pairs={{0,1},{1,0},{2,3},{3,2},{4,5},{5,4},{6,7},{7,6},{8,9},{9,8},{10,11... | collective-permute-start | bytes 1572872 | tf_op jit(solution)/shard_map/ppermute | solution.py:304
  145.4 19.1 %collective-permute-start.25 = (bf16[512,512]{1,0:T(8,128)(2,1)}, bf16[512,512]{1,0:T(8,128)(2,1)S(1)}, u32[]{:S(2)}, u32[]{:S(2)}) collective-permute-start(bf16[512,512]{1,0:T(8,128)(2,1)} %collective-permute-done.23), channel_id=1, source_target_pairs={{0,1},{1,0},{2,3},{3,2},{4,5},{5,4},{6,7},{7,6},{8,9},{9,8},{10,11... | collective-permute-start | bytes 1572872 | tf_op jit(solution)/shard_map/ppermute | solution.py:304
  255.8 113.7 %collective-permute-start.96 = (f32[8,128]{1,0:T(8,128)S(1)}, f32[8,128]{1,0:T(8,128)S(1)}, u32[]{:S(2)}, u32[]{:S(2)}) collective-permute-start(f32[8,128]{1,0:T(8,128)S(1)} %broadcast_in_dim.30), channel_id=1, source_target_pairs={{0,2},{1,3},{2,0},{3,1},{4,6},{5,7},{6,4},{7,5},{8,10},{9,11},{10,... | collective-permute-start | bytes 12296 | tf_op jit(solution)/shard_map/ppermute | solution.py:299
  279.1 25.6 %collective-permute-start.40 = (bf16[256,2048]{1,0:T(8,128)(2,1)S(1)}, bf16[256,2048]{1,0:T(8,128)(2,1)S(1)}, u32[]{:S(2)}, u32[]{:S(2)}) collective-permute-start(bf16[256,2048]{1,0:T(8,128)(2,1)S(1)} %constant_dynamic-slice_fusion.40), channel_id=1, source_target_pairs={{0,8},{8,16},{16,24},{24,28},{28,20},{20,12},{12,4},{4,0},{1,9},{9... | collective-permute-start | bytes 3145736 | tf_op jit(solution)/shard_map/ppermute | solution.py:417
  288.5 20.4 %collective-permute-start.37 = (bf16[512,512]{1,0:T(8,128)(2,1)S(1)}, bf16[512,512]{1,0:T(8,128)(2,1)S(1)}, u32[]{:S(2)}, u32[]{:S(2)}) collective-permute-start(bf16[512,512]{1,0:T(8,128)(2,1)S(1)} %get-tuple-element.398), channel_id=1, source_target_pairs={{0,2},{1,3},{2,0},{3,1},{4,6},{5,7},{6,4},{7,5},{8,10},{9,11},{10,... | collective-permute-start | bytes 1572872 | tf_op jit(solution)/shard_map/ppermute | solution.py:299
  302.6 27.3 %collective-permute-start.44 = (bf16[256,2048]{1,0:T(8,128)(2,1)S(1)}, bf16[256,2048]{1,0:T(8,128)(2,1)S(1)}, u32[]{:S(2)}, u32[]{:S(2)}) collective-permute-start(bf16[256,2048]{1,0:T(8,128)(2,1)S(1)} %constant_dynamic-slice_fusion.34), channel_id=1, source_target_pairs={{0,4},{8,0},{16,8},{24,16},{28,24},{20,28},{12,20},{4,12},{1,5},{9... | collective-permute-start | bytes 3145736 | tf_op jit(solution)/shard_map/ppermute | solution.py:417
  306.3 26.3 %collective-permute-start.43 = (bf16[256,2048]{1,0:T(8,128)(2,1)S(1)}, bf16[256,2048]{1,0:T(8,128)(2,1)S(1)}, u32[]{:S(2)}, u32[]{:S(2)}) collective-permute-start(bf16[256,2048]{1,0:T(8,128)(2,1)S(1)} %add_convert_fusion.29), channel_id=1, source_target_pairs={{0,8},{8,16},{16,24},{24,28},{28,20},{20,12},{12,4},{4,0},{1,9},{9... | collective-permute-start | bytes 3145736 | tf_op jit(solution)/shard_map/ppermute | solution.py:417
  335.1 29.4 %collective-permute-start.45 = (bf16[256,2048]{1,0:T(8,128)(2,1)}, bf16[256,2048]{1,0:T(8,128)(2,1)}, u32[]{:S(2)}, u32[]{:S(2)}) collective-permute-start(bf16[256,2048]{1,0:T(8,128)(2,1)} %add_convert_fusion.26), channel_id=1, source_target_pairs={{0,8},{8,16},{16,24},{24,28},{28,20},{20,12},{12,4},{4,0},{1,9},{9... | collective-permute-start | bytes 3145736 | tf_op jit(solution)/shard_map/ppermute | solution.py:417
  338.6 23.8 %collective-permute-start.46 = (bf16[256,2048]{1,0:T(8,128)(2,1)}, bf16[256,2048]{1,0:T(8,128)(2,1)}, u32[]{:S(2)}, u32[]{:S(2)}) collective-permute-start(bf16[256,2048]{1,0:T(8,128)(2,1)} %add_convert_fusion.27), channel_id=1, source_target_pairs={{0,4},{8,0},{16,8},{24,16},{28,24},{20,28},{12,20},{4,12},{1,5},{9... | collective-permute-start | bytes 3145736 | tf_op jit(solution)/shard_map/ppermute | solution.py:417
  376.3 41.4 %collective-permute-start.47 = (bf16[256,2048]{1,0:T(8,128)(2,1)S(1)}, bf16[256,2048]{1,0:T(8,128)(2,1)S(1)}, u32[]{:S(2)}, u32[]{:S(2)}) collective-permute-start(bf16[256,2048]{1,0:T(8,128)(2,1)S(1)} %add_convert_fusion.24), channel_id=1, source_target_pairs={{0,8},{8,16},{16,24},{24,28},{28,20},{20,12},{12,4},{4,0},{1,9},{9... | collective-permute-start | bytes 3145736 | tf_op jit(solution)/shard_map/ppermute | solution.py:417
  384.2 30.9 %collective-permute-start.48 = (bf16[256,2048]{1,0:T(8,128)(2,1)S(1)}, bf16[256,2048]{1,0:T(8,128)(2,1)S(1)}, u32[]{:S(2)}, u32[]{:S(2)}) collective-permute-start(bf16[256,2048]{1,0:T(8,128)(2,1)S(1)} %add_convert_fusion.25), channel_id=1, source_target_pairs={{0,4},{8,0},{16,8},{24,16},{28,24},{20,28},{12,20},{4,12},{1,5},{9... | collective-permute-start | bytes 3145736 | tf_op jit(solution)/shard_map/ppermute | solution.py:417
  394.4 64.3 %collective-permute-start.58 = (bf16[256,2048]{1,0:T(8,128)(2,1)}, bf16[256,2048]{1,0:T(8,128)(2,1)}, u32[]{:S(2)}, u32[]{:S(2)}) collective-permute-start(bf16[256,2048]{1,0:T(8,128)(2,1)} %get-tuple-element.636), channel_id=1, source_target_pairs={{0,4},{4,0},{8,12},{12,8},{16,20},{20,16},{24,28},{28,24},{1,5},{5... | collective-permute-start | bytes 3145736 | tf_op jit(solution)/shard_map/ppermute | solution.py:458
  420.3 36.3 %collective-permute-start.53 = (bf16[256,2048]{1,0:T(8,128)(2,1)}, bf16[256,2048]{1,0:T(8,128)(2,1)}, u32[]{:S(2)}, u32[]{:S(2)}) collective-permute-start(bf16[256,2048]{1,0:T(8,128)(2,1)} %add_convert_fusion.21), channel_id=1, source_target_pairs={{0,8},{8,16},{16,24},{24,28},{28,20},{20,12},{12,4},{4,0},{1,9},{9... | collective-permute-start | bytes 3145736 | tf_op jit(solution)/shard_map/ppermute | solution.py:417
  427.7 24.5 %collective-permute-start.54 = (bf16[256,2048]{1,0:T(8,128)(2,1)}, bf16[256,2048]{1,0:T(8,128)(2,1)}, u32[]{:S(2)}, u32[]{:S(2)}) collective-permute-start(bf16[256,2048]{1,0:T(8,128)(2,1)} %add_convert_fusion.22), channel_id=1, source_target_pairs={{0,4},{8,0},{16,8},{24,16},{28,24},{20,28},{12,20},{4,12},{1,5},{9... | collective-permute-start | bytes 3145736 | tf_op jit(solution)/shard_map/ppermute | solution.py:417
  443.3 21.4 %collective-permute-start.57 = (bf16[4096,128]{1,0:T(8,128)(2,1)S(1)}, bf16[4096,128]{1,0:T(8,128)(2,1)S(1)}, u32[]{:S(2)}, u32[]{:S(2)}) collective-permute-start(bf16[4096,128]{1,0:T(8,128)(2,1)S(1)} %get-tuple-element.638), channel_id=1, source_target_pairs={{0,1},{1,0},{2,3},{3,2},{4,5},{5,4},{6,7},{7,6},{8,9},{9,8},{10,11... | collective-permute-start | bytes 3145736 | tf_op jit(solution)/shard_map/ppermute | solution.py:773
  454.3 29.9 %collective-permute-start.56 = (bf16[256,2048]{1,0:T(8,128)(2,1)S(1)}, bf16[256,2048]{1,0:T(8,128)(2,1)S(1)}, u32[]{:S(2)}, u32[]{:S(2)}) collective-permute-start(bf16[256,2048]{1,0:T(8,128)(2,1)S(1)} %add_convert_fusion.20), channel_id=1, source_target_pairs={{0,4},{8,0},{16,8},{24,16},{28,24},{20,28},{12,20},{4,12},{1,5},{9... | collective-permute-start | bytes 3145736 | tf_op jit(solution)/shard_map/ppermute | solution.py:417
  458.6 28.4 %collective-permute-start.55 = (bf16[256,2048]{1,0:T(8,128)(2,1)S(1)}, bf16[256,2048]{1,0:T(8,128)(2,1)S(1)}, u32[]{:S(2)}, u32[]{:S(2)}) collective-permute-start(bf16[256,2048]{1,0:T(8,128)(2,1)S(1)} %add_convert_fusion.19), channel_id=1, source_target_pairs={{0,8},{8,16},{16,24},{24,28},{28,20},{20,12},{12,4},{4,0},{1,9},{9... | collective-permute-start | bytes 3145736 | tf_op jit(solution)/shard_map/ppermute | solution.py:417
  465.1 45.9 %collective-permute-start.64 = (bf16[64,2048]{1,0:T(8,128)(2,1)S(1)}, bf16[64,2048]{1,0:T(8,128)(2,1)S(1)}, u32[]{:S(2)}, u32[]{:S(2)}) collective-permute-start(bf16[64,2048]{1,0:T(8,128)(2,1)S(1)} %get-tuple-element.698), channel_id=1, source_target_pairs={{0,24},{4,28},{8,0},{12,4},{16,8},{20,12},{24,16},{28,20},{1,25},{... | collective-permute-start | bytes 786440 | tf_op jit(solution)/shard_map/ppermute | solution.py:463
  481.5 29.7 %collective-permute-start.63 = (bf16[64,2048]{1,0:T(8,128)(2,1)S(1)}, bf16[64,2048]{1,0:T(8,128)(2,1)S(1)}, u32[]{:S(2)}, u32[]{:S(2)}) collective-permute-start(bf16[64,2048]{1,0:T(8,128)(2,1)S(1)} %get-tuple-element.699), channel_id=1, source_target_pairs={{0,16},{4,20},{8,24},{12,28},{16,0},{20,4},{24,8},{28,12},{1,17},{... | collective-permute-start | bytes 786440 | tf_op jit(solution)/shard_map/ppermute | solution.py:463
  481.5 29.7 %collective-permute-start.62 = (bf16[64,2048]{1,0:T(8,128)(2,1)S(1)}, bf16[64,2048]{1,0:T(8,128)(2,1)S(1)}, u32[]{:S(2)}, u32[]{:S(2)}) collective-permute-start(bf16[64,2048]{1,0:T(8,128)(2,1)S(1)} %get-tuple-element.700), channel_id=1, source_target_pairs={{0,8},{4,12},{8,16},{12,20},{16,24},{20,28},{24,0},{28,4},{1,9},{5... | collective-permute-start | bytes 786440 | tf_op jit(solution)/shard_map/ppermute | solution.py:463
  484.2 22.9 %collective-permute-start.65 = (bf16[8,512,128]{2,1,0:T(8,128)(2,1)S(1)}, bf16[8,512,128]{2,1,0:T(8,128)(2,1)S(1)}, u32[]{:S(2)}, u32[]{:S(2)}) collective-permute-start(bf16[8,512,128]{2,1,0:T(8,128)(2,1)S(1)} %get-tuple-element.634), channel_id=1, source_target_pairs={{0,2},{1,3},{2,0},{3,1},{4,6},{5,7},{6,4},{7,5},{8,10},{9,11},{10,... | collective-permute-start | bytes 3145736 | tf_op jit(solution)/shard_map/ppermute | solution.py:830
  486.9 89.4 %collective-permute-start.74 = (bf16[1024,512]{1,0:T(8,128)(2,1)}, bf16[1024,512]{1,0:T(8,128)(2,1)}, u32[]{:S(2)}, u32[]{:S(2)}) collective-permute-start(bf16[1024,512]{1,0:T(8,128)(2,1)} %get-tuple-element.624), channel_id=1, source_target_pairs={{0,4},{4,0},{8,12},{12,8},{16,20},{20,16},{24,28},{28,24},{1,5},{5... | collective-permute-start | bytes 3145736 | tf_op jit(solution)/shard_map/ppermute | solution.py:458
  507.1 36.2 %collective-permute-start.60 = (bf16[256,2048]{1,0:T(8,128)(2,1)S(1)}, bf16[256,2048]{1,0:T(8,128)(2,1)S(1)}, u32[]{:S(2)}, u32[]{:S(2)}) collective-permute-start(bf16[256,2048]{1,0:T(8,128)(2,1)S(1)} %add_convert_fusion.15), channel_id=1, source_target_pairs={{0,8},{8,16},{16,24},{24,28},{28,20},{20,12},{12,4},{4,0},{1,9},{9... | collective-permute-start | bytes 3145736 | tf_op jit(solution)/shard_map/ppermute | solution.py:417
  511.0 29.6 %collective-permute-start.61 = (bf16[256,2048]{1,0:T(8,128)(2,1)S(1)}, bf16[256,2048]{1,0:T(8,128)(2,1)S(1)}, u32[]{:S(2)}, u32[]{:S(2)}) collective-permute-start(bf16[256,2048]{1,0:T(8,128)(2,1)S(1)} %add_convert_fusion.16), channel_id=1, source_target_pairs={{0,4},{8,0},{16,8},{24,16},{28,24},{20,28},{12,20},{4,12},{1,5},{9... | collective-permute-start | bytes 3145736 | tf_op jit(solution)/shard_map/ppermute | solution.py:417
  511.3 106.9 %collective-permute-start.85 = (bf16[64,2048]{1,0:T(8,128)(2,1)S(1)}, bf16[64,2048]{1,0:T(8,128)(2,1)}, u32[]{:S(2)}, u32[]{:S(2)}) collective-permute-start(bf16[64,2048]{1,0:T(8,128)(2,1)S(1)} %add_convert_fusion.35), channel_id=1, source_target_pairs={{0,24},{4,28},{8,0},{12,4},{16,8},{20,12},{24,16},{28,20},{1,25},{... | collective-permute-start | bytes 786440 | tf_op jit(solution)/shard_map/ppermute | solution.py:463
  531.7 27.8 %collective-permute-start.59 = (bf16[512,1024]{1,0:T(8,128)(2,1)}, bf16[512,1024]{1,0:T(8,128)(2,1)}, u32[]{:S(2)}, u32[]{:S(2)}) collective-permute-start(bf16[512,1024]{1,0:T(8,128)(2,1)} %pad_maximum_fusion.19), channel_id=1, source_target_pairs={{0,1},{1,0},{2,3},{3,2},{4,5},{5,4},{6,7},{7,6},{8,9},{9,8},{10,11... | collective-permute-start | bytes 3145736 | tf_op jit(solution)/shard_map/ppermute | solution.py:340
  540.6 23.2 %collective-permute-start.68 = (bf16[512,1024]{1,0:T(8,128)(2,1)}, bf16[512,1024]{1,0:T(8,128)(2,1)}, u32[]{:S(2)}, u32[]{:S(2)}) collective-permute-start(bf16[512,1024]{1,0:T(8,128)(2,1)} %pad_maximum_fusion.21), channel_id=1, source_target_pairs={{0,1},{1,0},{2,3},{3,2},{4,5},{5,4},{6,7},{7,6},{8,9},{9,8},{10,11... | collective-permute-start | bytes 3145736 | tf_op jit(solution)/shard_map/ppermute | solution.py:340
  543.3 77.1 %collective-permute-start.84 = (bf16[64,2048]{1,0:T(8,128)(2,1)S(1)}, bf16[64,2048]{1,0:T(8,128)(2,1)}, u32[]{:S(2)}, u32[]{:S(2)}) collective-permute-start(bf16[64,2048]{1,0:T(8,128)(2,1)S(1)} %add_convert_fusion.35), channel_id=1, source_target_pairs={{0,16},{4,20},{8,24},{12,28},{16,0},{20,4},{24,8},{28,12},{1,17},{... | collective-permute-start | bytes 786440 | tf_op jit(solution)/shard_map/ppermute | solution.py:463
  563.9 56.5 %collective-permute-start.83 = (bf16[64,2048]{1,0:T(8,128)(2,1)S(1)}, bf16[64,2048]{1,0:T(8,128)(2,1)}, u32[]{:S(2)}, u32[]{:S(2)}) collective-permute-start(bf16[64,2048]{1,0:T(8,128)(2,1)S(1)} %add_convert_fusion.35), channel_id=1, source_target_pairs={{0,8},{4,12},{8,16},{12,20},{16,24},{20,28},{24,0},{28,4},{1,9},{5... | collective-permute-start | bytes 786440 | tf_op jit(solution)/shard_map/ppermute | solution.py:463
  574.4 25.5 %collective-permute-start.73 = (bf16[256,2048]{1,0:T(8,128)(2,1)S(1)}, bf16[256,2048]{1,0:T(8,128)(2,1)S(1)}, u32[]{:S(2)}, u32[]{:S(2)}) collective-permute-start(bf16[256,2048]{1,0:T(8,128)(2,1)S(1)} %copy-done.83), channel_id=1, source_target_pairs={{0,4},{8,0},{16,8},{24,16},{28,24},{20,28},{12,20},{4,12},{1,5},{9... | collective-permute-start | bytes 3145736 | tf_op jit(solution)/shard_map/ppermute | solution.py:417
  576.3 30.4 %collective-permute-start.72 = (bf16[256,2048]{1,0:T(8,128)(2,1)}, bf16[256,2048]{1,0:T(8,128)(2,1)}, u32[]{:S(2)}, u32[]{:S(2)}) collective-permute-start(bf16[256,2048]{1,0:T(8,128)(2,1)} %add_convert_fusion.12.block_ref), channel_id=1, source_target_pairs={{0,8},{8,16},{16,24},{24,28},{28,20},{20,12},{12,4},{4,0},{1,9},{9... | collective-permute-start | bytes 3145736 | tf_op jit(solution)/shard_map/ppermute | solution.py:417
  615.4 57.8 %collective-permute-start.66 = (bf16[512,512]{1,0:T(8,128)(2,1)}, bf16[512,512]{1,0:T(8,128)(2,1)S(1)}, u32[]{:S(2)}, u32[]{:S(2)}) collective-permute-start(bf16[512,512]{1,0:T(8,128)(2,1)} %constant_dynamic-slice_fusion.19), channel_id=1, source_target_pairs={{0,2},{1,3},{2,0},{3,1},{4,6},{5,7},{6,4},{7,5},{8,10},{9,11},{10,... | collective-permute-start | bytes 1572872 | tf_op jit(solution)/shard_map/ppermute | solution.py:348
  616.5 26.3 %collective-permute-start.82 = (bf16[256,2048]{1,0:T(8,128)(2,1)}, bf16[256,2048]{1,0:T(8,128)(2,1)S(1)}, u32[]{:S(2)}, u32[]{:S(2)}) collective-permute-start(bf16[256,2048]{1,0:T(8,128)(2,1)} %add_convert_fusion.8.block_ref), channel_id=1, source_target_pairs={{0,4},{8,0},{16,8},{24,16},{28,24},{20,28},{12,20},{4,12},{1,5},{9... | collective-permute-start | bytes 3145736 | tf_op jit(solution)/shard_map/ppermute | solution.py:417
  618.2 39.9 %collective-permute-start.80 = (bf16[256,512]{1,0:T(8,128)(2,1)}, bf16[256,512]{1,0:T(8,128)(2,1)S(1)}, u32[]{:S(2)}, u32[]{:S(2)}) collective-permute-start(bf16[256,512]{1,0:T(8,128)(2,1)} %get-tuple-element.694), channel_id=1, source_target_pairs={{0,24},{4,28},{8,0},{12,4},{16,8},{20,12},{24,16},{28,20},{1,25},{... | collective-permute-start | bytes 786440 | tf_op jit(solution)/shard_map/ppermute | solution.py:463
  620.4 44.0 %collective-permute-start.79 = (bf16[256,512]{1,0:T(8,128)(2,1)}, bf16[256,512]{1,0:T(8,128)(2,1)S(1)}, u32[]{:S(2)}, u32[]{:S(2)}) collective-permute-start(bf16[256,512]{1,0:T(8,128)(2,1)} %get-tuple-element.695), channel_id=1, source_target_pairs={{0,16},{4,20},{8,24},{12,28},{16,0},{20,4},{24,8},{28,12},{1,17},{... | collective-permute-start | bytes 786440 | tf_op jit(solution)/shard_map/ppermute | solution.py:463
  620.4 35.2 %collective-permute-start.81 = (bf16[256,2048]{1,0:T(8,128)(2,1)}, bf16[256,2048]{1,0:T(8,128)(2,1)S(1)}, u32[]{:S(2)}, u32[]{:S(2)}) collective-permute-start(bf16[256,2048]{1,0:T(8,128)(2,1)} %collective-permute-done.72), channel_id=1, source_target_pairs={{0,8},{8,16},{16,24},{24,28},{28,20},{20,12},{12,4},{4,0},{1,9},{9... | collective-permute-start | bytes 3145736 | tf_op jit(solution)/shard_map/ppermute | solution.py:417
  642.9 21.6 %collective-permute-start.78 = (bf16[256,512]{1,0:T(8,128)(2,1)S(1)}, bf16[256,512]{1,0:T(8,128)(2,1)S(1)}, u32[]{:S(2)}, u32[]{:S(2)}) collective-permute-start(bf16[256,512]{1,0:T(8,128)(2,1)S(1)} %copy-done.85), channel_id=1, source_target_pairs={{0,8},{4,12},{8,16},{12,20},{16,24},{20,28},{24,0},{28,4},{1,9},{5... | collective-permute-start | bytes 786440 | tf_op jit(solution)/shard_map/ppermute | solution.py:463
  664.4 51.5 %collective-permute-start.93 = (bf16[256,2048]{1,0:T(8,128)(2,1)S(1)}, bf16[256,2048]{1,0:T(8,128)(2,1)S(1)}, u32[]{:S(2)}, u32[]{:S(2)}) collective-permute-start(bf16[256,2048]{1,0:T(8,128)(2,1)S(1)} %constant_dynamic-update-slice_fusion.23), channel_id=1, source_target_pairs={{0,4},{4,0},{8,12},{12,8},{16,20},{20,16},{24,28},{28,24},{1,5},{5... | collective-permute-start | bytes 3145736 | tf_op jit(solution)/shard_map/ppermute | solution.py:458
  665.8 44.5 %collective-permute-start.95 = (bf16[256,2048]{1,0:T(8,128)(2,1)S(1)}, bf16[256,2048]{1,0:T(8,128)(2,1)S(1)}, u32[]{:S(2)}, u32[]{:S(2)}) collective-permute-start(bf16[256,2048]{1,0:T(8,128)(2,1)S(1)} %collective-permute-done.82), channel_id=1, source_target_pairs={{0,4},{8,0},{16,8},{24,16},{28,24},{20,28},{12,20},{4,12},{1,5},{9... | collective-permute-start | bytes 3145736 | tf_op jit(solution)/shard_map/ppermute | solution.py:417
  666.9 53.8 %collective-permute-start.91 = (bf16[256,512]{1,0:T(8,128)(2,1)S(1)}, bf16[256,512]{1,0:T(8,128)(2,1)S(1)}, u32[]{:S(2)}, u32[]{:S(2)}) collective-permute-start(bf16[256,512]{1,0:T(8,128)(2,1)S(1)} %add_convert_fusion.34), channel_id=1, source_target_pairs={{0,24},{4,28},{8,0},{12,4},{16,8},{20,12},{24,16},{28,20},{1,25},{... | collective-permute-start | bytes 786440 | tf_op jit(solution)/shard_map/ppermute | solution.py:463
  675.2 37.3 %collective-permute-start.94 = (bf16[256,2048]{1,0:T(8,128)(2,1)S(1)}, bf16[256,2048]{1,0:T(8,128)(2,1)S(1)}, u32[]{:S(2)}, u32[]{:S(2)}) collective-permute-start(bf16[256,2048]{1,0:T(8,128)(2,1)S(1)} %collective-permute-done.81), channel_id=1, source_target_pairs={{0,8},{8,16},{16,24},{24,28},{28,20},{20,12},{12,4},{4,0},{1,9},{9... | collective-permute-start | bytes 3145736 | tf_op jit(solution)/shard_map/ppermute | solution.py:417
  682.3 38.4 %collective-permute-start.90 = (bf16[256,512]{1,0:T(8,128)(2,1)S(1)}, bf16[256,512]{1,0:T(8,128)(2,1)S(1)}, u32[]{:S(2)}, u32[]{:S(2)}) collective-permute-start(bf16[256,512]{1,0:T(8,128)(2,1)S(1)} %add_convert_fusion.34), channel_id=1, source_target_pairs={{0,16},{4,20},{8,24},{12,28},{16,0},{20,4},{24,8},{28,12},{1,17},{... | collective-permute-start | bytes 786440 | tf_op jit(solution)/shard_map/ppermute | solution.py:463
  715.9 26.9 %collective-permute-start.103 = (bf16[256,2048]{1,0:T(8,128)(2,1)S(1)}, bf16[256,2048]{1,0:T(8,128)(2,1)S(1)}, u32[]{:S(2)}, u32[]{:S(2)}) collective-permute-start(bf16[256,2048]{1,0:T(8,128)(2,1)S(1)} %collective-permute-done.95), channel_id=1, source_target_pairs={{0,4},{8,0},{16,8},{24,16},{28,24},{20,28},{12,20},{4,12},{1,5},{9... | collective-permute-start | bytes 3145736 | tf_op jit(solution)/shard_map/ppermute | solution.py:417
  718.8 26.5 %collective-permute-start.102 = (bf16[256,2048]{1,0:T(8,128)(2,1)S(1)}, bf16[256,2048]{1,0:T(8,128)(2,1)S(1)}, u32[]{:S(2)}, u32[]{:S(2)}) collective-permute-start(bf16[256,2048]{1,0:T(8,128)(2,1)S(1)} %collective-permute-done.94), channel_id=1, source_target_pairs={{0,8},{8,16},{16,24},{24,28},{28,20},{20,12},{12,4},{4,0},{1,9},{9... | collective-permute-start | bytes 3145736 | tf_op jit(solution)/shard_map/ppermute | solution.py:417
  720.9 44.9 %collective-permute-start.110 = (bf16[1024,512]{1,0:T(8,128)(2,1)S(1)}, bf16[1024,512]{1,0:T(8,128)(2,1)S(1)}, u32[]{:S(2)}, u32[]{:S(2)}) collective-permute-start(bf16[1024,512]{1,0:T(8,128)(2,1)S(1)} %constant_dynamic-update-slice_fusion.19), channel_id=1, source_target_pairs={{0,4},{4,0},{8,12},{12,8},{16,20},{20,16},{24,28},{28,24},{1,5},{5... | collective-permute-start | bytes 3145736 | tf_op jit(solution)/shard_map/ppermute | solution.py:458
  727.9 19.0 %collective-permute-start.101 = (bf16[64,256]{1,0:T(8,128)(2,1)S(1)}, bf16[64,256]{1,0:T(8,128)(2,1)S(1)}, u32[]{:S(2)}, u32[]{:S(2)}) collective-permute-start(bf16[64,256]{1,0:T(8,128)(2,1)S(1)} %get-tuple-element.722), channel_id=1, source_target_pairs={{0,24},{4,28},{8,0},{12,4},{16,8},{20,12},{24,16},{28,20},{1,25},{... | collective-permute-start | bytes 98312 | tf_op jit(solution)/shard_map/ppermute | solution.py:463
  748.5 44.3 %collective-permute-start.107 = (bf16[64,256]{1,0:T(8,128)(2,1)S(1)}, bf16[64,256]{1,0:T(8,128)(2,1)S(1)}, u32[]{:S(2)}, u32[]{:S(2)}) collective-permute-start(bf16[64,256]{1,0:T(8,128)(2,1)S(1)} %add_convert_fusion.38), channel_id=1, source_target_pairs={{0,24},{4,28},{8,0},{12,4},{16,8},{20,12},{24,16},{28,20},{1,25},{... | collective-permute-start | bytes 98312 | tf_op jit(solution)/shard_map/ppermute | solution.py:463
  750.2 44.6 %collective-permute-start.106 = (bf16[64,256]{1,0:T(8,128)(2,1)S(1)}, bf16[64,256]{1,0:T(8,128)(2,1)S(1)}, u32[]{:S(2)}, u32[]{:S(2)}) collective-permute-start(bf16[64,256]{1,0:T(8,128)(2,1)S(1)} %add_convert_fusion.38), channel_id=1, source_target_pairs={{0,16},{4,20},{8,24},{12,28},{16,0},{20,4},{24,8},{28,12},{1,17},{... | collective-permute-start | bytes 98312 | tf_op jit(solution)/shard_map/ppermute | solution.py:463
  750.2 44.6 %collective-permute-start.105 = (bf16[64,256]{1,0:T(8,128)(2,1)S(1)}, bf16[64,256]{1,0:T(8,128)(2,1)S(1)}, u32[]{:S(2)}, u32[]{:S(2)}) collective-permute-start(bf16[64,256]{1,0:T(8,128)(2,1)S(1)} %add_convert_fusion.38), channel_id=1, source_target_pairs={{0,8},{4,12},{8,16},{12,20},{16,24},{20,28},{24,0},{28,4},{1,9},{5... | collective-permute-start | bytes 98312 | tf_op jit(solution)/shard_map/ppermute | solution.py:463
  751.6 33.0 %collective-permute-start.109 = (bf16[256,2048]{1,0:T(8,128)(2,1)S(1)}, bf16[256,2048]{1,0:T(8,128)(2,1)}, u32[]{:S(2)}, u32[]{:S(2)}) collective-permute-start(bf16[256,2048]{1,0:T(8,128)(2,1)S(1)} %collective-permute-done.103), channel_id=1, source_target_pairs={{0,4},{8,0},{16,8},{24,16},{28,24},{20,28},{12,20},{4,12},{1,5},{9... | collective-permute-start | bytes 3145736 | tf_op jit(solution)/shard_map/ppermute | solution.py:417
  765.8 24.2 %collective-permute-start.108 = (bf16[256,2048]{1,0:T(8,128)(2,1)S(1)}, bf16[256,2048]{1,0:T(8,128)(2,1)}, u32[]{:S(2)}, u32[]{:S(2)}) collective-permute-start(bf16[256,2048]{1,0:T(8,128)(2,1)S(1)} %collective-permute-done.102), channel_id=1, source_target_pairs={{0,8},{8,16},{16,24},{24,28},{28,20},{20,12},{12,4},{4,0},{1,9},{9... | collective-permute-start | bytes 3145736 | tf_op jit(solution)/shard_map/ppermute | solution.py:417
  784.6 32.5 %collective-permute-start.116 = (bf16[256,2048]{1,0:T(8,128)(2,1)}, bf16[256,2048]{1,0:T(8,128)(2,1)}, u32[]{:S(2)}, u32[]{:S(2)}) collective-permute-start(bf16[256,2048]{1,0:T(8,128)(2,1)} %collective-permute-done.109), channel_id=1, source_target_pairs={{0,4},{8,0},{16,8},{24,16},{28,24},{20,28},{12,20},{4,12},{1,5},{9... | collective-permute-start | bytes 3145736 | tf_op jit(solution)/shard_map/ppermute | solution.py:417
  790.0 31.9 %collective-permute-start.115 = (bf16[256,2048]{1,0:T(8,128)(2,1)}, bf16[256,2048]{1,0:T(8,128)(2,1)S(1)}, u32[]{:S(2)}, u32[]{:S(2)}) collective-permute-start(bf16[256,2048]{1,0:T(8,128)(2,1)} %collective-permute-done.108), channel_id=1, source_target_pairs={{0,8},{8,16},{16,24},{24,28},{28,20},{20,12},{12,4},{4,0},{1,9},{9... | collective-permute-start | bytes 3145736 | tf_op jit(solution)/shard_map/ppermute | solution.py:417
  792.8 21.8 %collective-permute-start.104 = (f32[5888]{0:T(1024)S(1)}, f32[5888]{0:T(1024)S(1)}, u32[]{:S(2)}, u32[]{:S(2)}) collective-permute-start(f32[5888]{0:T(1024)S(1)} %constant_dynamic-update-slice_fusion.28), channel_id=1, source_target_pairs={{0,4},{4,0},{8,12},{12,8},{16,20},{20,16},{24,28},{28,24},{1,5},{5... | collective-permute-start | bytes 70664 | tf_op jit(solution)/shard_map/ppermute | solution.py:458
  821.9 22.8 %collective-permute-start.117 = (bf16[256,2048]{1,0:T(8,128)(2,1)}, bf16[256,2048]{1,0:T(8,128)(2,1)}, u32[]{:S(2)}, u32[]{:S(2)}) collective-permute-start(bf16[256,2048]{1,0:T(8,128)(2,1)} %collective-permute-done.116), channel_id=1, source_target_pairs={{0,4},{8,0},{16,8},{24,16},{28,24},{20,28},{12,20},{4,12},{1,5},{9... | collective-permute-start | bytes 3145736 | tf_op jit(solution)/shard_map/ppermute | solution.py:417
  823.5 25.1 %collective-permute-start.119 = (bf16[256,2048]{1,0:T(8,128)(2,1)S(1)}, bf16[256,2048]{1,0:T(8,128)(2,1)}, u32[]{:S(2)}, u32[]{:S(2)}) collective-permute-start(bf16[256,2048]{1,0:T(8,128)(2,1)S(1)} %collective-permute-done.115), channel_id=1, source_target_pairs={{0,8},{8,16},{16,24},{24,28},{28,20},{20,12},{12,4},{4,0},{1,9},{9... | collective-permute-start | bytes 3145736 | tf_op jit(solution)/shard_map/ppermute | solution.py:417
  844.7 21.9 %collective-permute-start.118 = (bf16[256,2048]{1,0:T(8,128)(2,1)}, bf16[256,2048]{1,0:T(8,128)(2,1)S(1)}, u32[]{:S(2)}, u32[]{:S(2)}) collective-permute-start(bf16[256,2048]{1,0:T(8,128)(2,1)} %collective-permute-done.117), channel_id=1, source_target_pairs={{0,4},{8,0},{16,8},{24,16},{28,24},{20,28},{12,20},{4,12},{1,5},{9... | collective-permute-start | bytes 3145736 | tf_op jit(solution)/shard_map/ppermute | solution.py:417
  (174 other events, 1662.9 us)
Sparse Core Ops, SparseCore 0:
  15.9 70.1 all-gather.2
  827.2 15.1 all-gather.4

commit v2 on v1

--- a/solution.py
+++ b/solution.py
@@ -231,6 +231,89 @@
     )(*lefts, *rights)
 
 
+def pair_kernel(count, *refs):
+    out = refs[-1]
+    middle = refs[count].shape[1]
+    for start, base in ((0, 0), (middle, 2 * count)):
+        total = dot_tn(refs[base][...], refs[base + count][...])
+        for i in range(1, count):
+            total += dot_tn(refs[base + i][...], refs[base + count + i][...])
+        out[:, start : start + middle] = total.astype(BF16)
+
+
+def pair_grad(lefts, rights, more_lefts, more_rights):
+    rows, m = lefts[0].shape
+    n = rights[0].shape[1]
+    bm = min(m, 256)
+    count = len(lefts)
+    left = [pl.BlockSpec((rows, bm), lambda i: (0, i))] * count
+    right = [pl.BlockSpec((rows, n), lambda i: (0, 0))] * count
+    return pl.pallas_call(
+        functools.partial(pair_kernel, count),
+        grid=(m // bm,),
+        in_specs=left + right + left + right,
+        out_specs=pl.BlockSpec((bm, 2 * n), lambda i: (i, 0)),
+        out_shape=jax.ShapeDtypeStruct((m, 2 * n), BF16),
+        compiler_params=pltpu.CompilerParams(vmem_limit_bytes=40 * MIB),
+        cost_estimate=pl.CostEstimate(
+            flops=4 * count * rows * m * n,
+            bytes_accessed=4 * (count * rows * (m + n) + m * n),
+            transcendentals=0,
+        ),
+    )(*lefts, *rights, *more_lefts, *more_rights)
+
+
+def split_kernel(pair, left, right):
+    middle = left.shape[1]
+    left[...] = pair[:, :middle].astype(F32)
+    right[...] = pair[:, middle:].astype(F32).T
+
+
+def split_pair(pair):
+    rows, cols = pair.shape
+    middle = cols // 2
+    tile = math.gcd(rows, 256)
+    return pl.pallas_call(
+        split_kernel,
+        grid=(rows // tile,),
+        in_specs=[pl.BlockSpec((tile, cols), lambda i: (i, 0))],
+        out_specs=[
+            pl.BlockSpec((tile, middle), lambda i: (i, 0)),
+            pl.BlockSpec((middle, tile), lambda i: (0, i)),
+        ],
+        out_shape=[
+            jax.ShapeDtypeStruct((rows, middle), F32),
+            jax.ShapeDtypeStruct((middle, rows), F32),
+        ],
+        compiler_params=pltpu.CompilerParams(vmem_limit_bytes=40 * MIB),
+        cost_estimate=pl.CostEstimate(
+            flops=0, bytes_accessed=6 * rows * cols, transcendentals=0
+        ),
+    )(pair)
+
+
+def back_kernel(x, w, out):
+    out[...] = dot_nt(x[...], w[...]).astype(BF16)
+
+
+def times_transposed(x, w):
+    rows, depth = x.shape
+    cols = w.shape[0]
+    tile = math.gcd(cols, 512)
+    return pl.pallas_call(
+        back_kernel,
+        grid=(cols // tile,),
+        in_specs=[
+            pl.BlockSpec((rows, depth), lambda i: (0, 0)),
+            pl.BlockSpec((tile, depth), lambda i: (i, 0)),
+        ],
+        out_specs=pl.BlockSpec((rows, tile), lambda i: (0, i)),
+        out_shape=jax.ShapeDtypeStruct((rows, cols), BF16),
+        compiler_params=pltpu.CompilerParams(vmem_limit_bytes=40 * MIB),
+        cost_estimate=pl.CostEstimate(flops=1, bytes_accessed=1, transcendentals=0),
+    )(x, w)
+
+
 def place_kernel(index, block_ref, out_ref):
     out_ref[...] = block_ref[...].astype(F32)
 
@@ -403,64 +486,136 @@
         return out
 
 
-class Ring:
-    def __init__(self, clock, grad, way):
-        self.clock, self.grad, self.way = clock, grad, way
+class TwoWay:
+    def __init__(self):
         self.order, _, self.place = ring_table()
         self.size = len(self.order)
-        self.rows = grad.shape[0] // self.size
-        self.step = 0
-        self.out = None
-        self.send(rows_at(grad, self.place, self.rows))
-
-    def send(self, block):
-        self.arrived = lax.ppermute(block, "ctx", ring_shift(self.order, self.way))
+        self.reach = self.size // 2
+        self.holding, self.kept = False, None
+
+    def send(self, ahead, back):
+        if self.holding:
+            self.kept = (ahead, back)
+            return
+        self.arrived = [
+            lax.ppermute(block, "ctx", ring_shift(self.order, way))
+            for block, way in ((ahead, 1), (back, -1))
+        ]
+
+
+    def release(self, *before):
+        self.holding = False
+        if self.kept is not None:
+            kept, self.kept = after(self.kept, *before), None
+            self.send(*kept)
+
+
+def halves_of(block):
+    middle = block.shape[0] // 2
+    return block[:middle], block[middle:]
+
+
+class RingScatter(TwoWay):
+    def __init__(self, clock, own):
+        super().__init__()
+        self.clock, self.own, self.step = clock, own, 0
+        ahead, back = clock(lambda: (halves_of(own(self.reach))[0], halves_of(own(-self.reach))[1]))
+        self.send(ahead, back)
+
+    def turn(self):
+        self.step += 1
+        step, reach = self.step, self.reach
+        assert step <= reach
+
+        def combine(ahead, back):
+            if step == reach:
+                total = self.own(0).astype(F32) + ahead.astype(F32) + back.astype(F32)
+                return (total.astype(BF16),)
+            first, second = self.own(reach - step), self.own(step - reach)
+            if step == 1:
+                (near, far), (low, high) = halves_of(first), halves_of(second)
+                near, high = added([near, ahead]), added([high, back])
+                return jnp.concatenate([near, far]), jnp.concatenate([low, high])
+            return added([first, ahead]), added([second, back])
+
+        held = self.clock(combine, *self.arrived)
+        if step == reach:
+            self.result = held[0]
+        else:
+            self.send(*held)
+
+
+class RingGather(TwoWay):
+    def __init__(self, clock, block, hold=False):
+        super().__init__()
+        self.clock, self.step, self.holding = clock, 0, hold
+        self.send(block, block)
+
+    def turn(self):
+        self.step += 1
+        step, reach = self.step, self.reach
+        assert step <= reach
+        held = self.clock(lambda *blocks: blocks, *self.arrived)
+        if step == reach:
+            return {reach: jnp.concatenate(held)}
+        if step == reach - 1:
+            self.send(halves_of(held[0])[0], halves_of(held[1])[1])
+        else:
+            self.send(*held)
+        return {-step: held[0], step: held[1]}
+
+
+def slot_of(ahead, size):
+    ahead = ahead % size
+    return 2 * ahead if ahead < size // 2 else 2 * (size - ahead) - 1
+
+
+def join_slots(blocks):
+    size = len(blocks)
+    by_slot = {slot_of(ahead, size): block for ahead, block in blocks.items()}
+    return jnp.concatenate([by_slot[i] for i in range(size)], axis=0)
+
+
+def ring_slots():
+    order, table, own = ring_table()
+    size = len(order)
+    ahead = lax.rem(table + jnp.uint32(size) - own, jnp.full((size,), size, jnp.uint32))
+    slots = jnp.where(ahead < size // 2, 2 * ahead, 2 * (size - ahead) - 1)
+    return slots.astype(jnp.int32)
+
+
+class RingSum:
+    def __init__(self, clock, grad, outs, write):
+        self.clock, self.outs, self.write = clock, outs, write
+        place, size = ring_table()[2], lax.axis_size("ctx")
+        rows = grad.shape[0] // size
+        self.place, self.size = place, size
+        self.scatter = RingScatter(
+            clock, lambda i: rows_at(grad, shifted(place, i % size, size), rows)
+        )
+        self.gather = None
 
     def done(self):
-        return self.step == 2 * (self.size - 1)
-
-    def turn(self):
+        return self.gather is not None and self.gather.step == self.gather.reach
+
+    def release(self):
+        (self.gather or self.scatter).release(self.clock.last)
+
+    def turn(self, hold=False):
         if self.done():
             return
-        self.step += 1
-        n = self.size
-        index = shifted(self.place, -self.way * self.step % n, n)
-
-        def add(arrived):
-            own = rows_at(self.grad, index, self.rows)
-            return (arrived.astype(F32) + own.astype(F32)).astype(BF16)
-
-        held = self.clock(add if self.step <= n - 1 else lambda arrived: arrived, self.arrived)
-        if not self.done():
-            self.send(held)
-        if self.step == n - 1:
-            self.out = self.clock(lambda block: place_first(block, index, self.grad.shape), held)
-        elif self.step >= n:
-            self.out = self.clock(
-                lambda out, block: put_rows(out, block.astype(F32), index), self.out, held
-            )
-
-
-def grid_of(size):
-    across = 2 ** (int(math.log2(size)) // 2)
-    return size // across, across
-
-
-class Grid:
-    def __init__(self):
-        self.down, self.across = grid_of(lax.axis_size("ctx"))
-        me = place_of("ctx")
-        self.a, self.b = lax.div(me, jnp.uint32(self.across)), lax.rem(me, jnp.uint32(self.across))
-
-    def send_row(self, values, k):
-        n = self.across
-        pairs = [(a * n + b, a * n + (b + k) % n) for a in range(self.down) for b in range(n)]
-        return lax.ppermute(values, "ctx", pairs)
-
-    def send_column(self, values, k):
-        n, m = self.across, self.down
-        pairs = [(a * n + b, (a + k) % m * n + b) for a in range(m) for b in range(n)]
-        return lax.ppermute(values, "ctx", pairs)
+        (self.gather or self.scatter).holding = hold
+        if self.gather is None:
+            self.scatter.turn()
+            if self.scatter.step < self.scatter.reach:
+                return
+            self.gather = RingGather(self.clock, self.scatter.result, hold)
+            blocks = {0: self.scatter.result}
+        else:
+            blocks = self.gather.turn()
+        for ahead, block in blocks.items():
+            index = shifted(self.place, ahead % self.size, self.size)
+            self.outs = self.clock(lambda outs, b: self.write(outs, b, index), self.outs, block)
 
 
 def added(parts):
@@ -468,108 +623,6 @@
     for part in parts[1:]:
         total = total + part.astype(F32)
     return total.astype(BF16)
-
-
-class GridGather(Grid):
-    def __init__(self, values):
-        super().__init__()
-        self.flight = [values] + [self.send_row(values, j) for j in range(1, self.across)]
-
-    def second(self, clock):
-        row = clock(lambda *parts: jnp.concatenate(parts, axis=0), *self.flight)
-        self.flight = [row] + [self.send_column(row, k) for k in range(1, self.down)]
-
-    def joined(self, clock):
-        return clock(lambda *parts: jnp.concatenate(parts, axis=0), *self.flight)
-
-
-def grid_slots():
-    grid = Grid()
-    down, across = grid.down, grid.across
-    every_a = jnp.array([i // across for i in range(down * across)], jnp.uint32)
-    every_b = jnp.array([i % across for i in range(down * across)], jnp.uint32)
-    k = lax.rem(grid.a + jnp.uint32(down) - every_a, jnp.full_like(every_a, down))
-    j = lax.rem(grid.b + jnp.uint32(across) - every_b, jnp.full_like(every_b, across))
-    return (k * jnp.uint32(across) + j).astype(jnp.int32)
-
-
-class GridScatter(Grid):
-    def __init__(self, clock, values):
-        super().__init__()
-        parts = values.reshape((self.down, self.across) + values.shape[1:])
-        kept = clock(lambda v: [v[:, j] for j in range(self.across)], parts)
-        self.flight = [kept[0]] + [self.send_row(kept[j], -j) for j in range(1, self.across)]
-
-    def second(self, clock):
-        held = clock(lambda *parts: added(parts), *self.flight)
-        self.flight = [held[0]] + [self.send_column(held[k], -k) for k in range(1, self.down)]
-
-    def result(self, clock):
-        return clock(lambda *parts: added(parts), *self.flight)
-
-
-class GridSum(Grid):
-    def __init__(self, grad):
-        super().__init__()
-        self.half, self.block = grad.shape[0] // self.across, grad.shape[0] // lax.axis_size("ctx")
-        self.shape = grad.shape
-        self.flight = [rows_at(grad, self.b, self.half)] + [
-            self.send_row(rows_at(grad, shifted(self.b, k, self.across), self.half), k)
-            for k in range(1, self.across)
-        ]
-
-    def second(self, clock):
-        held = clock(lambda *parts: added(parts), *self.flight)
-        self.flight = [rows_at(held, self.a, self.block)] + [
-            self.send_column(rows_at(held, shifted(self.a, k, self.down), self.block), k)
-            for k in range(1, self.down)
-        ]
-
-    def third(self, clock):
-        held = clock(lambda *parts: added(parts), *self.flight)
-        self.flight = [held] + [self.send_column(held, k) for k in range(1, self.down)]
-
-    def fourth(self, clock):
-        def joined(*blocks):
-            half = jnp.zeros((self.half, self.shape[1]), BF16)
-            for k, block in enumerate(blocks):
-                half = put_rows(half, block, shifted(self.a, -k, self.down))
-            return half
-
-        half = clock(joined, *self.flight)
-        self.flight = [half] + [self.send_row(half, k) for k in range(1, self.across)]
-
-    def result(self, clock, dtype=F32):
-        def joined(*blocks):
-            if self.across == 2:
-                first, last = self.b == 0, self.b == 1
-                sides = [jnp.where(first, *blocks), jnp.where(last, *blocks)]
-                return jnp.concatenate(sides, axis=0).astype(dtype)
-            out = jnp.zeros(self.shape, dtype)
-            for k, block in enumerate(blocks):
-                out = put_rows(out, block.astype(dtype), shifted(self.b, -k, self.across))
-            return out
-
-        return clock(joined, *self.flight)
-
-
-class GridSmallSum(Grid):
-    def __init__(self, values):
-        super().__init__()
-        self.flight = [values] + [self.send_row(values, k) for k in range(1, self.across)]
-
-    def in_order(self, place, size, parts):
-        rows = jnp.zeros((size,) + parts[0].shape, F32)
-        for k, part in enumerate(parts):
-            rows = put_rows(rows, part[None], shifted(place, -k, size))
-        return jnp.sum(rows, axis=0)
-
-    def second(self, clock):
-        held = clock(lambda *parts: self.in_order(self.b, self.across, parts), *self.flight)
-        self.flight = [held] + [self.send_column(held, k) for k in range(1, self.down)]
-
-    def result(self, clock):
-        return clock(lambda *parts: self.in_order(self.a, self.down, parts), *self.flight)
 
 
 def row_stats(values):
@@ -622,7 +675,7 @@
     y, core = tp_place()
     core_swap = tp_pairs(lax.axis_size("tp"), 0, 1)
     query_pos = position * rows + jnp.arange(rows, dtype=jnp.int32)
-    slots = grid_slots()
+    slots = ring_slots()
     info = [
         jnp.concatenate([jnp.stack([lengths[s], position]).astype(jnp.int32), slots]) for s in every
     ]
@@ -683,7 +736,7 @@
     clock = Clock()
     source = clock(lambda t: t, tokens[0])
     near0 = tp_near(source)
-    w_output_all = lax.all_gather(w_output, "tp", axis=0, tiled=True)
+    w_output_all = lax.all_gather(after(w_output, near0), "tp", axis=0, tiled=True)
     vectors = (gain_first, bias_first, gain_second, bias_second, b_output)
     vectors = clock(lambda *v: jnp.stack(v), *vectors)
     vectors = tp_join(tp_near(vectors)).astype(F32)
@@ -697,21 +750,30 @@
         return values, stats, normed, my_half(normed)
 
     x0, stats0, first0, mine0 = clock(enter, *crossed(near0))
-    kv0 = GridGather(mine0)
+    kv0 = RingGather(clock, mine0)
+    keys0, keys1 = {0: mine0}, {}
     q0 = clock(to_queries, first0)
-    cross1 = crossed(after(near1, q0))
-    kv0.second(clock)
+    keys0.update(kv0.turn())
+    cross1 = crossed(after(near1, clock.last))
     x1, stats1, first1, mine1 = clock(enter, *cross1)
-    kv1 = GridGather(mine1)
+    kv1 = RingGather(clock, mine1)
+    keys1[0] = mine1
+    keys0.update(kv0.turn())
     q1 = clock(to_queries, first1)
-    kv1.second(clock)
     inputs, stats_one, first, queries = [x0, x1], [stats0, stats1], [first0, first1], [q0, q1]
-
-    mine = kv0.joined(clock)
-    every_kv = [clock(both_halves, mine, lax.ppermute(mine, "tp", core_swap))]
+    while kv0.step < kv0.reach:
+        keys0.update(kv0.turn())
+        keys1.update(kv1.turn())
+
+    mine = clock(join_slots, keys0)
+    other = lax.ppermute(mine, "tp", core_swap)
+    keys1.update(kv1.turn())
+    every_kv = [clock(both_halves, mine, other)]
     outs = [clock(lambda q, kv: attend(q, kv, info[0], head), q0, every_kv[0])]
     near0 = tp_near(outs[0][1])
-    mine = kv1.joined(clock)
+    while kv1.step < kv1.reach:
+        keys1.update(kv1.turn())
+    mine = clock(join_slots, keys1)
     every_kv.append(clock(both_halves, mine, lax.ppermute(mine, "tp", core_swap)))
     outs.append(clock(lambda q, kv: attend(q, kv, info[1], head), q1, every_kv[1]))
     mixed, attended, lse = zip(*outs)
@@ -773,52 +835,47 @@
         return kept, lax.ppermute(sent, "tp", core_swap)
 
     def add_halves(kept, moved):
-        pair = (kept.astype(F32) + moved.astype(F32)).astype(BF16)
-        return pair.reshape(-1, yrows, rows // yrows, head)
-
-    partial0 = clock(second_partial, d_hidden0)
-    back0 = TpSum(partial0)
+        return added([kept, moved]).reshape(-1, yrows, rows // yrows, head)
+
+    back0 = TpSum(clock(times_transposed, d_hidden0, w_expand))
     back0.across(clock)
-    g1_all = clock(joined, *crossed(after(near_g1, partial0)))
+    g1_all = clock(joined, *crossed(near_g1))
     output = jnp.stack([out0, out1])
     objective = value0 + value1
     d_final, g_shrink, g_shrink_all = [d_final0, d_final1], [g0, g1], [g0_all, g1_all]
     yrows = lax.axis_size("tp") // CORES
 
-    ring_a = Ring(clock, clock(weight_grad, activated, g_shrink_all), 1)
+    def matrix_sum(grad):
+        def write(outs, block, index):
+            if outs is None:
+                return place_first(block, index, grad.shape)
+            return put_rows(outs, block.astype(F32), index)
+
+        return RingSum(clock, grad, None, write)
+
+    ring_s = matrix_sum(clock(weight_grad, activated, g_shrink_all))
     d_own0, near0 = d_second(back0)
     d_hidden1 = clock(lambda g: hidden_grad(1, g), g1_all)
     d_hidden = [d_hidden0, d_hidden1]
-    ring_b = Ring(clock, clock(weight_grad, second, d_hidden), -1)
-    ring_a.turn()
-    cross0 = crossed(after(near0, ring_b.grad))
-    partial1 = clock(second_partial, d_hidden1)
-    back1 = TpSum(partial1)
+    back1 = TpSum(clock(second_partial, d_hidden1))
+    ring_s.turn()
+    back1.across(clock)
+    cross0 = crossed(after(near0, clock.last))
+    ring_e = matrix_sum(clock(weight_grad, second, d_hidden))
     total0, cross_sum0, g_output0, d_att0 = clock(functools.partial(norm_two_back, 0), *cross0)
-    back1.across(clock)
-    ring_b.turn()
-    ring_a.turn()
+    d_own1, near1 = d_second(back1)
+    ring_s.turn()
     d_query0, d_keyval0 = clock(functools.partial(attention_back, 0), d_att0)
     halves0 = swap_halves(d_keyval0)
-    d_own1, near1 = d_second(back1)
-    d_mid0, sums0 = clock(functools.partial(norm_two_own, 0), d_own0, total0, cross_sum0)
-    ring_b.turn()
-    ring_a.turn()
-    pair0 = clock(add_halves, *halves0)
-    total1, cross_sum1, g_output1, d_att1 = clock(
-        functools.partial(norm_two_back, 1), *crossed(after(near1, pair0))
-    )
-    grad_output = GridSum(clock(weight_grad, attended, (g_output0, g_output1)))
-    ring_b.turn()
-    ring_a.turn()
+    ring_e.turn()
+    cross1 = crossed(after(near1, clock.last))
+    total1, cross_sum1, g_output1, d_att1 = clock(functools.partial(norm_two_back, 1), *cross1)
+    ring_s.turn()
     d_query1, d_keyval1 = clock(functools.partial(attention_back, 1), d_att1)
     halves1 = swap_halves(d_keyval1)
-    d_mid1, sums1 = clock(functools.partial(norm_two_own, 1), d_own1, total1, cross_sum1)
-    d_middle, d_queries = [d_mid0, d_mid1], [d_query0, d_query1]
-    ring_b.turn()
-    ring_a.turn()
-    grad_output.second(clock)
-    grad_query = GridSum(clock(weight_grad, first, d_queries))
+    d_queries = [d_query0, d_query1]
+    ring_e.turn()
+    pair0 = clock(add_halves, *halves0)
     pair1 = clock(add_halves, *halves1)
     pair = clock(lambda *v: jnp.concatenate(v, axis=2), pair0, pair1)
 
@@ -830,58 +887,64 @@
         lax.ppermute(split(shifted(y, k, yrows)), "tp", tp_pairs(lax.axis_size("tp"), k, 0))
         for k in range(1, yrows)
     ]
-    ring_b.turn()
-    ring_a.turn()
+    ring_s.turn()
+    grad_pair = clock(pair_grad, first, d_queries, (g_output0, g_output1), attended)
+    ring_e.turn(hold=True)
+    kv_sum = clock(lambda *parts: added(parts), kept, *moved)
+    size = lax.axis_size("ctx")
+    ring_k = RingScatter(clock, lambda i: kv_sum[slot_of(i, size)])
     partials = [
         clock(lambda d: dot_nt(d, w_query).astype(BF16), d_query) for d_query in d_queries
     ]
     sums = [TpSum(p) for p in partials]
-    kv_scatter = GridScatter(clock, clock(lambda *parts: added(parts), kept, *moved))
-    grad_output.third(clock)
-    ring_b.turn()
-    ring_a.turn()
+    ring_s.turn(hold=True)
+    ring_k.turn()
     for part_sum in sums:
         part_sum.across(clock)
-    kv_scatter.second(clock)
-    grad_query.second(clock)
-    ring_b.turn()
-    ring_a.turn()
-    mine = kv_scatter.result(clock).reshape(seqs, -1, head)
-    near = tp_near(mine)
-    grad_output.fourth(clock)
-    ring_b.turn()
-    ring_a.turn()
-    grad_query.third(clock)
+    while ring_k.step < ring_k.reach:
+        ring_k.turn()
+    near = tp_near(ring_k.result.reshape(seqs, -1, head))
+    ring_e.release()
+    ring_s.release()
+    d_mid0, sums0 = clock(functools.partial(norm_two_own, 0), d_own0, total0, cross_sum0)
+    d_mid1, sums1 = clock(functools.partial(norm_two_own, 1), d_own1, total1, cross_sum1)
+    d_middle = [d_mid0, d_mid1]
+    d_firsts = [clock(part_sum.total, part_sum.pair, part_sum.moved) for part_sum in sums]
+    big = [ring_e, ring_s] * size
+    big.pop(0).turn()
+    big.pop(0).turn()
+    shares = clock(
+        lambda *v: tp_ordered(pairs_of(v)),
+        *crossed(tp_near(jnp.broadcast_to(objective, (8, 128)))),
+    )
 
     def join_kv(*blocks):
         blocks = tp_ordered(pairs_of(blocks))
         halves = [jnp.concatenate(blocks[c::CORES], axis=1) for c in range(CORES)]
         return jnp.concatenate(halves, axis=2)
 
-    d_kv_all = clock(join_kv, *crossed(near))
+    d_kv_all = clock(join_kv, *crossed(after(near, clock.last)))
     d_kv = [d_kv_all[s] for s in every]
-    grad_kv = GridSum(clock(weight_grad, [own_cols(f) for f in first], d_kv))
+    grad_kv = clock(weight_grad, [own_cols(f) for f in first], d_kv)
     kv_rows = rows_at(w_keyval, tp_index, part)
 
-    def norm_one_back(s, total, pair, moved):
+    def norm_one_back(s, partial_sum):
         mean, factor = stats_one[s]
-        d_first = total(pair, moved) + dot_nt(d_kv[s], kv_rows)
+        d_first = partial_sum + dot_nt(d_kv[s], kv_rows)
         normed = (tokens[s].astype(F32) - mean) * factor
         scaled = d_first * own_gain_first
         return d_first, jnp.stack([jnp.sum(scaled, axis=-1), jnp.sum(scaled * normed, axis=-1)])
 
     d_firsts, row_sums = zip(
-        *[
-            clock(functools.partial(norm_one_back, s, sums[s].total), sums[s].pair, sums[s].moved)
-            for s in every
-        ]
+        *[clock(functools.partial(norm_one_back, s), d_firsts[s]) for s in every]
     )
-    row_sums = tp_sum(jnp.concatenate(row_sums, axis=0))
-    ring_b.turn()
-    ring_a.turn()
-    grad_w_output = grad_output.result(clock)
-    grad_kv.second(clock)
-    grad_query.fourth(clock)
+    row_sums = clock(lambda *v: jnp.concatenate(v, axis=0), *row_sums)
+    pair = clock(jnp.add, row_sums, lax.ppermute(row_sums, "tp", core_swap))
+    moved = [
+        lax.ppermute(pair, "tp", tp_pairs(lax.axis_size("tp"), k, 0)) for k in range(1, yrows)
+    ]
+    big.pop(0).turn()
+    row_sums = clock(lambda *v: sum(v[1:], v[0]), pair, *moved)
 
     def norm_one_end(s, d_first, row_sums):
         mean, factor = stats_one[s]
@@ -893,10 +956,6 @@
     tokens_grad, sums_first = zip(
         *[clock(functools.partial(norm_one_end, s), d_firsts[s], row_sums) for s in every]
     )
-    shares = tp_ordered(tp_cross(tp_near(jnp.broadcast_to(objective, (8, 128)))))
-    ring_b.turn()
-    ring_a.turn()
-    grad_kv.third(clock)
     objective = sum(part_sum[0, 0] for part_sum in shares)
     small = [
         sum(column_sum(d) for d in d_queries),
@@ -908,24 +967,53 @@
         sums_first[0][1] + sums_first[1][1],
         sums0[0] + sums1[0],
         sums0[1] + sums1[1],
-        jnp.broadcast_to(objective, (128,)),
     ]
-    small_sum = GridSmallSum(clock(lambda v: jnp.concatenate(v), small))
-    grad_w_query = grad_query.result(clock)
-    ring_b.turn()
-    ring_a.turn()
-    grad_kv.fourth(clock)
-    small_sum.second(clock)
-    ring_b.turn()
-    ring_a.turn()
-    grad_w_keyval = grad_kv.result(clock, BF16)
-    grad_w_keyval = lax.all_gather(grad_w_keyval, "tp", axis=0, tiled=True)
-    summed = small_sum.result(clock)
-    while not (ring_a.done() and ring_b.done()):
-        ring_b.turn()
-        ring_a.turn()
-    grad_w_keyval = clock(lambda g: g.astype(F32), grad_w_keyval)
-    grad_w_shrink, grad_w_expand = ring_a.out, ring_b.out
+    kv_shape = grad_kv.shape
+    pieces, rest = [], objective
+    for _ in range(3):
+        pieces.append(rest.astype(BF16).astype(F32))
+        rest = rest - pieces[-1]
+    small.append(jnp.concatenate([jnp.broadcast_to(piece, (128,)) for piece in pieces]))
+    count = sum(v.shape[0] for v in small)
+    more_rows = -(-count // (32 * kv_shape[1])) * 32
+
+    def pack(kv, vectors):
+        vectors = list(vectors) + [jnp.zeros((more_rows * kv_shape[1] - count,), F32)]
+        vectors = jnp.concatenate(vectors).astype(BF16).reshape(more_rows, kv_shape[1])
+        return jnp.concatenate([kv, vectors], axis=0)
+
+    packed = clock(pack, grad_kv, small)
+    big.pop(0).turn()
+    big.pop(0).turn()
+    ring_g = RingGather(clock, packed)
+    every_packed = {0: packed}
+    while ring_g.step < ring_g.reach:
+        big.pop(0).turn()
+        every_packed.update(ring_g.turn())
+    while not ring_s.done():
+        ring_s.turn()
+        ring_e.turn()
+    ring_m = RingSum(clock, grad_pair, jnp.zeros(grad_pair.shape, BF16), put_rows)
+    ring_e.turn()
+    ring_m.turn()
+    place = ring_table()[2]
+
+    def total_of(blocks):
+        rows = jnp.zeros((size * packed.shape[0], kv_shape[1]), BF16)
+        for ahead, block in blocks.items():
+            rows = put_rows(rows, block, shifted(place, ahead % size, size))
+        return jnp.sum(rows.reshape((size,) + packed.shape).astype(F32), axis=0)
+
+    packed_sum = clock(total_of, every_packed)
+    kv_near = tp_near(packed_sum[: kv_shape[0]].astype(BF16))
+    while not (ring_m.done() and ring_e.done()):
+        ring_e.turn()
+        ring_m.turn()
+    grad_w_query, grad_w_output = clock(split_pair, ring_m.outs)
+    kv_blocks = tp_ordered(tp_cross(kv_near))
+    grad_w_keyval = jnp.concatenate(kv_blocks, axis=0).astype(F32)
+    summed = packed_sum[kv_shape[0] :].reshape(-1)
+    grad_w_shrink, grad_w_expand = ring_s.outs, ring_e.outs
 
     pieces, start = [], 0
     for vector in small:
@@ -943,7 +1031,8 @@
         grad_bias_second,
         grand_total,
     ) = pieces
-    loss = grand_total[0] / (jnp.sum(lengths).astype(F32) * width)
+    grand_total = grand_total[0] + grand_total[128] + grand_total[256]
+    loss = grand_total / (jnp.sum(lengths).astype(F32) * width)
     return (
         output,
         jnp.stack(tokens_grad),

time: 884 us -> 800 us (0.905)
  waiting for transfers between devices: 322 us -> 236 us
  starting transfers between devices: 179 us -> 146 us
  local copies, waits for them, and re-layouts: 38.9 us -> 70 us
  Pallas kernels: 71 us -> 85.5 us
  matrix products: 98.6 us -> 88.4 us
    ppermute x71 -> x83, waiting for transfers between devices: 254 us -> 181 us  [the longest x80 180 us: send(): lax.ppermute(block, 'ctx', ring_shift(self.order, way))]
    convert_element_type x20 -> x6, other arithmetic: 40.7 us -> 9.3 us  [the longest x4 7.18 us: combine(): return (total.astype(BF16),)]
    ppermute x71 -> x83, starting transfers between devices: 150 us -> 119 us  [the longest x80 118 us: send(): lax.ppermute(block, 'ctx', ring_shift(self.order, way))]
    convert_element_type x9 -> x15, other arithmetic: 3.95 us -> 25.5 us  [added(): return total.astype(BF16)]
    pallas_call x0 -> x3, Pallas kernels: none -> 20.7 us  [the longest x1 7.97 us: pair_grad(): pl.pallas_call(functools.partial(pair_kernel, count), grid=(m // bm,), in...]
    unnamed x250 -> x316, local copies, waits for them, and re-layouts: 7.71 us -> 24.1 us
    ppermute x1, waiting for transfers between devices: 15.9 us -> 0.01 us  [shards(): lax.ppermute(split(shifted(y, k, yrows)), 'tp', tp_pairs(lax.axis_size('t...]
    slice x1 -> x18, local copies, waits for them, and re-layouts: 0.51 us -> 11.8 us  [the longest x16 10.5 us: halves_of(): return (block[:middle], block[middle:])]
  transfers between devices with their start and end apart: 122 -> 136, of which waited for: 40 -> 64; matrix products, arithmetic and copies ran while one was open for 28% -> 33% of each run, Pallas kernels for 8% -> 9%
where the time goes in v2:
time: 800 us; the launch traced here: 802 us
  waiting for transfers between devices  236 us (30%)
  starting transfers between devices  146 us (18%)
  other arithmetic  146 us (18%)
  matrix products  88.4 us (11%)
  Pallas kernels  85.5 us (11%)
  local copies, waits for them, and re-layouts  70 us (9%)
  between operations  30 us (4%)
    ppermute x80, waiting for transfers between devices, send(): lax.ppermute(block, 'ctx', ring_shift(self.order, way))  180 us
    ppermute x80, starting transfers between devices, send(): lax.ppermute(block, 'ctx', ring_shift(self.order, way))  118 us
    dot_general x10, matrix products, dot_nn(): lax.dot_general(left, right, (((1,), (0,)), ((), ())), preferred_element_...  56.7 us
    ppermute x12, waiting for transfers between devices, tp_near(): lax.ppermute(values, 'tp', tp_pairs(size, k, 0))  38.1 us
    dynamic_update_slice x14, other arithmetic, put_rows(): lax.dynamic_update_slice(target, block, (index * jnp.uint32(block.shape[0...  31.8 us
    dot_general x9, matrix products, dot_nt(): lax.dot_general(left, right, (((1,), (1,)), ((), ())), preferred_element_...  31.7 us
    convert_element_type x15, other arithmetic, added(): return total.astype(BF16)  25.5 us
    pallas_call x3, Pallas kernels, weight_grad(): pl.pallas_call(functools.partial(grad_kernel, count), grid=(m // bm,), in...  25.1 us
  transfers between devices with their start and end apart: 136, of which 64 were waited for; matrix products, arithmetic and copies ran while one was open for 33% of the time, Pallas kernels for 9%

profile of v2, /device:TPU:0, one launch (start us, length us, event | category | flops | bytes accessed | tf_op | source)
XLA Modules:
  0.0 802.4 jit_solution(7614676473095967208)
XLA Ops:
  9.5 3.0 collective-permute-start.1
  16.5 8.0 collective-permute-done.3
  88.2 5.3 shard_map.350
  97.1 5.5 shard_map.351
  104.5 6.3 collective-permute-done.24
  113.8 3.0 broadcast_select_fusion.63
  116.8 9.2 %fusion.65 = (f32[512]{0:T(512)S(1)}, f32[512,2048]{1,0:T(8,128)S(1)}) fusion(f32[2048]{0:T(1024)S(1)} %bitcast.219, bf16[2048,2048]{1,0:T(8,128)(2,1)} %all-gather.2.cloned.1.call-done, bf16[512,512]{1,0:T(8,128)(2,1)} %get-tuple-element.802, bf16[512,512]{1,0:T(8,128)(2,1)} %get-tuple-element.803, bf16[512,512]{1,0:T(8,128)(2,1)} %get-tuple-element.804, ...), kind=kOutput, calls=%fused_computation.471 | convolution fusion | flops 4314889728 | bytes 16787456 | tf_op jit(solution)/shard_map/dot_general | solution.py:22
  128.1 12.9 %add_convert_fusion.4 = (bf16[512,2048]{1,0:T(8,128)(2,1)}, bf16[512,2048]{1,0:T(8,128)(2,1)S(1)}) fusion(f32[2048]{0:T(1024)S(1)} %convert_element_type.749, bf16[512,2048]{1,0:T(8,128)(2,1)S(1)} %add_convert_fusion.5.refs_0_, bf16[2048,2048]{1,0:T(8,128)(2,1)} %w), kind=kOutput, calls=%fused_computation.19 | convolution fusion | flops 4315938816 | bytes 14688256 | tf_op jit(solution)/shard_map/dot_general | solution.py:22
  141.0 5.2 convolution_convert_fusion.4
  148.6 8.2 %fusion.66 = (f32[512]{0:T(512)S(1)}, f32[512,2048]{1,0:T(8,128)S(1)}) fusion(f32[2048]{0:T(1024)S(1)} %bitcast.220, bf16[2048,2048]{1,0:T(8,128)(2,1)} %all-gather.2.cloned.1.call-done, bf16[512,512]{1,0:T(8,128)(2,1)S(1)} %get-tuple-element.798, bf16[512,512]{1,0:T(8,128)(2,1)S(1)} %get-tuple-element.799, bf16[512,512]{1,0:T(8,128)(2,1)S(1)} %get-tuple-element.800, ...), kind=kOutput, calls=%fused_computation.472 | convolution fusion | flops 4314889728 | bytes 16787456 | tf_op jit(solution)/shard_map/dot_general | solution.py:22
  159.6 8.1 %add_convert_fusion.2 = (bf16[512,2048]{1,0:T(8,128)(2,1)}, bf16[512,2048]{1,0:T(8,128)(2,1)S(1)}) fusion(f32[2048]{0:T(1024)S(1)} %copy-done.126, bf16[512,2048]{1,0:T(8,128)(2,1)S(1)} %add_convert_fusion.3.refs_1_, bf16[2048,2048]{1,0:T(8,128)(2,1)S(1)} %bitcast.182), kind=kOutput, calls=%fused_computation.13 | convolution fusion | flops 4315938816 | bytes 14688256 | tf_op jit(solution)/shard_map/dot_general | solution.py:22
  167.7 5.2 collective-permute-done.34
  176.3 8.3 %convolution_convert_fusion.3 = bf16[512,2048]{1,0:T(8,128)(2,1)S(1)} fusion(bf16[512,2048]{1,0:T(8,128)(2,1)S(1)} %get-tuple-element.453.refs_1_, bf16[2048,2048]{1,0:T(8,128)(2,1)} %param.35), kind=kOutput, calls=%fused_computation.36 | convolution fusion | flops 4296015872 | bytes 12582912 | tf_op jit(solution)/shard_map/dot_general | solution.py:22
  186.1 13.3 %collective-permute-done.37 = bf16[512,512]{1,0:T(8,128)(2,1)S(1)} collective-permute-done((bf16[512,512]{1,0:T(8,128)(2,1)S(1)}, bf16[512,512]{1,0:T(8,128)(2,1)S(1)}, u32[]{:S(2)}, u32[]{:S(2)}) %collective-permute-start.37) | collective-permute-done | bytes 524320 | tf_op jit(solution)/shard_map/ppermute | solution.py:382
  203.8 9.2 %convert_reduce_fusion.2 = (f32[2048]{0:T(1024)S(1)}, bf16[512,2048]{1,0:T(8,128)(2,1)S(1)}) fusion(bf16[512,2048]{1,0:T(8,128)(2,1)} %get-tuple-element.737, bf16[512,2048]{1,0:T(8,128)(2,1)S(1)} %pad_maximum_fusion.4.refs_2_, bf16[2048,2048]{1,0:T(8,128)(2,1)} %param.35), kind=kOutput, calls=%fused_computation.2 | convolution fusion | flops 4300208128 | bytes 14688256 | tf_op jit(solution)/shard_map/dot_general | solution.py:26
  215.5 3.0 convert_reduce_fusion.5
  220.4 5.3 shard_map.352
  239.6 3.1 collective-permute-done.43
  249.1 11.9 %shard_map.353 = bf16[2048,2048]{1,0:T(8,128)(2,1)} custom-call(bf16[512,2048]{1,0:T(8,128)(2,1)S(1)} %copy-done.31, bf16[512,2048]{1,0:T(8,128)(2,1)S(1)} %copy-done.33, bf16[512,2048]{1,0:T(8,128)(2,1)S(1)} %copy-done.12, bf16[512,2048]{1,0:T(8,128)(2,1)S(1)} %pad_maximum_fusion.5.refs_3_), custom_call_target="tpu_custom_call" | custom-call | flops 8589934592 | bytes 16777216 | tf_op jit(solution)/shard_map/pallas_call | solution.py:218
  261.1 3.0 constant_dynamic-slice_fusion.4
  264.1 3.8 collective-permute-start.47
  269.1 8.8 %convert_reduce_fusion.1 = (f32[2048]{0:T(1024)S(1)}, bf16[512,2048]{1,0:T(8,128)(2,1)S(1)}) fusion(bf16[512,2048]{1,0:T(8,128)(2,1)} %get-tuple-element.735, bf16[512,2048]{1,0:T(8,128)(2,1)S(1)} %pad_maximum_fusion.5.refs_3_, bf16[2048,2048]{1,0:T(8,128)(2,1)} %param.35), kind=kOutput, calls=%fused_computation.1 | convolution fusion | flops 4300208128 | bytes 14688256 | tf_op jit(solution)/shard_map/dot_general | solution.py:26
  278.0 4.8 convolution_convert_fusion.2
  283.3 5.4 collective-permute-done.48
  291.4 4.5 collective-permute-start.51
  298.3 5.3 collective-permute-done.45
  304.1 12.0 %shard_map.354 = bf16[2048,2048]{1,0:T(8,128)(2,1)} custom-call(bf16[512,2048]{1,0:T(8,128)(2,1)S(1)} %copy-done.14, bf16[512,2048]{1,0:T(8,128)(2,1)S(1)} %copy-done.16, bf16[512,2048]{1,0:T(8,128)(2,1)S(1)} %copy-done.18, bf16[512,2048]{1,0:T(8,128)(2,1)S(1)} %get-tuple-element.469.refs_3_), custom_call_target="tpu_custom_call" | custom-call | flops 8589934592 | bytes 16777216 | tf_op jit(solution)/shard_map/pallas_call | solution.py:218
  316.1 3.0 constant_dynamic-slice_fusion.2
  319.1 4.5 collective-permute-start.55
  332.2 4.0 add_convert_fusion.21
  336.2 3.1 collective-permute-start.62
  340.3 12.1 %shard_map.355 = (bf16[512,512]{1,0:T(8,128)(2,1)}, bf16[4096,256]{1,0:T(8,128)(2,1)}) custom-call(s32[10]{0:T(128)} %copy-done.27, bf16[512,512]{1,0:T(8,128)(2,1)} %copy-done.29, bf16[512,512]{1,0:T(8,128)(2,1)} %convolution_convert_fusion.6.do_ref, f32[512,512]{1,0:T(8,128)} %copy-done.36, f32[512,512]{1,0:T(8,128)} %copy-done.37, ...), custom_call_target="tpu_custom_call" | custom-call | flops 12884901888 | bytes 8388608 | tf_op jit(solution)/shard_map/pallas_call | solution.py:182
  355.4 7.9 collective-permute-start.57
  374.7 4.1 add_convert_fusion.19
  378.7 8.0 collective-permute-start.68
  386.7 11.8 %shard_map.356 = (bf16[512,512]{1,0:T(8,128)(2,1)}, bf16[4096,256]{1,0:T(8,128)(2,1)}) custom-call(s32[10]{0:T(128)} %copy-done.26, bf16[512,512]{1,0:T(8,128)(2,1)} %fusion.17.q_ref, bf16[512,512]{1,0:T(8,128)(2,1)} %convolution_convert_fusion.5.do_ref, f32[512,512]{1,0:T(8,128)} %copy-done.34, f32[512,512]{1,0:T(8,128)} %copy-done.35, ...), custom_call_target="tpu_custom_call" | custom-call | flops 12884901888 | bytes 8388608 | tf_op jit(solution)/shard_map/pallas_call | solution.py:182
  401.0 4.5 add_convert_fusion.17
  405.5 13.2 %collective-permute-start.66 = (bf16[256,2048]{1,0:T(8,128)(2,1)}, bf16[256,2048]{1,0:T(8,128)(2,1)}, u32[]{:S(2)}, u32[]{:S(2)}) collective-permute-start(bf16[256,2048]{1,0:T(8,128)(2,1)} %get-tuple-element.714), channel_id=1, source_target_pairs={{0,8},{8,16},{16,24},{24,28},{28,20},{20,12},{12,4},{4,0},{1,9},{9... | collective-permute-start | bytes 3145736 | tf_op jit(solution)/shard_map/ppermute | solution.py:501
  426.0 6.3 collective-permute-start.72
  444.4 8.0 shard_map.358
  452.4 3.0 add_convert_fusion.12
  467.4 2.8 convert_dynamic-update-slice_fusion.13
  470.2 2.8 convert_dynamic-update-slice_fusion.12
  473.4 7.2 collective-permute-start.74
  502.7 2.8 fusion.57
  508.3 7.1 collective-permute-done.82
  520.5 6.3 collective-permute-done.89
  532.0 13.8 %collective-permute-done.87 = bf16[256,2048]{1,0:T(8,128)(2,1)} collective-permute-done((bf16[256,2048]{1,0:T(8,128)(2,1)}, bf16[256,2048]{1,0:T(8,128)(2,1)}, u32[]{:S(2)}, u32[]{:S(2)}) %collective-permute-start.87) | collective-permute-done | bytes 1048608 | tf_op jit(solution)/shard_map/ppermute | solution.py:501
  549.8 2.8 convert_dynamic-update-slice_fusion.10
  571.0 10.6 %collective-permute-done.96 = bf16[256,2048]{1,0:T(8,128)(2,1)} collective-permute-done((bf16[256,2048]{1,0:T(8,128)(2,1)}, bf16[256,2048]{1,0:T(8,128)(2,1)}, u32[]{:S(2)}, u32[]{:S(2)}) %collective-permute-start.96) | collective-permute-done | bytes 1048608 | tf_op jit(solution)/shard_map/ppermute | solution.py:501
  583.6 2.8 convert_dynamic-update-slice_fusion.9
  586.4 2.9 convert_dynamic-update-slice_fusion.8
  594.9 9.1 %collective-permute-done.100 = bf16[256,2048]{1,0:T(8,128)(2,1)} collective-permute-done((bf16[256,2048]{1,0:T(8,128)(2,1)}, bf16[256,2048]{1,0:T(8,128)(2,1)}, u32[]{:S(2)}, u32[]{:S(2)}) %collective-permute-start.100) | collective-permute-done | bytes 1048608 | tf_op jit(solution)/shard_map/ppermute | solution.py:501
  614.0 2.8 convert_dynamic-update-slice_fusion.6
  616.8 16.7 %collective-permute-done.104 = bf16[256,2048]{1,0:T(8,128)(2,1)S(1)} collective-permute-done((bf16[256,2048]{1,0:T(8,128)(2,1)}, bf16[256,2048]{1,0:T(8,128)(2,1)S(1)}, u32[]{:S(2)}, u32[]{:S(2)}) %collective-permute-start.104) | collective-permute-done | bytes 1048608 | tf_op jit(solution)/shard_map/ppermute | solution.py:501
  639.7 4.9 collective-permute-done.102
  647.5 23.9 %collective-permute-done.99 = bf16[544,256]{1,0:T(8,128)(2,1)S(1)} collective-permute-done((bf16[544,256]{1,0:T(8,128)(2,1)S(1)}, bf16[544,256]{1,0:T(8,128)(2,1)S(1)}, u32[]{:S(2)}, u32[]{:S(2)}) %collective-permute-start.99) | collective-permute-done | bytes 278560 | tf_op jit(solution)/shard_map/ppermute | solution.py:501
  684.8 13.2 %collective-permute-done.110 = bf16[544,256]{1,0:T(8,128)(2,1)S(1)} collective-permute-done((bf16[544,256]{1,0:T(8,128)(2,1)S(1)}, bf16[544,256]{1,0:T(8,128)(2,1)S(1)}, u32[]{:S(2)}, u32[]{:S(2)}) %collective-permute-start.110) | collective-permute-done | bytes 278560 | tf_op jit(solution)/shard_map/ppermute | solution.py:501
  703.3 5.5 collective-permute-done.112
  712.9 8.8 %collective-permute-done.120 = bf16[256,1024]{1,0:T(8,128)(2,1)S(1)} collective-permute-done((bf16[256,1024]{1,0:T(8,128)(2,1)S(1)}, bf16[256,1024]{1,0:T(8,128)(2,1)S(1)}, u32[]{:S(2)}, u32[]{:S(2)}) %collective-permute-start.120) | collective-permute-done | bytes 524320 | tf_op jit(solution)/shard_map/ppermute | solution.py:501
  741.4 8.1 %collective-permute-done.124 = bf16[256,1024]{1,0:T(8,128)(2,1)S(1)} collective-permute-done((bf16[256,1024]{1,0:T(8,128)(2,1)S(1)}, bf16[256,1024]{1,0:T(8,128)(2,1)S(1)}, u32[]{:S(2)}, u32[]{:S(2)}) %collective-permute-start.124) | collective-permute-done | bytes 524320 | tf_op jit(solution)/shard_map/ppermute | solution.py:501
  759.2 3.9 collective-permute-done.126
  771.8 4.8 collective-permute-done.128
  786.8 7.4 shard_map.361
  (800 shorter events, 326.4 us)
Async XLA Ops:
  7.2 109.6 %all-gather.2.cloned.1.call-start = ((), (), s32[]{:S(2)}) async-start(), calls=%async_computation | async-start | bytes 10485760 | tf_op jit(solution)/shard_map/all_gather | solution.py:739
  9.5 15.1 %collective-permute-start.1 = (bf16[512,512]{1,0:T(8,128)(2,1)S(1)}, bf16[512,512]{1,0:T(8,128)(2,1)S(1)}, u32[]{:S(2)}, u32[]{:S(2)}) collective-permute-start(bf16[512,512]{1,0:T(8,128)(2,1)S(1)} %get-tuple-element.355), channel_id=1, source_target_pairs={{0,2},{1,3},{2,0},{3,1},{4,6},{5,7},{6,4},{7,5},{8,10},{9,11},{10,... | collective-permute-start | bytes 1572872 | tf_op jit(solution)/shard_map/ppermute | solution.py:382
  93.9 16.9 %collective-permute-start.24 = (bf16[512,512]{1,0:T(8,128)(2,1)S(1)}, bf16[512,512]{1,0:T(8,128)(2,1)}, u32[]{:S(2)}, u32[]{:S(2)}) collective-permute-start(bf16[512,512]{1,0:T(8,128)(2,1)S(1)} %get-tuple-element.511.refs_6_), channel_id=1, source_target_pairs={{0,2},{1,3},{2,0},{3,1},{4,6},{5,7},{6,4},{7,5},{8,10},{9,11},{10,... | collective-permute-start | bytes 1572872 | tf_op jit(solution)/shard_map/ppermute | solution.py:382
  127.5 19.6 %collective-permute-start.32 = (bf16[512,512]{1,0:T(8,128)(2,1)S(1)}, bf16[512,512]{1,0:T(8,128)(2,1)S(1)}, u32[]{:S(2)}, u32[]{:S(2)}) collective-permute-start(bf16[512,512]{1,0:T(8,128)(2,1)S(1)} %get-tuple-element.512.refs_7_), channel_id=1, source_target_pairs={{0,1},{1,0},{2,3},{3,2},{4,5},{5,4},{6,7},{7,6},{8,9},{9,8},{10,11... | collective-permute-start | bytes 1572872 | tf_op jit(solution)/shard_map/ppermute | solution.py:387
  127.7 19.4 %collective-permute-start.33 = (bf16[512,512]{1,0:T(8,128)(2,1)}, bf16[512,512]{1,0:T(8,128)(2,1)S(1)}, u32[]{:S(2)}, u32[]{:S(2)}) collective-permute-start(bf16[512,512]{1,0:T(8,128)(2,1)} %collective-permute-done.31), channel_id=1, source_target_pairs={{0,1},{1,0},{2,3},{3,2},{4,5},{5,4},{6,7},{7,6},{8,9},{9,8},{10,11... | collective-permute-start | bytes 1572872 | tf_op jit(solution)/shard_map/ppermute | solution.py:387
  184.9 15.1 %collective-permute-start.35 = (bf16[512,1024]{1,0:T(8,128)(2,1)S(1)}, bf16[512,1024]{1,0:T(8,128)(2,1)S(1)}, u32[]{:S(2)}, u32[]{:S(2)}) collective-permute-start(bf16[512,1024]{1,0:T(8,128)(2,1)S(1)} %pad_maximum_fusion.12), channel_id=1, source_target_pairs={{0,1},{1,0},{2,3},{3,2},{4,5},{5,4},{6,7},{7,6},{8,9},{9,8},{10,11... | collective-permute-start | bytes 3145736 | tf_op jit(solution)/shard_map/ppermute | solution.py:423
  228.0 16.0 %collective-permute-start.40 = (bf16[512,1024]{1,0:T(8,128)(2,1)}, bf16[512,1024]{1,0:T(8,128)(2,1)}, u32[]{:S(2)}, u32[]{:S(2)}) collective-permute-start(bf16[512,1024]{1,0:T(8,128)(2,1)} %pad_maximum_fusion.15), channel_id=1, source_target_pairs={{0,1},{1,0},{2,3},{3,2},{4,5},{5,4},{6,7},{7,6},{8,9},{9,8},{10,11... | collective-permute-start | bytes 3145736 | tf_op jit(solution)/shard_map/ppermute | solution.py:423
  245.7 22.1 %collective-permute-start.41 = (bf16[512,512]{1,0:T(8,128)(2,1)S(1)}, bf16[512,512]{1,0:T(8,128)(2,1)S(1)}, u32[]{:S(2)}, u32[]{:S(2)}) collective-permute-start(bf16[512,512]{1,0:T(8,128)(2,1)S(1)} %constant_dynamic-slice_fusion.33), channel_id=1, source_target_pairs={{0,2},{1,3},{2,0},{3,1},{4,6},{5,7},{6,4},{7,5},{8,10},{9,11},{10,... | collective-permute-start | bytes 1572872 | tf_op jit(solution)/shard_map/ppermute | solution.py:431
  264.1 19.2 %collective-permute-start.47 = (bf16[128,2048]{1,0:T(8,128)(2,1)}, bf16[128,2048]{1,0:T(8,128)(2,1)S(1)}, u32[]{:S(2)}, u32[]{:S(2)}) collective-permute-start(bf16[128,2048]{1,0:T(8,128)(2,1)} %get-tuple-element.726), channel_id=1, source_target_pairs={{0,8},{8,16},{16,24},{24,28},{28,20},{20,12},{12,4},{4,0},{1,9},{9... | collective-permute-start | bytes 1572872 | tf_op jit(solution)/shard_map/ppermute | solution.py:501
  267.8 20.8 %collective-permute-start.48 = (bf16[128,2048]{1,0:T(8,128)(2,1)}, bf16[128,2048]{1,0:T(8,128)(2,1)S(1)}, u32[]{:S(2)}, u32[]{:S(2)}) collective-permute-start(bf16[128,2048]{1,0:T(8,128)(2,1)} %get-tuple-element.728), channel_id=1, source_target_pairs={{0,4},{8,0},{16,8},{24,16},{28,24},{20,28},{12,20},{4,12},{1,5},{9... | collective-permute-start | bytes 1572872 | tf_op jit(solution)/shard_map/ppermute | solution.py:501
  288.6 15.0 %collective-permute-start.45 = (bf16[512,512]{1,0:T(8,128)(2,1)S(1)}, bf16[512,512]{1,0:T(8,128)(2,1)}, u32[]{:S(2)}, u32[]{:S(2)}) collective-permute-start(bf16[512,512]{1,0:T(8,128)(2,1)S(1)} %get-tuple-element.472), channel_id=1, source_target_pairs={{0,2},{1,3},{2,0},{3,1},{4,6},{5,7},{6,4},{7,5},{8,10},{9,11},{10,... | collective-permute-start | bytes 1572872 | tf_op jit(solution)/shard_map/ppermute | solution.py:382
  291.4 40.8 %collective-permute-start.51 = (bf16[256,2048]{1,0:T(8,128)(2,1)S(1)}, bf16[256,2048]{1,0:T(8,128)(2,1)S(1)}, u32[]{:S(2)}, u32[]{:S(2)}) collective-permute-start(bf16[256,2048]{1,0:T(8,128)(2,1)S(1)} %pad_maximum_fusion.18), channel_id=1, source_target_pairs={{0,8},{8,16},{16,24},{24,28},{28,20},{20,12},{12,4},{4,0},{1,9},{9... | collective-permute-start | bytes 3145736 | tf_op jit(solution)/shard_map/ppermute | solution.py:501
  296.0 36.2 %collective-permute-start.52 = (bf16[256,2048]{1,0:T(8,128)(2,1)S(1)}, bf16[256,2048]{1,0:T(8,128)(2,1)}, u32[]{:S(2)}, u32[]{:S(2)}) collective-permute-start(bf16[256,2048]{1,0:T(8,128)(2,1)S(1)} %pad_maximum_fusion.19), channel_id=1, source_target_pairs={{0,4},{8,0},{16,8},{24,16},{28,24},{20,28},{12,20},{4,12},{1,5},{9... | collective-permute-start | bytes 3145736 | tf_op jit(solution)/shard_map/ppermute | solution.py:501
  297.3 33.7 %collective-permute-start.53 = (bf16[512,512]{1,0:T(8,128)(2,1)S(1)}, bf16[512,512]{1,0:T(8,128)(2,1)S(1)}, u32[]{:S(2)}, u32[]{:S(2)}) collective-permute-start(bf16[512,512]{1,0:T(8,128)(2,1)S(1)} %constant_dynamic-slice_fusion.25), channel_id=1, source_target_pairs={{0,2},{1,3},{2,0},{3,1},{4,6},{5,7},{6,4},{7,5},{8,10},{9,11},{10,... | collective-permute-start | bytes 1572872 | tf_op jit(solution)/shard_map/ppermute | solution.py:431
  303.6 15.5 %collective-permute-start.49 = (bf16[512,512]{1,0:T(8,128)(2,1)S(1)}, bf16[512,512]{1,0:T(8,128)(2,1)S(1)}, u32[]{:S(2)}, u32[]{:S(2)}) collective-permute-start(bf16[512,512]{1,0:T(8,128)(2,1)S(1)} %get-tuple-element.472), channel_id=1, source_target_pairs={{0,1},{1,0},{2,3},{3,2},{4,5},{5,4},{6,7},{7,6},{8,9},{9,8},{10,11... | collective-permute-start | bytes 1572872 | tf_op jit(solution)/shard_map/ppermute | solution.py:387
  303.6 20.0 %collective-permute-start.50 = (bf16[512,512]{1,0:T(8,128)(2,1)}, bf16[512,512]{1,0:T(8,128)(2,1)S(1)}, u32[]{:S(2)}, u32[]{:S(2)}) collective-permute-start(bf16[512,512]{1,0:T(8,128)(2,1)} %collective-permute-done.45), channel_id=1, source_target_pairs={{0,1},{1,0},{2,3},{3,2},{4,5},{5,4},{6,7},{7,6},{8,9},{9,8},{10,11... | collective-permute-start | bytes 1572872 | tf_op jit(solution)/shard_map/ppermute | solution.py:387
  319.1 33.3 %collective-permute-start.55 = (bf16[128,2048]{1,0:T(8,128)(2,1)}, bf16[128,2048]{1,0:T(8,128)(2,1)S(1)}, u32[]{:S(2)}, u32[]{:S(2)}) collective-permute-start(bf16[128,2048]{1,0:T(8,128)(2,1)} %get-tuple-element.718), channel_id=1, source_target_pairs={{0,8},{8,16},{16,24},{24,28},{28,20},{20,12},{12,4},{4,0},{1,9},{9... | collective-permute-start | bytes 1572872 | tf_op jit(solution)/shard_map/ppermute | solution.py:501
  323.6 28.8 %collective-permute-start.56 = (bf16[128,2048]{1,0:T(8,128)(2,1)}, bf16[128,2048]{1,0:T(8,128)(2,1)}, u32[]{:S(2)}, u32[]{:S(2)}) collective-permute-start(bf16[128,2048]{1,0:T(8,128)(2,1)} %get-tuple-element.720), channel_id=1, source_target_pairs={{0,4},{8,0},{16,8},{24,16},{28,24},{20,28},{12,20},{4,12},{1,5},{9... | collective-permute-start | bytes 1572872 | tf_op jit(solution)/shard_map/ppermute | solution.py:501
  336.2 38.4 %collective-permute-start.62 = (bf16[256,2048]{1,0:T(8,128)(2,1)}, bf16[256,2048]{1,0:T(8,128)(2,1)}, u32[]{:S(2)}, u32[]{:S(2)}) collective-permute-start(bf16[256,2048]{1,0:T(8,128)(2,1)} %get-tuple-element.724), channel_id=1, source_target_pairs={{0,8},{8,16},{16,24},{24,28},{28,20},{20,12},{12,4},{4,0},{1,9},{9... | collective-permute-start | bytes 3145736 | tf_op jit(solution)/shard_map/ppermute | solution.py:501
  339.3 35.4 %collective-permute-start.63 = (bf16[256,2048]{1,0:T(8,128)(2,1)}, bf16[256,2048]{1,0:T(8,128)(2,1)}, u32[]{:S(2)}, u32[]{:S(2)}) collective-permute-start(bf16[256,2048]{1,0:T(8,128)(2,1)} %get-tuple-element.723), channel_id=1, source_target_pairs={{0,4},{8,0},{16,8},{24,16},{28,24},{20,28},{12,20},{4,12},{1,5},{9... | collective-permute-start | bytes 3145736 | tf_op jit(solution)/shard_map/ppermute | solution.py:501
  339.3 25.1 %collective-permute-start.59 = (bf16[512,512]{1,0:T(8,128)(2,1)S(1)}, bf16[512,512]{1,0:T(8,128)(2,1)}, u32[]{:S(2)}, u32[]{:S(2)}) collective-permute-start(bf16[512,512]{1,0:T(8,128)(2,1)S(1)} %get-tuple-element.487), channel_id=1, source_target_pairs={{0,2},{1,3},{2,0},{3,1},{4,6},{5,7},{6,4},{7,5},{8,10},{9,11},{10,... | collective-permute-start | bytes 1572872 | tf_op jit(solution)/shard_map/ppermute | solution.py:382
  355.4 43.1 %collective-permute-start.57 = (bf16[256,2048]{1,0:T(8,128)(2,1)}, bf16[256,2048]{1,0:T(8,128)(2,1)}, u32[]{:S(2)}, u32[]{:S(2)}) collective-permute-start(bf16[256,2048]{1,0:T(8,128)(2,1)} %pad_maximum_fusion.20), channel_id=1, source_target_pairs={{0,8},{8,16},{16,24},{24,28},{28,20},{20,12},{12,4},{4,0},{1,9},{9... | collective-permute-start | bytes 3145736 | tf_op jit(solution)/shard_map/ppermute | solution.py:501
  367.0 32.2 %collective-permute-start.58 = (bf16[256,2048]{1,0:T(8,128)(2,1)}, bf16[256,2048]{1,0:T(8,128)(2,1)}, u32[]{:S(2)}, u32[]{:S(2)}) collective-permute-start(bf16[256,2048]{1,0:T(8,128)(2,1)} %pad_maximum_fusion.21), channel_id=1, source_target_pairs={{0,4},{8,0},{16,8},{24,16},{28,24},{20,28},{12,20},{4,12},{1,5},{9... | collective-permute-start | bytes 3145736 | tf_op jit(solution)/shard_map/ppermute | solution.py:501
  367.3 51.4 %collective-permute-start.54 = (bf16[4096,128]{1,0:T(8,128)(2,1)}, bf16[4096,128]{1,0:T(8,128)(2,1)}, u32[]{:S(2)}, u32[]{:S(2)}) collective-permute-start(bf16[4096,128]{1,0:T(8,128)(2,1)} %get-tuple-element.763), channel_id=1, source_target_pairs={{0,1},{1,0},{2,3},{3,2},{4,5},{5,4},{6,7},{7,6},{8,9},{9,8},{10,11... | collective-permute-start | bytes 3145736 | tf_op jit(solution)/shard_map/ppermute | solution.py:835
  378.7 44.5 %collective-permute-start.68 = (bf16[256,2048]{1,0:T(8,128)(2,1)}, bf16[256,2048]{1,0:T(8,128)(2,1)S(1)}, u32[]{:S(2)}, u32[]{:S(2)}) collective-permute-start(bf16[256,2048]{1,0:T(8,128)(2,1)} %get-tuple-element.716), channel_id=1, source_target_pairs={{0,8},{8,16},{16,24},{24,28},{28,20},{20,12},{12,4},{4,0},{1,9},{9... | collective-permute-start | bytes 3145736 | tf_op jit(solution)/shard_map/ppermute | solution.py:501
  386.7 36.5 %collective-permute-start.69 = (bf16[256,2048]{1,0:T(8,128)(2,1)S(1)}, bf16[256,2048]{1,0:T(8,128)(2,1)S(1)}, u32[]{:S(2)}, u32[]{:S(2)}) collective-permute-start(bf16[256,2048]{1,0:T(8,128)(2,1)S(1)} %get-tuple-element.715), channel_id=1, source_target_pairs={{0,4},{8,0},{16,8},{24,16},{28,24},{20,28},{12,20},{4,12},{1,5},{9... | collective-permute-start | bytes 3145736 | tf_op jit(solution)/shard_map/ppermute | solution.py:501
  400.9 19.3 %collective-permute-start.64 = (bf16[4096,128]{1,0:T(8,128)(2,1)S(1)}, bf16[4096,128]{1,0:T(8,128)(2,1)S(1)}, u32[]{:S(2)}, u32[]{:S(2)}) collective-permute-start(bf16[4096,128]{1,0:T(8,128)(2,1)S(1)} %get-tuple-element.761), channel_id=1, source_target_pairs={{0,1},{1,0},{2,3},{3,2},{4,5},{5,4},{6,7},{7,6},{8,9},{9,8},{10,11... | collective-permute-start | bytes 3145736 | tf_op jit(solution)/shard_map/ppermute | solution.py:835
  405.5 46.9 %collective-permute-start.66 = (bf16[256,2048]{1,0:T(8,128)(2,1)}, bf16[256,2048]{1,0:T(8,128)(2,1)}, u32[]{:S(2)}, u32[]{:S(2)}) collective-permute-start(bf16[256,2048]{1,0:T(8,128)(2,1)} %get-tuple-element.714), channel_id=1, source_target_pairs={{0,8},{8,16},{16,24},{24,28},{28,20},{20,12},{12,4},{4,0},{1,9},{9... | collective-permute-start | bytes 3145736 | tf_op jit(solution)/shard_map/ppermute | solution.py:501
  418.7 33.7 %collective-permute-start.67 = (bf16[256,2048]{1,0:T(8,128)(2,1)}, bf16[256,2048]{1,0:T(8,128)(2,1)}, u32[]{:S(2)}, u32[]{:S(2)}) collective-permute-start(bf16[256,2048]{1,0:T(8,128)(2,1)} %get-tuple-element.713), channel_id=1, source_target_pairs={{0,4},{8,0},{16,8},{24,16},{28,24},{20,28},{12,20},{4,12},{1,5},{9... | collective-permute-start | bytes 3145736 | tf_op jit(solution)/shard_map/ppermute | solution.py:501
  422.2 33.2 %collective-permute-start.65 = (bf16[8,512,128]{2,1,0:T(8,128)(2,1)}, bf16[8,512,128]{2,1,0:T(8,128)(2,1)}, u32[]{:S(2)}, u32[]{:S(2)}) collective-permute-start(bf16[8,512,128]{2,1,0:T(8,128)(2,1)} %get-tuple-element.759), channel_id=1, source_target_pairs={{0,2},{1,3},{2,0},{3,1},{4,6},{5,7},{6,4},{7,5},{8,10},{9,11},{10,... | collective-permute-start | bytes 3145736 | tf_op jit(solution)/shard_map/ppermute | solution.py:887
  426.0 38.9 %collective-permute-start.72 = (bf16[256,2048]{1,0:T(8,128)(2,1)}, bf16[256,2048]{1,0:T(8,128)(2,1)}, u32[]{:S(2)}, u32[]{:S(2)}) collective-permute-start(bf16[256,2048]{1,0:T(8,128)(2,1)} %add_convert_fusion.14.block_ref), channel_id=1, source_target_pairs={{0,8},{8,16},{16,24},{24,28},{28,20},{20,12},{12,4},{4,0},{1,9},{9... | collective-permute-start | bytes 3145736 | tf_op jit(solution)/shard_map/ppermute | solution.py:501
  432.3 35.1 %collective-permute-start.73 = (bf16[256,2048]{1,0:T(8,128)(2,1)}, bf16[256,2048]{1,0:T(8,128)(2,1)}, u32[]{:S(2)}, u32[]{:S(2)}) collective-permute-start(bf16[256,2048]{1,0:T(8,128)(2,1)} %add_convert_fusion.14.block_ref), channel_id=1, source_target_pairs={{0,4},{8,0},{16,8},{24,16},{28,24},{20,28},{12,20},{4,12},{1,5},{9... | collective-permute-start | bytes 3145736 | tf_op jit(solution)/shard_map/ppermute | solution.py:501
  457.0 16.3 %collective-permute-start.70 = (bf16[256,128]{1,0:T(8,128)(2,1)S(1)}, bf16[256,128]{1,0:T(8,128)(2,1)S(1)}, u32[]{:S(2)}, u32[]{:S(2)}) collective-permute-start(bf16[256,128]{1,0:T(8,128)(2,1)S(1)} %get-tuple-element.828), channel_id=1, source_target_pairs={{0,8},{8,16},{16,24},{24,28},{28,20},{20,12},{12,4},{4,0},{1,9},{9... | collective-permute-start | bytes 196616 | tf_op jit(solution)/shard_map/ppermute | solution.py:501
  462.1 19.0 %collective-permute-start.76 = (bf16[512,1024]{1,0:T(8,128)(2,1)S(1)}, bf16[512,1024]{1,0:T(8,128)(2,1)S(1)}, u32[]{:S(2)}, u32[]{:S(2)}) collective-permute-start(bf16[512,1024]{1,0:T(8,128)(2,1)S(1)} %pad_maximum_fusion.23), channel_id=1, source_target_pairs={{0,1},{1,0},{2,3},{3,2},{4,5},{5,4},{6,7},{7,6},{8,9},{9,8},{10,11... | collective-permute-start | bytes 3145736 | tf_op jit(solution)/shard_map/ppermute | solution.py:423
  465.0 15.6 %collective-permute-start.77 = (bf16[512,1024]{1,0:T(8,128)(2,1)S(1)}, bf16[512,1024]{1,0:T(8,128)(2,1)S(1)}, u32[]{:S(2)}, u32[]{:S(2)}) collective-permute-start(bf16[512,1024]{1,0:T(8,128)(2,1)S(1)} %pad_maximum_fusion.25), channel_id=1, source_target_pairs={{0,1},{1,0},{2,3},{3,2},{4,5},{5,4},{6,7},{7,6},{8,9},{9,8},{10,11... | collective-permute-start | bytes 3145736 | tf_op jit(solution)/shard_map/ppermute | solution.py:423
  496.0 20.9 %collective-permute-start.91 = (bf16[512,512]{1,0:T(8,128)(2,1)S(1)}, bf16[512,512]{1,0:T(8,128)(2,1)S(1)}, u32[]{:S(2)}, u32[]{:S(2)}) collective-permute-start(bf16[512,512]{1,0:T(8,128)(2,1)S(1)} %constant_dynamic-slice_fusion.8), channel_id=1, source_target_pairs={{0,2},{1,3},{2,0},{3,1},{4,6},{5,7},{6,4},{7,5},{8,10},{9,11},{10,... | collective-permute-start | bytes 1572872 | tf_op jit(solution)/shard_map/ppermute | solution.py:431
  497.1 18.3 %collective-permute-start.82 = (bf16[512,512]{1,0:T(8,128)(2,1)S(1)}, bf16[512,512]{1,0:T(8,128)(2,1)S(1)}, u32[]{:S(2)}, u32[]{:S(2)}) collective-permute-start(bf16[512,512]{1,0:T(8,128)(2,1)S(1)} %constant_dynamic-slice_fusion.11), channel_id=1, source_target_pairs={{0,2},{1,3},{2,0},{3,1},{4,6},{5,7},{6,4},{7,5},{8,10},{9,11},{10,... | collective-permute-start | bytes 1572872 | tf_op jit(solution)/shard_map/ppermute | solution.py:431
  500.6 26.1 %collective-permute-start.89 = (bf16[256,2048]{1,0:T(8,128)(2,1)S(1)}, bf16[256,2048]{1,0:T(8,128)(2,1)S(1)}, u32[]{:S(2)}, u32[]{:S(2)}) collective-permute-start(bf16[256,2048]{1,0:T(8,128)(2,1)S(1)} %get-tuple-element.547), channel_id=1, source_target_pairs={{0,8},{8,16},{16,24},{24,28},{28,20},{20,12},{12,4},{4,0},{1,9},{9... | collective-permute-start | bytes 3145736 | tf_op jit(solution)/shard_map/ppermute | solution.py:501
  500.7 26.1 %collective-permute-start.90 = (bf16[256,2048]{1,0:T(8,128)(2,1)S(1)}, bf16[256,2048]{1,0:T(8,128)(2,1)S(1)}, u32[]{:S(2)}, u32[]{:S(2)}) collective-permute-start(bf16[256,2048]{1,0:T(8,128)(2,1)S(1)} %get-tuple-element.548), channel_id=1, source_target_pairs={{0,4},{8,0},{16,8},{24,16},{28,24},{20,28},{12,20},{4,12},{1,5},{9... | collective-permute-start | bytes 3145736 | tf_op jit(solution)/shard_map/ppermute | solution.py:501
  505.5 40.3 %collective-permute-start.87 = (bf16[256,2048]{1,0:T(8,128)(2,1)}, bf16[256,2048]{1,0:T(8,128)(2,1)}, u32[]{:S(2)}, u32[]{:S(2)}) collective-permute-start(bf16[256,2048]{1,0:T(8,128)(2,1)} %collective-permute-done.72), channel_id=1, source_target_pairs={{0,8},{8,16},{16,24},{24,28},{28,20},{20,12},{12,4},{4,0},{1,9},{9... | collective-permute-start | bytes 3145736 | tf_op jit(solution)/shard_map/ppermute | solution.py:501
  515.5 30.5 %collective-permute-start.88 = (bf16[256,2048]{1,0:T(8,128)(2,1)}, bf16[256,2048]{1,0:T(8,128)(2,1)}, u32[]{:S(2)}, u32[]{:S(2)}) collective-permute-start(bf16[256,2048]{1,0:T(8,128)(2,1)} %collective-permute-done.73), channel_id=1, source_target_pairs={{0,4},{8,0},{16,8},{24,16},{28,24},{20,28},{12,20},{4,12},{1,5},{9... | collective-permute-start | bytes 3145736 | tf_op jit(solution)/shard_map/ppermute | solution.py:501
  520.5 32.1 %collective-permute-start.84 = (f32[8,128]{1,0:T(8,128)S(1)}, f32[8,128]{1,0:T(8,128)S(1)}, u32[]{:S(2)}, u32[]{:S(2)}) collective-permute-start(f32[8,128]{1,0:T(8,128)S(1)} %broadcast_in_dim.14), channel_id=1, source_target_pairs={{0,1},{1,0},{2,3},{3,2},{4,5},{5,4},{6,7},{7,6},{8,9},{9,8},{10,11... | collective-permute-start | bytes 12296 | tf_op jit(solution)/shard_map/ppermute | solution.py:387
  526.8 25.8 %collective-permute-start.86 = (f32[8,128]{1,0:T(8,128)S(1)}, f32[8,128]{1,0:T(8,128)}, u32[]{:S(2)}, u32[]{:S(2)}) collective-permute-start(f32[8,128]{1,0:T(8,128)S(1)} %collective-permute-done.85), channel_id=1, source_target_pairs={{0,1},{1,0},{2,3},{3,2},{4,5},{5,4},{6,7},{7,6},{8,9},{9,8},{10,11... | collective-permute-start | bytes 12296 | tf_op jit(solution)/shard_map/ppermute | solution.py:387
  526.9 27.6 %collective-permute-start.116 = (bf16[128,1024]{1,0:T(8,128)(2,1)}, bf16[128,1024]{1,0:T(8,128)(2,1)}, u32[]{:S(2)}, u32[]{:S(2)}) collective-permute-start(bf16[128,1024]{1,0:T(8,128)(2,1)} %get-tuple-element.744), channel_id=1, source_target_pairs={{0,8},{8,16},{16,24},{24,28},{28,20},{20,12},{12,4},{4,0},{1,9},{9... | collective-permute-start | bytes 786440 | tf_op jit(solution)/shard_map/ppermute | solution.py:501
  555.2 26.4 %collective-permute-start.96 = (bf16[256,2048]{1,0:T(8,128)(2,1)}, bf16[256,2048]{1,0:T(8,128)(2,1)}, u32[]{:S(2)}, u32[]{:S(2)}) collective-permute-start(bf16[256,2048]{1,0:T(8,128)(2,1)} %add_convert_fusion.8.block_ref), channel_id=1, source_target_pairs={{0,8},{8,16},{16,24},{24,28},{28,20},{20,12},{12,4},{4,0},{1,9},{9... | collective-permute-start | bytes 3145736 | tf_op jit(solution)/shard_map/ppermute | solution.py:501
  557.2 26.4 %collective-permute-start.97 = (bf16[256,2048]{1,0:T(8,128)(2,1)}, bf16[256,2048]{1,0:T(8,128)(2,1)}, u32[]{:S(2)}, u32[]{:S(2)}) collective-permute-start(bf16[256,2048]{1,0:T(8,128)(2,1)} %add_convert_fusion.8.block_ref), channel_id=1, source_target_pairs={{0,4},{8,0},{16,8},{24,16},{28,24},{20,28},{12,20},{4,12},{1,5},{9... | collective-permute-start | bytes 3145736 | tf_op jit(solution)/shard_map/ppermute | solution.py:501
  559.4 44.7 %collective-permute-start.100 = (bf16[256,2048]{1,0:T(8,128)(2,1)}, bf16[256,2048]{1,0:T(8,128)(2,1)}, u32[]{:S(2)}, u32[]{:S(2)}) collective-permute-start(bf16[256,2048]{1,0:T(8,128)(2,1)} %collective-permute-done.87), channel_id=1, source_target_pairs={{0,8},{8,16},{16,24},{24,28},{28,20},{20,12},{12,4},{4,0},{1,9},{9... | collective-permute-start | bytes 3145736 | tf_op jit(solution)/shard_map/ppermute | solution.py:501
  564.0 40.8 %collective-permute-start.101 = (bf16[256,2048]{1,0:T(8,128)(2,1)}, bf16[256,2048]{1,0:T(8,128)(2,1)}, u32[]{:S(2)}, u32[]{:S(2)}) collective-permute-start(bf16[256,2048]{1,0:T(8,128)(2,1)} %collective-permute-done.88), channel_id=1, source_target_pairs={{0,4},{8,0},{16,8},{24,16},{28,24},{20,28},{12,20},{4,12},{1,5},{9... | collective-permute-start | bytes 3145736 | tf_op jit(solution)/shard_map/ppermute | solution.py:501
  570.0 19.3 %collective-permute-start.95 = (f32[4,512]{1,0:T(4,128)S(1)}, f32[4,512]{1,0:T(4,128)S(1)}, u32[]{:S(2)}, u32[]{:S(2)}) collective-permute-start(f32[4,512]{1,0:T(4,128)S(1)} %add.723), channel_id=1, source_target_pairs={{0,2},{1,3},{2,0},{3,1},{4,6},{5,7},{6,4},{7,5},{8,10},{9,11},{10,... | collective-permute-start | bytes 24584 | tf_op jit(solution)/shard_map/ppermute | solution.py:944
  594.6 52.9 %collective-permute-start.98 = (bf16[544,256]{1,0:T(8,128)(2,1)S(1)}, bf16[544,256]{1,0:T(8,128)(2,1)S(1)}, u32[]{:S(2)}, u32[]{:S(2)}) collective-permute-start(bf16[544,256]{1,0:T(8,128)(2,1)S(1)} %constant_dynamic-update-slice_fusion.18), channel_id=1, source_target_pairs={{0,8},{8,16},{16,24},{24,28},{28,20},{20,12},{12,4},{4,0},{1,9},{9... | collective-permute-start | bytes 835592 | tf_op jit(solution)/shard_map/ppermute | solution.py:501
  607.1 26.4 %collective-permute-start.104 = (bf16[256,2048]{1,0:T(8,128)(2,1)}, bf16[256,2048]{1,0:T(8,128)(2,1)S(1)}, u32[]{:S(2)}, u32[]{:S(2)}) collective-permute-start(bf16[256,2048]{1,0:T(8,128)(2,1)} %collective-permute-done.96), channel_id=1, source_target_pairs={{0,8},{8,16},{16,24},{24,28},{28,20},{20,12},{12,4},{4,0},{1,9},{9... | collective-permute-start | bytes 3145736 | tf_op jit(solution)/shard_map/ppermute | solution.py:501
  608.3 26.3 %collective-permute-start.105 = (bf16[256,2048]{1,0:T(8,128)(2,1)}, bf16[256,2048]{1,0:T(8,128)(2,1)S(1)}, u32[]{:S(2)}, u32[]{:S(2)}) collective-permute-start(bf16[256,2048]{1,0:T(8,128)(2,1)} %collective-permute-done.97), channel_id=1, source_target_pairs={{0,4},{8,0},{16,8},{24,16},{28,24},{20,28},{12,20},{4,12},{1,5},{9... | collective-permute-start | bytes 3145736 | tf_op jit(solution)/shard_map/ppermute | solution.py:501
  611.9 32.7 %collective-permute-start.102 = (bf16[128,2048]{1,0:T(8,128)(2,1)S(1)}, bf16[128,2048]{1,0:T(8,128)(2,1)S(1)}, u32[]{:S(2)}, u32[]{:S(2)}) collective-permute-start(bf16[128,2048]{1,0:T(8,128)(2,1)S(1)} %slice.315), channel_id=1, source_target_pairs={{0,8},{8,16},{16,24},{24,28},{28,20},{20,12},{12,4},{4,0},{1,9},{9... | collective-permute-start | bytes 1572872 | tf_op jit(solution)/shard_map/ppermute | solution.py:501
  613.1 32.7 %collective-permute-start.103 = (bf16[128,2048]{1,0:T(8,128)(2,1)S(1)}, bf16[128,2048]{1,0:T(8,128)(2,1)S(1)}, u32[]{:S(2)}, u32[]{:S(2)}) collective-permute-start(bf16[128,2048]{1,0:T(8,128)(2,1)S(1)} %slice.316), channel_id=1, source_target_pairs={{0,4},{8,0},{16,8},{24,16},{28,24},{20,28},{12,20},{4,12},{1,5},{9... | collective-permute-start | bytes 1572872 | tf_op jit(solution)/shard_map/ppermute | solution.py:501
  634.6 38.8 %collective-permute-start.108 = (bf16[256,2048]{1,0:T(8,128)(2,1)S(1)}, bf16[256,2048]{1,0:T(8,128)(2,1)S(1)}, u32[]{:S(2)}, u32[]{:S(2)}) collective-permute-start(bf16[256,2048]{1,0:T(8,128)(2,1)S(1)} %collective-permute-done.104), channel_id=1, source_target_pairs={{0,8},{8,16},{16,24},{24,28},{28,20},{20,12},{12,4},{4,0},{1,9},{9... | collective-permute-start | bytes 3145736 | tf_op jit(solution)/shard_map/ppermute | solution.py:501
  634.9 38.5 %collective-permute-start.109 = (bf16[256,2048]{1,0:T(8,128)(2,1)S(1)}, bf16[256,2048]{1,0:T(8,128)(2,1)S(1)}, u32[]{:S(2)}, u32[]{:S(2)}) collective-permute-start(bf16[256,2048]{1,0:T(8,128)(2,1)S(1)} %collective-permute-done.105), channel_id=1, source_target_pairs={{0,4},{8,0},{16,8},{24,16},{28,24},{20,28},{12,20},{4,12},{1,5},{9... | collective-permute-start | bytes 3145736 | tf_op jit(solution)/shard_map/ppermute | solution.py:501
  644.7 26.7 %collective-permute-start.99 = (bf16[544,256]{1,0:T(8,128)(2,1)S(1)}, bf16[544,256]{1,0:T(8,128)(2,1)S(1)}, u32[]{:S(2)}, u32[]{:S(2)}) collective-permute-start(bf16[544,256]{1,0:T(8,128)(2,1)S(1)} %constant_dynamic-update-slice_fusion.18), channel_id=1, source_target_pairs={{0,4},{8,0},{16,8},{24,16},{28,24},{20,28},{12,20},{4,12},{1,5},{9... | collective-permute-start | bytes 835592 | tf_op jit(solution)/shard_map/ppermute | solution.py:501
  675.1 25.1 %collective-permute-start.114 = (bf16[128,2048]{1,0:T(8,128)(2,1)S(1)}, bf16[128,2048]{1,0:T(8,128)(2,1)S(1)}, u32[]{:S(2)}, u32[]{:S(2)}) collective-permute-start(bf16[128,2048]{1,0:T(8,128)(2,1)S(1)} %slice.319), channel_id=1, source_target_pairs={{0,8},{8,16},{16,24},{24,28},{28,20},{20,12},{12,4},{4,0},{1,9},{9... | collective-permute-start | bytes 1572872 | tf_op jit(solution)/shard_map/ppermute | solution.py:501
  675.4 26.3 %collective-permute-start.115 = (bf16[128,2048]{1,0:T(8,128)(2,1)S(1)}, bf16[128,2048]{1,0:T(8,128)(2,1)S(1)}, u32[]{:S(2)}, u32[]{:S(2)}) collective-permute-start(bf16[128,2048]{1,0:T(8,128)(2,1)S(1)} %slice.320), channel_id=1, source_target_pairs={{0,4},{8,0},{16,8},{24,16},{28,24},{20,28},{12,20},{4,12},{1,5},{9... | collective-permute-start | bytes 1572872 | tf_op jit(solution)/shard_map/ppermute | solution.py:501
  681.1 16.9 %collective-permute-start.110 = (bf16[544,256]{1,0:T(8,128)(2,1)S(1)}, bf16[544,256]{1,0:T(8,128)(2,1)S(1)}, u32[]{:S(2)}, u32[]{:S(2)}) collective-permute-start(bf16[544,256]{1,0:T(8,128)(2,1)S(1)} %collective-permute-done.106), channel_id=1, source_target_pairs={{0,8},{8,16},{16,24},{24,28},{28,20},{20,12},{12,4},{4,0},{1,9},{9... | collective-permute-start | bytes 835592 | tf_op jit(solution)/shard_map/ppermute | solution.py:501
  681.5 18.0 %collective-permute-start.111 = (bf16[544,256]{1,0:T(8,128)(2,1)S(1)}, bf16[544,256]{1,0:T(8,128)(2,1)S(1)}, u32[]{:S(2)}, u32[]{:S(2)}) collective-permute-start(bf16[544,256]{1,0:T(8,128)(2,1)S(1)} %collective-permute-done.107), channel_id=1, source_target_pairs={{0,4},{8,0},{16,8},{24,16},{28,24},{20,28},{12,20},{4,12},{1,5},{9... | collective-permute-start | bytes 835592 | tf_op jit(solution)/shard_map/ppermute | solution.py:501
  684.4 26.0 %collective-permute-start.118 = (bf16[256,1024]{1,0:T(8,128)(2,1)S(1)}, bf16[256,1024]{1,0:T(8,128)(2,1)S(1)}, u32[]{:S(2)}, u32[]{:S(2)}) collective-permute-start(bf16[256,1024]{1,0:T(8,128)(2,1)S(1)} %pad_maximum_fusion.28), channel_id=1, source_target_pairs={{0,8},{8,16},{16,24},{24,28},{28,20},{20,12},{12,4},{4,0},{1,9},{9... | collective-permute-start | bytes 1572872 | tf_op jit(solution)/shard_map/ppermute | solution.py:501
  732.4 19.8 %collective-permute-start.132 = (bf16[512,256]{1,0:T(8,128)(2,1)}, bf16[512,256]{1,0:T(8,128)(2,1)S(1)}, u32[]{:S(2)}, u32[]{:S(2)}) collective-permute-start(bf16[512,256]{1,0:T(8,128)(2,1)} %slice.433), channel_id=1, source_target_pairs={{0,2},{1,3},{2,0},{3,1},{4,6},{5,7},{6,4},{7,5},{8,10},{9,11},{10,... | collective-permute-start | bytes 786440 | tf_op jit(solution)/shard_map/ppermute | solution.py:382
  733.4 33.4 %collective-permute-start.134 = (bf16[512,256]{1,0:T(8,128)(2,1)}, bf16[512,256]{1,0:T(8,128)(2,1)}, u32[]{:S(2)}, u32[]{:S(2)}) collective-permute-start(bf16[512,256]{1,0:T(8,128)(2,1)} %slice.433), channel_id=1, source_target_pairs={{0,1},{1,0},{2,3},{3,2},{4,5},{5,4},{6,7},{7,6},{8,9},{9,8},{10,11... | collective-permute-start | bytes 786440 | tf_op jit(solution)/shard_map/ppermute | solution.py:387
  (215 other events, 1993.4 us)
Sparse Core Ops, SparseCore 0:
  41.5 62.2 all-gather.1

commit v3 on v2

--- a/solution.py
+++ b/solution.py
@@ -985,17 +985,14 @@
     packed = clock(pack, grad_kv, small)
     big.pop(0).turn()
     big.pop(0).turn()
+    while not (ring_s.done() and ring_e.done()):
+        big.pop(0).turn()
+    ring_m = RingSum(clock, grad_pair, jnp.zeros(grad_pair.shape, BF16), put_rows)
     ring_g = RingGather(clock, packed)
     every_packed = {0: packed}
     while ring_g.step < ring_g.reach:
-        big.pop(0).turn()
+        ring_m.turn()
         every_packed.update(ring_g.turn())
-    while not ring_s.done():
-        ring_s.turn()
-        ring_e.turn()
-    ring_m = RingSum(clock, grad_pair, jnp.zeros(grad_pair.shape, BF16), put_rows)
-    ring_e.turn()
-    ring_m.turn()
     place = ring_table()[2]
 
     def total_of(blocks):
@@ -1006,8 +1003,7 @@
 
     packed_sum = clock(total_of, every_packed)
     kv_near = tp_near(packed_sum[: kv_shape[0]].astype(BF16))
-    while not (ring_m.done() and ring_e.done()):
-        ring_e.turn()
+    while not ring_m.done():
         ring_m.turn()
     grad_w_query, grad_w_output = clock(split_pair, ring_m.outs)
     kv_blocks = tp_ordered(tp_cross(kv_near))

time: 800 us -> 810 us (1.012); the launches traced: 802 us -> 801 us
  starting transfers between devices: 146 us -> 156 us
    ppermute x80, waiting for transfers between devices: 180 us -> 167 us  [send(): lax.ppermute(block, 'ctx', ring_shift(self.order, way))]
    ppermute x12, waiting for transfers between devices: 38.1 us -> 49.9 us  [tp_near(): lax.ppermute(values, 'tp', tp_pairs(size, k, 0))]
    ppermute x80, starting transfers between devices: 118 us -> 127 us  [send(): lax.ppermute(block, 'ctx', ring_shift(self.order, way))]
    unnamed x316 -> x304, local copies, waits for them, and re-layouts: 24.1 us -> 22.5 us
  transfers between devices with their start and end apart: 136 -> 136, of which waited for: 64 -> 61; matrix products, arithmetic and copies ran while one was open for 33% -> 32% of each run, Pallas kernels for 9% -> 9%
where the time goes in v3:
time: 810 us; the launch traced here: 801 us
  waiting for transfers between devices  238 us (29%)
  starting transfers between devices  156 us (19%)
  other arithmetic  144 us (18%)
  matrix products  88.5 us (11%)
  Pallas kernels  81.5 us (10%)
  local copies, waits for them, and re-layouts  62.4 us (8%)
  between operations  30.3 us (4%)
    ppermute x80, waiting for transfers between devices, send(): lax.ppermute(block, 'ctx', ring_shift(self.order, way))  167 us
    ppermute x80, starting transfers between devices, send(): lax.ppermute(block, 'ctx', ring_shift(self.order, way))  127 us
    dot_general x10, matrix products, dot_nn(): lax.dot_general(left, right, (((1,), (0,)), ((), ())), preferred_element_...  57.1 us
    ppermute x12, waiting for transfers between devices, tp_near(): lax.ppermute(values, 'tp', tp_pairs(size, k, 0))  49.9 us
    dynamic_update_slice x14, other arithmetic, put_rows(): lax.dynamic_update_slice(target, block, (index * jnp.uint32(block.shape[0...  35.6 us
    dot_general x9, matrix products, dot_nt(): lax.dot_general(left, right, (((1,), (1,)), ((), ())), preferred_element_...  31.4 us
    convert_element_type x15, other arithmetic, added(): return total.astype(BF16)  25.2 us
    pallas_call x3, Pallas kernels, weight_grad(): pl.pallas_call(functools.partial(grad_kernel, count), grid=(m // bm,), in...  24.7 us
  transfers between devices with their start and end apart: 136, of which 61 were waited for; matrix products, arithmetic and copies ran while one was open for 32% of the time, Pallas kernels for 9%

profile of v3, /device:TPU:0, one launch (start us, length us, event | category | flops | bytes accessed | tf_op | source)
XLA Modules:
  0.0 800.6 jit_solution(9351075344673063778)
XLA Ops:
  8.7 3.0 collective-permute-start.1
  15.8 8.0 %collective-permute-done.3 = bf16[5,512]{1,0:T(8,128)(2,1)S(1)} collective-permute-done((bf16[5,512]{1,0:T(8,128)(2,1)S(1)}, bf16[5,512]{1,0:T(8,128)(2,1)S(1)}, u32[]{:S(2)}, u32[]{:S(2)}) %collective-permute-start.3) | collective-permute-done | bytes 5152 | tf_op jit(solution)/shard_map/ppermute | solution.py:382
  82.9 5.1 shard_map.350
  91.5 5.3 shard_map.351
  98.8 11.0 %collective-permute-done.24 = bf16[512,512]{1,0:T(8,128)(2,1)} collective-permute-done((bf16[512,512]{1,0:T(8,128)(2,1)S(1)}, bf16[512,512]{1,0:T(8,128)(2,1)}, u32[]{:S(2)}, u32[]{:S(2)}) %collective-permute-start.24) | collective-permute-done | bytes 524320 | tf_op jit(solution)/shard_map/ppermute | solution.py:382
  112.8 3.0 broadcast_select_fusion.63
  115.8 9.2 %fusion.65 = (f32[512]{0:T(512)S(1)}, f32[512,2048]{1,0:T(8,128)S(1)}) fusion(f32[2048]{0:T(1024)S(1)} %bitcast.219, bf16[2048,2048]{1,0:T(8,128)(2,1)} %all-gather.2.cloned.1.call-done, bf16[512,512]{1,0:T(8,128)(2,1)} %get-tuple-element.802, bf16[512,512]{1,0:T(8,128)(2,1)} %get-tuple-element.803, bf16[512,512]{1,0:T(8,128)(2,1)} %get-tuple-element.804, ...), kind=kOutput, calls=%fused_computation.471 | convolution fusion | flops 4314889728 | bytes 16787456 | tf_op jit(solution)/shard_map/dot_general | solution.py:22
  126.5 13.3 %add_convert_fusion.4 = (bf16[512,2048]{1,0:T(8,128)(2,1)}, bf16[512,2048]{1,0:T(8,128)(2,1)S(1)}) fusion(f32[2048]{0:T(1024)S(1)} %convert_element_type.749, bf16[512,2048]{1,0:T(8,128)(2,1)S(1)} %add_convert_fusion.5.refs_0_, bf16[2048,2048]{1,0:T(8,128)(2,1)} %w), kind=kOutput, calls=%fused_computation.19 | convolution fusion | flops 4315938816 | bytes 14688256 | tf_op jit(solution)/shard_map/dot_general | solution.py:22
  140.4 5.2 convolution_convert_fusion.4
  147.9 8.2 %fusion.66 = (f32[512]{0:T(512)S(1)}, f32[512,2048]{1,0:T(8,128)S(1)}) fusion(f32[2048]{0:T(1024)S(1)} %bitcast.220, bf16[2048,2048]{1,0:T(8,128)(2,1)} %all-gather.2.cloned.1.call-done, bf16[512,512]{1,0:T(8,128)(2,1)S(1)} %get-tuple-element.798, bf16[512,512]{1,0:T(8,128)(2,1)S(1)} %get-tuple-element.799, bf16[512,512]{1,0:T(8,128)(2,1)S(1)} %get-tuple-element.800, ...), kind=kOutput, calls=%fused_computation.472 | convolution fusion | flops 4314889728 | bytes 16787456 | tf_op jit(solution)/shard_map/dot_general | solution.py:22
  159.0 8.1 %add_convert_fusion.2 = (bf16[512,2048]{1,0:T(8,128)(2,1)}, bf16[512,2048]{1,0:T(8,128)(2,1)S(1)}) fusion(f32[2048]{0:T(1024)S(1)} %copy-done.119, bf16[512,2048]{1,0:T(8,128)(2,1)S(1)} %add_convert_fusion.3.refs_1_, bf16[2048,2048]{1,0:T(8,128)(2,1)S(1)} %bitcast.182), kind=kOutput, calls=%fused_computation.13 | convolution fusion | flops 4315938816 | bytes 14688256 | tf_op jit(solution)/shard_map/dot_general | solution.py:22
  167.1 5.2 collective-permute-done.34
  175.6 8.3 %convolution_convert_fusion.3 = bf16[512,2048]{1,0:T(8,128)(2,1)S(1)} fusion(bf16[512,2048]{1,0:T(8,128)(2,1)S(1)} %get-tuple-element.453.refs_1_, bf16[2048,2048]{1,0:T(8,128)(2,1)} %param.35), kind=kOutput, calls=%fused_computation.36 | convolution fusion | flops 4296015872 | bytes 12582912 | tf_op jit(solution)/shard_map/dot_general | solution.py:22
  185.4 13.3 %collective-permute-done.37 = bf16[512,512]{1,0:T(8,128)(2,1)S(1)} collective-permute-done((bf16[512,512]{1,0:T(8,128)(2,1)S(1)}, bf16[512,512]{1,0:T(8,128)(2,1)S(1)}, u32[]{:S(2)}, u32[]{:S(2)}) %collective-permute-start.37) | collective-permute-done | bytes 524320 | tf_op jit(solution)/shard_map/ppermute | solution.py:382
  203.9 9.1 %convert_reduce_fusion.2 = (f32[2048]{0:T(1024)}, bf16[512,2048]{1,0:T(8,128)(2,1)S(1)}) fusion(bf16[512,2048]{1,0:T(8,128)(2,1)} %get-tuple-element.737, bf16[512,2048]{1,0:T(8,128)(2,1)S(1)} %pad_maximum_fusion.4.refs_2_, bf16[2048,2048]{1,0:T(8,128)(2,1)} %param.35), kind=kOutput, calls=%fused_computation.2 | convolution fusion | flops 4300208128 | bytes 14688256 | tf_op jit(solution)/shard_map/dot_general | solution.py:26
  213.0 4.2 collective-permute-done.36
  217.2 2.8 convert_reduce_fusion.5
  221.9 5.3 shard_map.352
  251.6 11.9 %shard_map.353 = bf16[2048,2048]{1,0:T(8,128)(2,1)} custom-call(bf16[512,2048]{1,0:T(8,128)(2,1)S(1)} %copy-done.33, bf16[512,2048]{1,0:T(8,128)(2,1)S(1)} %copy-done.35, bf16[512,2048]{1,0:T(8,128)(2,1)S(1)} %copy-done.14, bf16[512,2048]{1,0:T(8,128)(2,1)S(1)} %pad_maximum_fusion.5.refs_3_), custom_call_target="tpu_custom_call" | custom-call | flops 8589934592 | bytes 16777216 | tf_op jit(solution)/shard_map/pallas_call | solution.py:218
  263.5 3.1 constant_dynamic-slice_fusion.4
  269.8 8.8 %convert_reduce_fusion.1 = (f32[2048]{0:T(1024)S(1)}, bf16[512,2048]{1,0:T(8,128)(2,1)S(1)}) fusion(bf16[512,2048]{1,0:T(8,128)(2,1)} %get-tuple-element.735, bf16[512,2048]{1,0:T(8,128)(2,1)S(1)} %pad_maximum_fusion.5.refs_3_, bf16[2048,2048]{1,0:T(8,128)(2,1)} %param.35), kind=kOutput, calls=%fused_computation.1 | convolution fusion | flops 4300208128 | bytes 14688256 | tf_op jit(solution)/shard_map/dot_general | solution.py:26
  278.7 4.8 convolution_convert_fusion.2
  289.8 8.3 %collective-permute-start.51 = (bf16[256,2048]{1,0:T(8,128)(2,1)S(1)}, bf16[256,2048]{1,0:T(8,128)(2,1)S(1)}, u32[]{:S(2)}, u32[]{:S(2)}) collective-permute-start(bf16[256,2048]{1,0:T(8,128)(2,1)S(1)} %pad_maximum_fusion.18), channel_id=1, source_target_pairs={{0,8},{8,16},{16,24},{24,28},{28,20},{20,12},{12,4},{4,0},{1,9},{9... | collective-permute-start | bytes 3145736 | tf_op jit(solution)/shard_map/ppermute | solution.py:501
  302.5 11.9 %shard_map.354 = bf16[2048,2048]{1,0:T(8,128)(2,1)} custom-call(bf16[512,2048]{1,0:T(8,128)(2,1)S(1)} %copy-done.16, bf16[512,2048]{1,0:T(8,128)(2,1)S(1)} %copy-done.18, bf16[512,2048]{1,0:T(8,128)(2,1)S(1)} %copy-done.20, bf16[512,2048]{1,0:T(8,128)(2,1)S(1)} %get-tuple-element.469.refs_3_), custom_call_target="tpu_custom_call" | custom-call | flops 8589934592 | bytes 16777216 | tf_op jit(solution)/shard_map/pallas_call | solution.py:218
  314.4 3.0 constant_dynamic-slice_fusion.2
  317.4 8.2 %collective-permute-start.55 = (bf16[128,2048]{1,0:T(8,128)(2,1)}, bf16[128,2048]{1,0:T(8,128)(2,1)}, u32[]{:S(2)}, u32[]{:S(2)}) collective-permute-start(bf16[128,2048]{1,0:T(8,128)(2,1)} %get-tuple-element.718), channel_id=1, source_target_pairs={{0,8},{8,16},{16,24},{24,28},{28,20},{20,12},{12,4},{4,0},{1,9},{9... | collective-permute-start | bytes 1572872 | tf_op jit(solution)/shard_map/ppermute | solution.py:501
  334.1 3.7 add_convert_fusion.21
  340.4 12.1 %shard_map.355 = (bf16[512,512]{1,0:T(8,128)(2,1)}, bf16[4096,256]{1,0:T(8,128)(2,1)}) custom-call(s32[10]{0:T(128)} %copy-done.29, bf16[512,512]{1,0:T(8,128)(2,1)} %copy-done.31, bf16[512,512]{1,0:T(8,128)(2,1)} %convolution_convert_fusion.6.do_ref, f32[512,512]{1,0:T(8,128)} %copy-done.38, f32[512,512]{1,0:T(8,128)} %copy-done.39, ...), custom_call_target="tpu_custom_call" | custom-call | flops 12884901888 | bytes 8388608 | tf_op jit(solution)/shard_map/pallas_call | solution.py:182
  357.1 8.4 %collective-permute-done.59 = bf16[512,512]{1,0:T(8,128)(2,1)S(1)} collective-permute-done((bf16[512,512]{1,0:T(8,128)(2,1)S(1)}, bf16[512,512]{1,0:T(8,128)(2,1)S(1)}, u32[]{:S(2)}, u32[]{:S(2)}) %collective-permute-start.59) | collective-permute-done | bytes 524320 | tf_op jit(solution)/shard_map/ppermute | solution.py:382
  367.5 8.0 collective-permute-start.57
  381.6 4.4 add_convert_fusion.19
  385.9 7.7 collective-permute-start.68
  393.8 11.7 %shard_map.356 = (bf16[512,512]{1,0:T(8,128)(2,1)}, bf16[4096,256]{1,0:T(8,128)(2,1)}) custom-call(s32[10]{0:T(128)} %copy-done.28, bf16[512,512]{1,0:T(8,128)(2,1)} %fusion.17.q_ref, bf16[512,512]{1,0:T(8,128)(2,1)} %convolution_convert_fusion.5.do_ref, f32[512,512]{1,0:T(8,128)} %copy-done.36, f32[512,512]{1,0:T(8,128)} %copy-done.37, ...), custom_call_target="tpu_custom_call" | custom-call | flops 12884901888 | bytes 8388608 | tf_op jit(solution)/shard_map/pallas_call | solution.py:182
  407.4 4.4 add_convert_fusion.17
  411.8 7.7 collective-permute-start.66
  424.1 2.8 add_convert_fusion.14.block_ref
  426.9 7.8 collective-permute-start.72
  446.9 8.0 shard_map.358
  454.9 3.2 add_convert_fusion.12
  459.6 5.1 collective-permute-start.70
  467.8 5.5 collective-permute-done.73
  480.2 5.9 collective-permute-start.74
  515.2 6.7 collective-permute-done.91
  525.5 4.6 collective-permute-done.89
  539.3 12.0 %collective-permute-done.87 = bf16[256,2048]{1,0:T(8,128)(2,1)} collective-permute-done((bf16[256,2048]{1,0:T(8,128)(2,1)}, bf16[256,2048]{1,0:T(8,128)(2,1)}, u32[]{:S(2)}, u32[]{:S(2)}) %collective-permute-start.87) | collective-permute-done | bytes 1048608 | tf_op jit(solution)/shard_map/ppermute | solution.py:501
  555.4 2.8 convert_dynamic-update-slice_fusion.10
  576.1 12.6 %collective-permute-done.96 = bf16[256,2048]{1,0:T(8,128)(2,1)} collective-permute-done((bf16[256,2048]{1,0:T(8,128)(2,1)}, bf16[256,2048]{1,0:T(8,128)(2,1)}, u32[]{:S(2)}, u32[]{:S(2)}) %collective-permute-start.96) | collective-permute-done | bytes 1048608 | tf_op jit(solution)/shard_map/ppermute | solution.py:501
  593.3 2.9 convert_dynamic-update-slice_fusion.8
  606.2 4.9 collective-permute-done.127
  622.9 7.2 collective-permute-done.105
  632.6 24.1 %collective-permute-done.102 = bf16[544,256]{1,0:T(8,128)(2,1)S(1)} collective-permute-done((bf16[544,256]{1,0:T(8,128)(2,1)S(1)}, bf16[544,256]{1,0:T(8,128)(2,1)S(1)}, u32[]{:S(2)}, u32[]{:S(2)}) %collective-permute-start.102) | collective-permute-done | bytes 278560 | tf_op jit(solution)/shard_map/ppermute | solution.py:501
  661.5 6.4 collective-permute-done.108
  684.4 3.5 collective-permute-done.131
  692.5 6.6 collective-permute-done.112
  709.3 4.9 collective-permute-done.122
  714.2 18.7 %collective-permute-done.114 = bf16[256,1024]{1,0:T(8,128)(2,1)} collective-permute-done((bf16[256,1024]{1,0:T(8,128)(2,1)}, bf16[256,1024]{1,0:T(8,128)(2,1)}, u32[]{:S(2)}, u32[]{:S(2)}) %collective-permute-start.114) | collective-permute-done | bytes 524320 | tf_op jit(solution)/shard_map/ppermute | solution.py:501
  747.1 2.9 convert_dynamic-update-slice_fusion.2
  752.0 5.1 collective-permute-done.117
  760.8 4.0 collective-permute-done.133
  764.8 3.6 collective-permute-done.134
  768.4 6.5 collective-permute-done.118
  775.0 3.9 collective-permute-done.119
  782.7 3.9 collective-permute-done.120
  787.8 4.6 shard_map.361
  (788 shorter events, 324.2 us)
Async XLA Ops:
  7.2 108.6 %all-gather.2.cloned.1.call-start = ((), (), s32[]{:S(2)}) async-start(), calls=%async_computation | async-start | bytes 10485760 | tf_op jit(solution)/shard_map/all_gather | solution.py:739
  8.7 15.2 %collective-permute-start.1 = (bf16[512,512]{1,0:T(8,128)(2,1)S(1)}, bf16[512,512]{1,0:T(8,128)(2,1)}, u32[]{:S(2)}, u32[]{:S(2)}) collective-permute-start(bf16[512,512]{1,0:T(8,128)(2,1)S(1)} %get-tuple-element.355), channel_id=1, source_target_pairs={{0,2},{1,3},{2,0},{3,1},{4,6},{5,7},{6,4},{7,5},{8,10},{9,11},{10,... | collective-permute-start | bytes 1572872 | tf_op jit(solution)/shard_map/ppermute | solution.py:382
  88.4 21.4 %collective-permute-start.24 = (bf16[512,512]{1,0:T(8,128)(2,1)S(1)}, bf16[512,512]{1,0:T(8,128)(2,1)}, u32[]{:S(2)}, u32[]{:S(2)}) collective-permute-start(bf16[512,512]{1,0:T(8,128)(2,1)S(1)} %get-tuple-element.511.refs_6_), channel_id=1, source_target_pairs={{0,2},{1,3},{2,0},{3,1},{4,6},{5,7},{6,4},{7,5},{8,10},{9,11},{10,... | collective-permute-start | bytes 1572872 | tf_op jit(solution)/shard_map/ppermute | solution.py:382
  111.7 28.2 %collective-permute-start.31 = (bf16[512,512]{1,0:T(8,128)(2,1)S(1)}, bf16[512,512]{1,0:T(8,128)(2,1)}, u32[]{:S(2)}, u32[]{:S(2)}) collective-permute-start(bf16[512,512]{1,0:T(8,128)(2,1)S(1)} %get-tuple-element.512.refs_7_), channel_id=1, source_target_pairs={{0,2},{1,3},{2,0},{3,1},{4,6},{5,7},{6,4},{7,5},{8,10},{9,11},{10,... | collective-permute-start | bytes 1572872 | tf_op jit(solution)/shard_map/ppermute | solution.py:382
  229.6 16.9 %collective-permute-start.40 = (bf16[512,1024]{1,0:T(8,128)(2,1)}, bf16[512,1024]{1,0:T(8,128)(2,1)}, u32[]{:S(2)}, u32[]{:S(2)}) collective-permute-start(bf16[512,1024]{1,0:T(8,128)(2,1)} %pad_maximum_fusion.15), channel_id=1, source_target_pairs={{0,1},{1,0},{2,3},{3,2},{4,5},{5,4},{6,7},{7,6},{8,9},{9,8},{10,11... | collective-permute-start | bytes 3145736 | tf_op jit(solution)/shard_map/ppermute | solution.py:423
  250.3 18.3 %collective-permute-start.41 = (bf16[512,512]{1,0:T(8,128)(2,1)S(1)}, bf16[512,512]{1,0:T(8,128)(2,1)S(1)}, u32[]{:S(2)}, u32[]{:S(2)}) collective-permute-start(bf16[512,512]{1,0:T(8,128)(2,1)S(1)} %constant_dynamic-slice_fusion.33), channel_id=1, source_target_pairs={{0,2},{1,3},{2,0},{3,1},{4,6},{5,7},{6,4},{7,5},{8,10},{9,11},{10,... | collective-permute-start | bytes 1572872 | tf_op jit(solution)/shard_map/ppermute | solution.py:431
  266.5 17.2 %collective-permute-start.47 = (bf16[128,2048]{1,0:T(8,128)(2,1)}, bf16[128,2048]{1,0:T(8,128)(2,1)}, u32[]{:S(2)}, u32[]{:S(2)}) collective-permute-start(bf16[128,2048]{1,0:T(8,128)(2,1)} %get-tuple-element.726), channel_id=1, source_target_pairs={{0,8},{8,16},{16,24},{24,28},{28,20},{20,12},{12,4},{4,0},{1,9},{9... | collective-permute-start | bytes 1572872 | tf_op jit(solution)/shard_map/ppermute | solution.py:501
  268.0 18.2 %collective-permute-start.48 = (bf16[128,2048]{1,0:T(8,128)(2,1)}, bf16[128,2048]{1,0:T(8,128)(2,1)}, u32[]{:S(2)}, u32[]{:S(2)}) collective-permute-start(bf16[128,2048]{1,0:T(8,128)(2,1)} %get-tuple-element.728), channel_id=1, source_target_pairs={{0,4},{8,0},{16,8},{24,16},{28,24},{20,28},{12,20},{4,12},{1,5},{9... | collective-permute-start | bytes 1572872 | tf_op jit(solution)/shard_map/ppermute | solution.py:501
  289.6 44.5 %collective-permute-start.52 = (bf16[256,2048]{1,0:T(8,128)(2,1)S(1)}, bf16[256,2048]{1,0:T(8,128)(2,1)S(1)}, u32[]{:S(2)}, u32[]{:S(2)}) collective-permute-start(bf16[256,2048]{1,0:T(8,128)(2,1)S(1)} %pad_maximum_fusion.19), channel_id=1, source_target_pairs={{0,4},{8,0},{16,8},{24,16},{28,24},{20,28},{12,20},{4,12},{1,5},{9... | collective-permute-start | bytes 3145736 | tf_op jit(solution)/shard_map/ppermute | solution.py:501
  289.8 44.3 %collective-permute-start.51 = (bf16[256,2048]{1,0:T(8,128)(2,1)S(1)}, bf16[256,2048]{1,0:T(8,128)(2,1)S(1)}, u32[]{:S(2)}, u32[]{:S(2)}) collective-permute-start(bf16[256,2048]{1,0:T(8,128)(2,1)S(1)} %pad_maximum_fusion.18), channel_id=1, source_target_pairs={{0,8},{8,16},{16,24},{24,28},{28,20},{20,12},{12,4},{4,0},{1,9},{9... | collective-permute-start | bytes 3145736 | tf_op jit(solution)/shard_map/ppermute | solution.py:501
  300.9 16.5 %collective-permute-start.49 = (bf16[512,512]{1,0:T(8,128)(2,1)S(1)}, bf16[512,512]{1,0:T(8,128)(2,1)S(1)}, u32[]{:S(2)}, u32[]{:S(2)}) collective-permute-start(bf16[512,512]{1,0:T(8,128)(2,1)S(1)} %get-tuple-element.472), channel_id=1, source_target_pairs={{0,1},{1,0},{2,3},{3,2},{4,5},{5,4},{6,7},{7,6},{8,9},{9,8},{10,11... | collective-permute-start | bytes 1572872 | tf_op jit(solution)/shard_map/ppermute | solution.py:387
  300.9 24.7 %collective-permute-start.50 = (bf16[512,512]{1,0:T(8,128)(2,1)}, bf16[512,512]{1,0:T(8,128)(2,1)S(1)}, u32[]{:S(2)}, u32[]{:S(2)}) collective-permute-start(bf16[512,512]{1,0:T(8,128)(2,1)} %collective-permute-done.45), channel_id=1, source_target_pairs={{0,1},{1,0},{2,3},{3,2},{4,5},{5,4},{6,7},{7,6},{8,9},{9,8},{10,11... | collective-permute-start | bytes 1572872 | tf_op jit(solution)/shard_map/ppermute | solution.py:387
  301.4 31.5 %collective-permute-start.53 = (bf16[512,512]{1,0:T(8,128)(2,1)S(1)}, bf16[512,512]{1,0:T(8,128)(2,1)S(1)}, u32[]{:S(2)}, u32[]{:S(2)}) collective-permute-start(bf16[512,512]{1,0:T(8,128)(2,1)S(1)} %constant_dynamic-slice_fusion.25), channel_id=1, source_target_pairs={{0,2},{1,3},{2,0},{3,1},{4,6},{5,7},{6,4},{7,5},{8,10},{9,11},{10,... | collective-permute-start | bytes 1572872 | tf_op jit(solution)/shard_map/ppermute | solution.py:431
  317.4 35.1 %collective-permute-start.55 = (bf16[128,2048]{1,0:T(8,128)(2,1)}, bf16[128,2048]{1,0:T(8,128)(2,1)}, u32[]{:S(2)}, u32[]{:S(2)}) collective-permute-start(bf16[128,2048]{1,0:T(8,128)(2,1)} %get-tuple-element.718), channel_id=1, source_target_pairs={{0,8},{8,16},{16,24},{24,28},{28,20},{20,12},{12,4},{4,0},{1,9},{9... | collective-permute-start | bytes 1572872 | tf_op jit(solution)/shard_map/ppermute | solution.py:501
  325.6 26.9 %collective-permute-start.56 = (bf16[128,2048]{1,0:T(8,128)(2,1)}, bf16[128,2048]{1,0:T(8,128)(2,1)}, u32[]{:S(2)}, u32[]{:S(2)}) collective-permute-start(bf16[128,2048]{1,0:T(8,128)(2,1)} %get-tuple-element.720), channel_id=1, source_target_pairs={{0,4},{8,0},{16,8},{24,16},{28,24},{20,28},{12,20},{4,12},{1,5},{9... | collective-permute-start | bytes 1572872 | tf_op jit(solution)/shard_map/ppermute | solution.py:501
  337.8 43.7 %collective-permute-start.62 = (bf16[256,2048]{1,0:T(8,128)(2,1)}, bf16[256,2048]{1,0:T(8,128)(2,1)}, u32[]{:S(2)}, u32[]{:S(2)}) collective-permute-start(bf16[256,2048]{1,0:T(8,128)(2,1)} %get-tuple-element.724), channel_id=1, source_target_pairs={{0,8},{8,16},{16,24},{24,28},{28,20},{20,12},{12,4},{4,0},{1,9},{9... | collective-permute-start | bytes 3145736 | tf_op jit(solution)/shard_map/ppermute | solution.py:501
  340.4 41.2 %collective-permute-start.63 = (bf16[256,2048]{1,0:T(8,128)(2,1)}, bf16[256,2048]{1,0:T(8,128)(2,1)}, u32[]{:S(2)}, u32[]{:S(2)}) collective-permute-start(bf16[256,2048]{1,0:T(8,128)(2,1)} %get-tuple-element.723), channel_id=1, source_target_pairs={{0,4},{8,0},{16,8},{24,16},{28,24},{20,28},{12,20},{4,12},{1,5},{9... | collective-permute-start | bytes 3145736 | tf_op jit(solution)/shard_map/ppermute | solution.py:501
  355.6 49.9 %collective-permute-start.58 = (bf16[256,2048]{1,0:T(8,128)(2,1)S(1)}, bf16[256,2048]{1,0:T(8,128)(2,1)}, u32[]{:S(2)}, u32[]{:S(2)}) collective-permute-start(bf16[256,2048]{1,0:T(8,128)(2,1)S(1)} %pad_maximum_fusion.21), channel_id=1, source_target_pairs={{0,4},{8,0},{16,8},{24,16},{28,24},{20,28},{12,20},{4,12},{1,5},{9... | collective-permute-start | bytes 3145736 | tf_op jit(solution)/shard_map/ppermute | solution.py:501
  367.5 38.0 %collective-permute-start.57 = (bf16[256,2048]{1,0:T(8,128)(2,1)}, bf16[256,2048]{1,0:T(8,128)(2,1)}, u32[]{:S(2)}, u32[]{:S(2)}) collective-permute-start(bf16[256,2048]{1,0:T(8,128)(2,1)} %pad_maximum_fusion.20), channel_id=1, source_target_pairs={{0,8},{8,16},{16,24},{24,28},{28,20},{20,12},{12,4},{4,0},{1,9},{9... | collective-permute-start | bytes 3145736 | tf_op jit(solution)/shard_map/ppermute | solution.py:501
  375.4 44.1 %collective-permute-start.54 = (bf16[4096,128]{1,0:T(8,128)(2,1)}, bf16[4096,128]{1,0:T(8,128)(2,1)}, u32[]{:S(2)}, u32[]{:S(2)}) collective-permute-start(bf16[4096,128]{1,0:T(8,128)(2,1)} %get-tuple-element.763), channel_id=1, source_target_pairs={{0,1},{1,0},{2,3},{3,2},{4,5},{5,4},{6,7},{7,6},{8,9},{9,8},{10,11... | collective-permute-start | bytes 3145736 | tf_op jit(solution)/shard_map/ppermute | solution.py:835
  385.9 35.7 %collective-permute-start.68 = (bf16[256,2048]{1,0:T(8,128)(2,1)}, bf16[256,2048]{1,0:T(8,128)(2,1)S(1)}, u32[]{:S(2)}, u32[]{:S(2)}) collective-permute-start(bf16[256,2048]{1,0:T(8,128)(2,1)} %get-tuple-element.716), channel_id=1, source_target_pairs={{0,8},{8,16},{16,24},{24,28},{28,20},{20,12},{12,4},{4,0},{1,9},{9... | collective-permute-start | bytes 3145736 | tf_op jit(solution)/shard_map/ppermute | solution.py:501
  393.6 28.0 %collective-permute-start.69 = (bf16[256,2048]{1,0:T(8,128)(2,1)}, bf16[256,2048]{1,0:T(8,128)(2,1)S(1)}, u32[]{:S(2)}, u32[]{:S(2)}) collective-permute-start(bf16[256,2048]{1,0:T(8,128)(2,1)} %get-tuple-element.715), channel_id=1, source_target_pairs={{0,4},{8,0},{16,8},{24,16},{28,24},{20,28},{12,20},{4,12},{1,5},{9... | collective-permute-start | bytes 3145736 | tf_op jit(solution)/shard_map/ppermute | solution.py:501
  411.8 43.0 %collective-permute-start.66 = (bf16[256,2048]{1,0:T(8,128)(2,1)}, bf16[256,2048]{1,0:T(8,128)(2,1)}, u32[]{:S(2)}, u32[]{:S(2)}) collective-permute-start(bf16[256,2048]{1,0:T(8,128)(2,1)} %get-tuple-element.714), channel_id=1, source_target_pairs={{0,8},{8,16},{16,24},{24,28},{28,20},{20,12},{12,4},{4,0},{1,9},{9... | collective-permute-start | bytes 3145736 | tf_op jit(solution)/shard_map/ppermute | solution.py:501
  419.6 35.3 %collective-permute-start.67 = (bf16[256,2048]{1,0:T(8,128)(2,1)}, bf16[256,2048]{1,0:T(8,128)(2,1)}, u32[]{:S(2)}, u32[]{:S(2)}) collective-permute-start(bf16[256,2048]{1,0:T(8,128)(2,1)} %get-tuple-element.713), channel_id=1, source_target_pairs={{0,4},{8,0},{16,8},{24,16},{28,24},{20,28},{12,20},{4,12},{1,5},{9... | collective-permute-start | bytes 3145736 | tf_op jit(solution)/shard_map/ppermute | solution.py:501
  423.1 34.9 %collective-permute-start.65 = (bf16[8,512,128]{2,1,0:T(8,128)(2,1)}, bf16[8,512,128]{2,1,0:T(8,128)(2,1)}, u32[]{:S(2)}, u32[]{:S(2)}) collective-permute-start(bf16[8,512,128]{2,1,0:T(8,128)(2,1)} %get-tuple-element.759), channel_id=1, source_target_pairs={{0,2},{1,3},{2,0},{3,1},{4,6},{5,7},{6,4},{7,5},{8,10},{9,11},{10,... | collective-permute-start | bytes 3145736 | tf_op jit(solution)/shard_map/ppermute | solution.py:887
  426.9 40.9 %collective-permute-start.72 = (bf16[256,2048]{1,0:T(8,128)(2,1)}, bf16[256,2048]{1,0:T(8,128)(2,1)}, u32[]{:S(2)}, u32[]{:S(2)}) collective-permute-start(bf16[256,2048]{1,0:T(8,128)(2,1)} %add_convert_fusion.14.block_ref), channel_id=1, source_target_pairs={{0,8},{8,16},{16,24},{24,28},{28,20},{20,12},{12,4},{4,0},{1,9},{9... | collective-permute-start | bytes 3145736 | tf_op jit(solution)/shard_map/ppermute | solution.py:501
  434.7 38.6 %collective-permute-start.73 = (bf16[256,2048]{1,0:T(8,128)(2,1)}, bf16[256,2048]{1,0:T(8,128)(2,1)}, u32[]{:S(2)}, u32[]{:S(2)}) collective-permute-start(bf16[256,2048]{1,0:T(8,128)(2,1)} %add_convert_fusion.14.block_ref), channel_id=1, source_target_pairs={{0,4},{8,0},{16,8},{24,16},{28,24},{20,28},{12,20},{4,12},{1,5},{9... | collective-permute-start | bytes 3145736 | tf_op jit(solution)/shard_map/ppermute | solution.py:501
  459.6 20.5 %collective-permute-start.70 = (bf16[256,128]{1,0:T(8,128)(2,1)S(1)}, bf16[256,128]{1,0:T(8,128)(2,1)S(1)}, u32[]{:S(2)}, u32[]{:S(2)}) collective-permute-start(bf16[256,128]{1,0:T(8,128)(2,1)S(1)} %get-tuple-element.828), channel_id=1, source_target_pairs={{0,8},{8,16},{16,24},{24,28},{28,20},{20,12},{12,4},{4,0},{1,9},{9... | collective-permute-start | bytes 196616 | tf_op jit(solution)/shard_map/ppermute | solution.py:501
  464.7 15.4 %collective-permute-start.71 = (bf16[256,128]{1,0:T(8,128)(2,1)S(1)}, bf16[256,128]{1,0:T(8,128)(2,1)S(1)}, u32[]{:S(2)}, u32[]{:S(2)}) collective-permute-start(bf16[256,128]{1,0:T(8,128)(2,1)S(1)} %get-tuple-element.827), channel_id=1, source_target_pairs={{0,4},{8,0},{16,8},{24,16},{28,24},{20,28},{12,20},{4,12},{1,5},{9... | collective-permute-start | bytes 196616 | tf_op jit(solution)/shard_map/ppermute | solution.py:501
  500.2 21.6 %collective-permute-start.91 = (bf16[512,512]{1,0:T(8,128)(2,1)S(1)}, bf16[512,512]{1,0:T(8,128)(2,1)S(1)}, u32[]{:S(2)}, u32[]{:S(2)}) collective-permute-start(bf16[512,512]{1,0:T(8,128)(2,1)S(1)} %constant_dynamic-slice_fusion.8), channel_id=1, source_target_pairs={{0,2},{1,3},{2,0},{3,1},{4,6},{5,7},{6,4},{7,5},{8,10},{9,11},{10,... | collective-permute-start | bytes 1572872 | tf_op jit(solution)/shard_map/ppermute | solution.py:431
  503.9 26.1 %collective-permute-start.89 = (bf16[256,2048]{1,0:T(8,128)(2,1)S(1)}, bf16[256,2048]{1,0:T(8,128)(2,1)S(1)}, u32[]{:S(2)}, u32[]{:S(2)}) collective-permute-start(bf16[256,2048]{1,0:T(8,128)(2,1)S(1)} %get-tuple-element.547), channel_id=1, source_target_pairs={{0,8},{8,16},{16,24},{24,28},{28,20},{20,12},{12,4},{4,0},{1,9},{9... | collective-permute-start | bytes 3145736 | tf_op jit(solution)/shard_map/ppermute | solution.py:501
  505.7 26.4 %collective-permute-start.90 = (bf16[256,2048]{1,0:T(8,128)(2,1)S(1)}, bf16[256,2048]{1,0:T(8,128)(2,1)S(1)}, u32[]{:S(2)}, u32[]{:S(2)}) collective-permute-start(bf16[256,2048]{1,0:T(8,128)(2,1)S(1)} %get-tuple-element.548), channel_id=1, source_target_pairs={{0,4},{8,0},{16,8},{24,16},{28,24},{20,28},{12,20},{4,12},{1,5},{9... | collective-permute-start | bytes 3145736 | tf_op jit(solution)/shard_map/ppermute | solution.py:501
  508.7 42.6 %collective-permute-start.87 = (bf16[256,2048]{1,0:T(8,128)(2,1)}, bf16[256,2048]{1,0:T(8,128)(2,1)}, u32[]{:S(2)}, u32[]{:S(2)}) collective-permute-start(bf16[256,2048]{1,0:T(8,128)(2,1)} %collective-permute-done.72), channel_id=1, source_target_pairs={{0,8},{8,16},{16,24},{24,28},{28,20},{20,12},{12,4},{4,0},{1,9},{9... | collective-permute-start | bytes 3145736 | tf_op jit(solution)/shard_map/ppermute | solution.py:501
  514.0 37.5 %collective-permute-start.88 = (bf16[256,2048]{1,0:T(8,128)(2,1)}, bf16[256,2048]{1,0:T(8,128)(2,1)}, u32[]{:S(2)}, u32[]{:S(2)}) collective-permute-start(bf16[256,2048]{1,0:T(8,128)(2,1)} %collective-permute-done.73), channel_id=1, source_target_pairs={{0,4},{8,0},{16,8},{24,16},{28,24},{20,28},{12,20},{4,12},{1,5},{9... | collective-permute-start | bytes 3145736 | tf_op jit(solution)/shard_map/ppermute | solution.py:501
  525.5 32.7 %collective-permute-start.84 = (f32[8,128]{1,0:T(8,128)S(1)}, f32[8,128]{1,0:T(8,128)S(1)}, u32[]{:S(2)}, u32[]{:S(2)}) collective-permute-start(f32[8,128]{1,0:T(8,128)S(1)} %broadcast_in_dim.14), channel_id=1, source_target_pairs={{0,1},{1,0},{2,3},{3,2},{4,5},{5,4},{6,7},{7,6},{8,9},{9,8},{10,11... | collective-permute-start | bytes 12296 | tf_op jit(solution)/shard_map/ppermute | solution.py:387
  530.0 28.2 %collective-permute-start.86 = (f32[8,128]{1,0:T(8,128)S(1)}, f32[8,128]{1,0:T(8,128)S(1)}, u32[]{:S(2)}, u32[]{:S(2)}) collective-permute-start(f32[8,128]{1,0:T(8,128)S(1)} %collective-permute-done.85), channel_id=1, source_target_pairs={{0,1},{1,0},{2,3},{3,2},{4,5},{5,4},{6,7},{7,6},{8,9},{9,8},{10,11... | collective-permute-start | bytes 12296 | tf_op jit(solution)/shard_map/ppermute | solution.py:387
  532.0 27.4 %collective-permute-start.100 = (bf16[128,1024]{1,0:T(8,128)(2,1)}, bf16[128,1024]{1,0:T(8,128)(2,1)}, u32[]{:S(2)}, u32[]{:S(2)}) collective-permute-start(bf16[128,1024]{1,0:T(8,128)(2,1)} %get-tuple-element.744), channel_id=1, source_target_pairs={{0,8},{8,16},{16,24},{24,28},{28,20},{20,12},{12,4},{4,0},{1,9},{9... | collective-permute-start | bytes 786440 | tf_op jit(solution)/shard_map/ppermute | solution.py:501
  562.3 26.3 %collective-permute-start.96 = (bf16[256,2048]{1,0:T(8,128)(2,1)}, bf16[256,2048]{1,0:T(8,128)(2,1)}, u32[]{:S(2)}, u32[]{:S(2)}) collective-permute-start(bf16[256,2048]{1,0:T(8,128)(2,1)} %add_convert_fusion.8.block_ref), channel_id=1, source_target_pairs={{0,8},{8,16},{16,24},{24,28},{28,20},{20,12},{12,4},{4,0},{1,9},{9... | collective-permute-start | bytes 3145736 | tf_op jit(solution)/shard_map/ppermute | solution.py:501
  564.2 26.4 %collective-permute-start.97 = (bf16[256,2048]{1,0:T(8,128)(2,1)}, bf16[256,2048]{1,0:T(8,128)(2,1)}, u32[]{:S(2)}, u32[]{:S(2)}) collective-permute-start(bf16[256,2048]{1,0:T(8,128)(2,1)} %add_convert_fusion.8.block_ref), channel_id=1, source_target_pairs={{0,4},{8,0},{16,8},{24,16},{28,24},{20,28},{12,20},{4,12},{1,5},{9... | collective-permute-start | bytes 3145736 | tf_op jit(solution)/shard_map/ppermute | solution.py:501
  564.3 46.8 %collective-permute-start.127 = (bf16[256,2048]{1,0:T(8,128)(2,1)}, bf16[256,2048]{1,0:T(8,128)(2,1)}, u32[]{:S(2)}, u32[]{:S(2)}) collective-permute-start(bf16[256,2048]{1,0:T(8,128)(2,1)} %collective-permute-done.87), channel_id=1, source_target_pairs={{0,8},{8,16},{16,24},{24,28},{28,20},{20,12},{12,4},{4,0},{1,9},{9... | collective-permute-start | bytes 3145736 | tf_op jit(solution)/shard_map/ppermute | solution.py:501
  568.9 44.1 %collective-permute-start.128 = (bf16[256,2048]{1,0:T(8,128)(2,1)}, bf16[256,2048]{1,0:T(8,128)(2,1)}, u32[]{:S(2)}, u32[]{:S(2)}) collective-permute-start(bf16[256,2048]{1,0:T(8,128)(2,1)} %collective-permute-done.88), channel_id=1, source_target_pairs={{0,4},{8,0},{16,8},{24,16},{28,24},{20,28},{12,20},{4,12},{1,5},{9... | collective-permute-start | bytes 3145736 | tf_op jit(solution)/shard_map/ppermute | solution.py:501
  575.0 21.2 %collective-permute-start.95 = (f32[4,512]{1,0:T(4,128)S(1)}, f32[4,512]{1,0:T(4,128)S(1)}, u32[]{:S(2)}, u32[]{:S(2)}) collective-permute-start(f32[4,512]{1,0:T(4,128)S(1)} %add.723), channel_id=1, source_target_pairs={{0,2},{1,3},{2,0},{3,1},{4,6},{5,7},{6,4},{7,5},{8,10},{9,11},{10,... | collective-permute-start | bytes 24584 | tf_op jit(solution)/shard_map/ppermute | solution.py:944
  600.5 16.4 %collective-permute-start.98 = (bf16[544,256]{1,0:T(8,128)(2,1)S(1)}, bf16[544,256]{1,0:T(8,128)(2,1)S(1)}, u32[]{:S(2)}, u32[]{:S(2)}) collective-permute-start(bf16[544,256]{1,0:T(8,128)(2,1)S(1)} %constant_dynamic-update-slice_fusion.18), channel_id=1, source_target_pairs={{0,8},{8,16},{16,24},{24,28},{28,20},{20,12},{12,4},{4,0},{1,9},{9... | collective-permute-start | bytes 835592 | tf_op jit(solution)/shard_map/ppermute | solution.py:501
  601.9 17.0 %collective-permute-start.99 = (bf16[544,256]{1,0:T(8,128)(2,1)S(1)}, bf16[544,256]{1,0:T(8,128)(2,1)S(1)}, u32[]{:S(2)}, u32[]{:S(2)}) collective-permute-start(bf16[544,256]{1,0:T(8,128)(2,1)S(1)} %constant_dynamic-update-slice_fusion.18), channel_id=1, source_target_pairs={{0,4},{8,0},{16,8},{24,16},{28,24},{20,28},{12,20},{4,12},{1,5},{9... | collective-permute-start | bytes 835592 | tf_op jit(solution)/shard_map/ppermute | solution.py:501
  605.0 25.1 %collective-permute-start.105 = (bf16[256,1024]{1,0:T(8,128)(2,1)S(1)}, bf16[256,1024]{1,0:T(8,128)(2,1)S(1)}, u32[]{:S(2)}, u32[]{:S(2)}) collective-permute-start(bf16[256,1024]{1,0:T(8,128)(2,1)S(1)} %pad_maximum_fusion.29), channel_id=1, source_target_pairs={{0,4},{8,0},{16,8},{24,16},{28,24},{20,28},{12,20},{4,12},{1,5},{9... | collective-permute-start | bytes 1572872 | tf_op jit(solution)/shard_map/ppermute | solution.py:501
  611.1 19.1 %collective-permute-start.104 = (bf16[256,1024]{1,0:T(8,128)(2,1)S(1)}, bf16[256,1024]{1,0:T(8,128)(2,1)S(1)}, u32[]{:S(2)}, u32[]{:S(2)}) collective-permute-start(bf16[256,1024]{1,0:T(8,128)(2,1)S(1)} %pad_maximum_fusion.28), channel_id=1, source_target_pairs={{0,8},{8,16},{16,24},{24,28},{28,20},{20,12},{12,4},{4,0},{1,9},{9... | collective-permute-start | bytes 1572872 | tf_op jit(solution)/shard_map/ppermute | solution.py:501
  613.0 63.7 %collective-permute-start.125 = (bf16[256,2048]{1,0:T(8,128)(2,1)}, bf16[256,2048]{1,0:T(8,128)(2,1)}, u32[]{:S(2)}, u32[]{:S(2)}) collective-permute-start(bf16[256,2048]{1,0:T(8,128)(2,1)} %collective-permute-done.96), channel_id=1, source_target_pairs={{0,8},{8,16},{16,24},{24,28},{28,20},{20,12},{12,4},{4,0},{1,9},{9... | collective-permute-start | bytes 3145736 | tf_op jit(solution)/shard_map/ppermute | solution.py:501
  617.0 60.6 %collective-permute-start.126 = (bf16[256,2048]{1,0:T(8,128)(2,1)}, bf16[256,2048]{1,0:T(8,128)(2,1)}, u32[]{:S(2)}, u32[]{:S(2)}) collective-permute-start(bf16[256,2048]{1,0:T(8,128)(2,1)} %collective-permute-done.97), channel_id=1, source_target_pairs={{0,4},{8,0},{16,8},{24,16},{28,24},{20,28},{12,20},{4,12},{1,5},{9... | collective-permute-start | bytes 3145736 | tf_op jit(solution)/shard_map/ppermute | solution.py:501
  618.9 37.8 %collective-permute-start.102 = (bf16[544,256]{1,0:T(8,128)(2,1)S(1)}, bf16[544,256]{1,0:T(8,128)(2,1)S(1)}, u32[]{:S(2)}, u32[]{:S(2)}) collective-permute-start(bf16[544,256]{1,0:T(8,128)(2,1)S(1)} %collective-permute-done.98), channel_id=1, source_target_pairs={{0,8},{8,16},{16,24},{24,28},{28,20},{20,12},{12,4},{4,0},{1,9},{9... | collective-permute-start | bytes 835592 | tf_op jit(solution)/shard_map/ppermute | solution.py:501
  630.1 30.6 %collective-permute-start.103 = (bf16[544,256]{1,0:T(8,128)(2,1)S(1)}, bf16[544,256]{1,0:T(8,128)(2,1)S(1)}, u32[]{:S(2)}, u32[]{:S(2)}) collective-permute-start(bf16[544,256]{1,0:T(8,128)(2,1)S(1)} %collective-permute-done.99), channel_id=1, source_target_pairs={{0,4},{8,0},{16,8},{24,16},{28,24},{20,28},{12,20},{4,12},{1,5},{9... | collective-permute-start | bytes 835592 | tf_op jit(solution)/shard_map/ppermute | solution.py:501
  630.7 37.2 %collective-permute-start.108 = (bf16[256,1024]{1,0:T(8,128)(2,1)S(1)}, bf16[256,1024]{1,0:T(8,128)(2,1)S(1)}, u32[]{:S(2)}, u32[]{:S(2)}) collective-permute-start(bf16[256,1024]{1,0:T(8,128)(2,1)S(1)} %get-tuple-element.742), channel_id=1, source_target_pairs={{0,8},{8,16},{16,24},{24,28},{28,20},{20,12},{12,4},{4,0},{1,9},{9... | collective-permute-start | bytes 1572872 | tf_op jit(solution)/shard_map/ppermute | solution.py:501
  656.7 16.2 %collective-permute-start.109 = (bf16[256,1024]{1,0:T(8,128)(2,1)S(1)}, bf16[256,1024]{1,0:T(8,128)(2,1)S(1)}, u32[]{:S(2)}, u32[]{:S(2)}) collective-permute-start(bf16[256,1024]{1,0:T(8,128)(2,1)S(1)} %get-tuple-element.741), channel_id=1, source_target_pairs={{0,4},{8,0},{16,8},{24,16},{28,24},{20,28},{12,20},{4,12},{1,5},{9... | collective-permute-start | bytes 1572872 | tf_op jit(solution)/shard_map/ppermute | solution.py:501
  675.5 23.6 %collective-permute-start.112 = (bf16[256,1024]{1,0:T(8,128)(2,1)S(1)}, bf16[256,1024]{1,0:T(8,128)(2,1)S(1)}, u32[]{:S(2)}, u32[]{:S(2)}) collective-permute-start(bf16[256,1024]{1,0:T(8,128)(2,1)S(1)} %get-tuple-element.740), channel_id=1, source_target_pairs={{0,8},{8,16},{16,24},{24,28},{28,20},{20,12},{12,4},{4,0},{1,9},{9... | collective-permute-start | bytes 1572872 | tf_op jit(solution)/shard_map/ppermute | solution.py:501
  676.7 23.6 %collective-permute-start.113 = (bf16[256,1024]{1,0:T(8,128)(2,1)S(1)}, bf16[256,1024]{1,0:T(8,128)(2,1)S(1)}, u32[]{:S(2)}, u32[]{:S(2)}) collective-permute-start(bf16[256,1024]{1,0:T(8,128)(2,1)S(1)} %get-tuple-element.739), channel_id=1, source_target_pairs={{0,4},{8,0},{16,8},{24,16},{28,24},{20,28},{12,20},{4,12},{1,5},{9... | collective-permute-start | bytes 1572872 | tf_op jit(solution)/shard_map/ppermute | solution.py:501
  677.6 27.2 %collective-permute-start.110 = (bf16[272,256]{1,0:T(8,128)(2,1)S(1)}, bf16[272,256]{1,0:T(8,128)(2,1)S(1)}, u32[]{:S(2)}, u32[]{:S(2)}) collective-permute-start(bf16[272,256]{1,0:T(8,128)(2,1)S(1)} %slice.321), channel_id=1, source_target_pairs={{0,8},{8,16},{16,24},{24,28},{28,20},{20,12},{12,4},{4,0},{1,9},{9... | collective-permute-start | bytes 417800 | tf_op jit(solution)/shard_map/ppermute | solution.py:501
  687.8 17.4 %collective-permute-start.111 = (bf16[272,256]{1,0:T(8,128)(2,1)S(1)}, bf16[272,256]{1,0:T(8,128)(2,1)S(1)}, u32[]{:S(2)}, u32[]{:S(2)}) collective-permute-start(bf16[272,256]{1,0:T(8,128)(2,1)S(1)} %slice.322), channel_id=1, source_target_pairs={{0,4},{8,0},{16,8},{24,16},{28,24},{20,28},{12,20},{4,12},{1,5},{9... | collective-permute-start | bytes 417800 | tf_op jit(solution)/shard_map/ppermute | solution.py:501
  689.0 56.7 %collective-permute-start.129 = (bf16[256,2048]{1,0:T(8,128)(2,1)}, bf16[256,2048]{1,0:T(8,128)(2,1)}, u32[]{:S(2)}, u32[]{:S(2)}) collective-permute-start(bf16[256,2048]{1,0:T(8,128)(2,1)} %collective-permute-done.125), channel_id=1, source_target_pairs={{0,8},{8,16},{16,24},{24,28},{28,20},{20,12},{12,4},{4,0},{1,9},{9... | collective-permute-start | bytes 3145736 | tf_op jit(solution)/shard_map/ppermute | solution.py:501
  699.1 46.7 %collective-permute-start.130 = (bf16[256,2048]{1,0:T(8,128)(2,1)}, bf16[256,2048]{1,0:T(8,128)(2,1)S(1)}, u32[]{:S(2)}, u32[]{:S(2)}) collective-permute-start(bf16[256,2048]{1,0:T(8,128)(2,1)} %collective-permute-done.126), channel_id=1, source_target_pairs={{0,4},{8,0},{16,8},{24,16},{28,24},{20,28},{12,20},{4,12},{1,5},{9... | collective-permute-start | bytes 3145736 | tf_op jit(solution)/shard_map/ppermute | solution.py:501
  701.3 31.6 %collective-permute-start.114 = (bf16[256,1024]{1,0:T(8,128)(2,1)}, bf16[256,1024]{1,0:T(8,128)(2,1)}, u32[]{:S(2)}, u32[]{:S(2)}) collective-permute-start(bf16[256,1024]{1,0:T(8,128)(2,1)} %add_convert_fusion.27), channel_id=1, source_target_pairs={{0,8},{8,16},{16,24},{24,28},{28,20},{20,12},{12,4},{4,0},{1,9},{9... | collective-permute-start | bytes 1572872 | tf_op jit(solution)/shard_map/ppermute | solution.py:501
  704.8 32.3 %collective-permute-start.115 = (bf16[256,1024]{1,0:T(8,128)(2,1)}, bf16[256,1024]{1,0:T(8,128)(2,1)}, u32[]{:S(2)}, u32[]{:S(2)}) collective-permute-start(bf16[256,1024]{1,0:T(8,128)(2,1)} %add_convert_fusion.27), channel_id=1, source_target_pairs={{0,4},{8,0},{16,8},{24,16},{28,24},{20,28},{12,20},{4,12},{1,5},{9... | collective-permute-start | bytes 1572872 | tf_op jit(solution)/shard_map/ppermute | solution.py:501
  714.2 27.9 %collective-permute-start.124 = (bf16[512,256]{1,0:T(8,128)(2,1)}, bf16[512,256]{1,0:T(8,128)(2,1)}, u32[]{:S(2)}, u32[]{:S(2)}) collective-permute-start(bf16[512,256]{1,0:T(8,128)(2,1)} %slice.433), channel_id=1, source_target_pairs={{0,1},{1,0},{2,3},{3,2},{4,5},{5,4},{6,7},{7,6},{8,9},{9,8},{10,11... | collective-permute-start | bytes 786440 | tf_op jit(solution)/shard_map/ppermute | solution.py:387
  751.2 17.2 %collective-permute-start.134 = (bf16[128,2048]{1,0:T(8,128)(2,1)S(1)}, bf16[128,2048]{1,0:T(8,128)(2,1)S(1)}, u32[]{:S(2)}, u32[]{:S(2)}) collective-permute-start(bf16[128,2048]{1,0:T(8,128)(2,1)S(1)} %slice.337), channel_id=1, source_target_pairs={{0,4},{8,0},{16,8},{24,16},{28,24},{20,28},{12,20},{4,12},{1,5},{9... | collective-permute-start | bytes 1572872 | tf_op jit(solution)/shard_map/ppermute | solution.py:501
  757.1 17.9 %collective-permute-start.118 = (bf16[256,1024]{1,0:T(8,128)(2,1)S(1)}, bf16[256,1024]{1,0:T(8,128)(2,1)S(1)}, u32[]{:S(2)}, u32[]{:S(2)}) collective-permute-start(bf16[256,1024]{1,0:T(8,128)(2,1)S(1)} %collective-permute-done.116), channel_id=1, source_target_pairs={{0,8},{8,16},{16,24},{24,28},{28,20},{20,12},{12,4},{4,0},{1,9},{9... | collective-permute-start | bytes 1572872 | tf_op jit(solution)/shard_map/ppermute | solution.py:501
  758.5 20.4 %collective-permute-start.119 = (bf16[256,1024]{1,0:T(8,128)(2,1)S(1)}, bf16[256,1024]{1,0:T(8,128)(2,1)S(1)}, u32[]{:S(2)}, u32[]{:S(2)}) collective-permute-start(bf16[256,1024]{1,0:T(8,128)(2,1)S(1)} %collective-permute-done.117), channel_id=1, source_target_pairs={{0,4},{8,0},{16,8},{24,16},{28,24},{20,28},{12,20},{4,12},{1,5},{9... | collective-permute-start | bytes 1572872 | tf_op jit(solution)/shard_map/ppermute | solution.py:501
  (209 other events, 1933.3 us)
Sparse Core Ops, SparseCore 0:
  40.5 66.7 all-gather.1
